TPU v7x, 128 devices: a whole 4x4x4 slice. The times are simulated.
128 devices in a mesh: grp: 8 (over z, core), mem: 16 (over x, y).
Axes of the slice: x: 4, y: 4, z: 4, core: 2. Of those that a mesh axis runs over, the one named last changes fastest.
Arguments:
- send_rows: bfloat16 [128, 128, 16, 512], P(('grp', 'mem')), may hold values from -6 to 6
- slot_pos: int32 [128, 128, 16], P(('grp', 'mem')), may hold values from -1 to 1023, as said below
- lengths: int32 [128, 8], P(('grp', 'mem')), may hold values from 1 to 512, 1024 in all within a row
- candidates: bfloat16 [16384, 512], P(('grp', 'mem')), may hold values from -6 to 6
- target_ids: int32 [1024, 16], P(('grp', 'mem')), may hold values from 0 to 2047
- w_proj: bfloat16 [512, 2048], replicated, may hold values from -0.25 to 0.25
- w_out: bfloat16 [512, 512], replicated, may hold values from -0.25 to 0.25
- grad_hist_out: bfloat16 [131072, 512], P(('grp', 'mem')), may hold values from -6 to 6
- grad_tgt_out: bfloat16 [16384, 512], P(('grp', 'mem')), may hold values from -6 to 6
Outputs:
- out_hist: bfloat16 [131072, 512], P(('grp', 'mem'))
- out_tgt: bfloat16 [16384, 512], P(('grp', 'mem'))
- d_send: bfloat16 [128, 128, 16, 512], P(('grp', 'mem'))
- d_cand: float32 [16384, 512], P(('grp', 'mem'))
- d_w_proj: float32 [512, 2048], replicated
- d_w_out: float32 [512, 512], replicated
Inputs may be any that keep to these rules, and one draw needn't show every extreme that they name: For each destination d the entries of slot_pos[d] that are not -1 are each of 0 to 1023 once; in slot_pos[d, s] the live slots come first; at most 16 slots are live for a pair, and every destination has a source with all 16 live. `lengths`: each row sums to 1024 and its largest entry is 512.
All inputs are finite; a program needn't handle non-finite values.
Results may differ from a plain program's by a relative error of at most 0.019.
Values may be sent and summed in bfloat16 or wider, within the bound.
No kernel may reach another device: no remote copies, remote signals or barrier semaphores. Data moves between devices by JAX's collectives and lax.ppermute only.
A program may use at most 192 MiB of HBM per device.

v0:
```python
import jax
import jax.numpy as jnp
from jax import lax
from jax.sharding import PartitionSpec as P

HEADS = 8


norm_epsilon = 1e-05


def norm_rows(values):
    row_mean = jnp.mean(values, axis=-1, keepdims=True)
    centred = values - row_mean
    variance = jnp.mean(centred * centred, axis=-1, keepdims=True)
    return centred * lax.rsqrt(variance + norm_epsilon)


def attend_block(queries, key_rows, val_rows, allowed, score_scale):
    scores = (
        jnp.einsum("qhe,khe->hqk", queries, key_rows, preferred_element_type=jnp.float32)
        * score_scale
    )
    weights = jnp.where(allowed[None], jax.nn.silu(scores), 0.0).astype(jnp.bfloat16)
    return jnp.einsum("hqk,khe->qhe", weights, val_rows, preferred_element_type=jnp.float32)


def segment_ids(user_lengths, row_count):
    ends = jnp.cumsum(user_lengths)
    return jnp.sum((jnp.arange(row_count)[:, None] >= ends[None, :]).astype(jnp.int32), axis=1)


def sequence_layer(x_hist, x_tgt, w_proj, w_out, seg_hist, seg_tgt):
    hist_rows = x_hist.shape[0]
    feature = x_hist.shape[1]
    head_size = feature // HEADS
    score_scale = 1.0 / head_size**0.5
    joined = jnp.concatenate([x_hist, x_tgt], axis=0)
    normed = norm_rows(joined.astype(jnp.float32)).astype(jnp.bfloat16)
    projected = jax.nn.silu(jnp.dot(normed, w_proj, preferred_element_type=jnp.float32)).astype(
        jnp.bfloat16
    )
    gate_rows = projected[:, :feature]
    val_rows = projected[:, feature : 2 * feature].reshape(-1, HEADS, head_size)
    queries = projected[:, 2 * feature : 3 * feature].reshape(-1, HEADS, head_size)
    key_rows = projected[:, 3 * feature :].reshape(-1, HEADS, head_size)
    row_block = min(512, hist_rows)
    positions = jnp.arange(hist_rows)
    outputs = []
    for first_row in range(0, hist_rows, row_block):
        last_row = first_row + row_block
        allowed = (seg_hist[first_row:last_row, None] == seg_hist[None, :last_row]) & (
            positions[first_row:last_row, None] >= positions[None, :last_row]
        )
        outputs.append(
            attend_block(
                queries[first_row:last_row],
                key_rows[:last_row],
                val_rows[:last_row],
                allowed,
                score_scale,
            )
        )
    target_queries = queries[hist_rows:]
    target_allowed = seg_tgt[:, None] == seg_hist[None, :]
    target_out = attend_block(
        target_queries, key_rows[:hist_rows], val_rows[:hist_rows], target_allowed, score_scale
    )
    self_score = (
        jnp.sum(
            target_queries.astype(jnp.float32) * key_rows[hist_rows:].astype(jnp.float32), axis=-1
        )
        * score_scale
    )
    self_weight = jax.nn.silu(self_score).astype(jnp.bfloat16)
    target_out = target_out + self_weight.astype(jnp.float32)[..., None] * val_rows[
        hist_rows:
    ].astype(jnp.float32)
    outputs.append(target_out)
    attended = jnp.concatenate(outputs, axis=0).reshape(-1, feature)
    mixed_rows = (norm_rows(attended) * gate_rows.astype(jnp.float32)).astype(jnp.bfloat16)
    result = (
        joined.astype(jnp.float32) + jnp.dot(mixed_rows, w_out, preferred_element_type=jnp.float32)
    ).astype(jnp.bfloat16)
    return (result[:hist_rows], result[hist_rows:])


def local(
    send_rows, slot_pos, lengths, candidates, target_ids, w_proj, w_out, grad_hist_out, grad_tgt_out
):
    feature = send_rows.shape[3]
    capacity = send_rows.shape[2]
    peer_count = send_rows.shape[1]
    hist_rows = grad_hist_out.shape[0]
    arrived = lax.all_to_all(send_rows, ("grp", "mem"), split_axis=1, concat_axis=0, tiled=True)
    arrived = arrived.reshape(peer_count * capacity, feature)
    flat_pos = slot_pos.reshape(-1)
    landing = jnp.where(flat_pos < 0, hist_rows, flat_pos)
    x_hist = (
        jnp.zeros((hist_rows + 1, feature), jnp.bfloat16)
        .at[landing]
        .set(arrived, mode="drop")[:hist_rows]
    )
    picked_ids = target_ids.reshape(-1)
    shard_rows = lax.all_gather(candidates, "mem", axis=0, tiled=True)
    present = (picked_ids >= 0) & (picked_ids < shard_rows.shape[0])
    fetched = jnp.take(shard_rows, jnp.clip(picked_ids, 0, shard_rows.shape[0] - 1), axis=0)
    x_tgt = jnp.where(
        present[:, None], fetched, jnp.zeros((picked_ids.shape[0], feature), jnp.bfloat16)
    )
    seg_hist = segment_ids(lengths[0], hist_rows)
    seg_tgt = jnp.arange(picked_ids.shape[0]) // target_ids.shape[1]

    def local_layer(hist_in, tgt_in, proj_in, out_in):
        return sequence_layer(hist_in, tgt_in, proj_in, out_in, seg_hist, seg_tgt)

    (out_hist, out_tgt), backward = jax.vjp(local_layer, x_hist, x_tgt, w_proj, w_out)
    grad_hist, grad_tgt, grad_proj, grad_out = backward((grad_hist_out, grad_tgt_out))
    fetched_grads = jnp.take(grad_hist, jnp.clip(flat_pos, 0, hist_rows - 1), axis=0)
    slot_grads = jnp.where(flat_pos[:, None] >= 0, fetched_grads, jnp.zeros_like(fetched_grads))
    returned = lax.all_to_all(
        slot_grads.reshape(peer_count, 1, capacity, feature),
        ("grp", "mem"),
        split_axis=0,
        concat_axis=1,
        tiled=True,
    )
    tangent_rows = grad_tgt.astype(jnp.float32)
    cand_count = candidates.shape[0]
    wanted = jnp.arange(cand_count * lax.axis_size("mem"))
    onehot = (wanted[:, None] == picked_ids[None, :]).astype(jnp.float32)
    d_cand = lax.psum_scatter(
        jnp.dot(
            onehot,
            tangent_rows,
            precision=lax.Precision.HIGHEST,
            preferred_element_type=jnp.float32,
        ).astype(jnp.bfloat16),
        "mem",
        scatter_dimension=0,
        tiled=True,
    ).astype(jnp.float32)
    weight_sums = lax.psum(
        (grad_proj.astype(jnp.float32), grad_out.astype(jnp.float32)), ("grp", "mem")
    )
    sum_proj = weight_sums[0]
    sum_out = weight_sums[1]
    return (out_hist, out_tgt, returned, d_cand, sum_proj, sum_out)


def solution(mesh):
    placed = (
        P(("grp", "mem"), None, None, None),
        P(("grp", "mem"), None, None),
        P(("grp", "mem"), None),
        P(("grp", "mem"), None),
        P(("grp", "mem"), None),
        P(),
        P(),
        P(("grp", "mem"), None),
        P(("grp", "mem"), None),
    )
    return jax.shard_map(
        local,
        mesh=mesh,
        in_specs=placed,
        out_specs=(
            P(("grp", "mem"), None),
            P(("grp", "mem"), None),
            P(("grp", "mem"), None, None, None),
            P(("grp", "mem"), None),
            P(),
            P(),
        ),
        check_vma=False,
    )
```

profile of v0, /device:TPU:1, one launch (start us, length us, event | category | flops | bytes accessed | tf_op | source)
XLA Modules:
  0.0 493.9 jit_solution(762196652577445508)
XLA Ops:
  7.9 12.0 %all-to-all-start = ((bf16[1,128,16,512]{3,2,0,1:T(8,128)(2,1)}), bf16[1,128,16,512]{3,2,0,1:T(8,128)(2,1)}, u32[]{:S(2)}, u32[]{:S(2)}) async-start(bf16[1,128,16,512]{3,2,0,1:T(8,128)(2,1)} %bitcast.147), calls=%async_computation | async-start | bytes 4194304 | tf_op jit(solution)/shard_map/all_to_all | solution.py:95
  24.5 26.9 %all-to-all-done = bf16[1,128,16,512]{3,2,0,1:T(8,128)(2,1)} async-done(((bf16[1,128,16,512]{3,2,0,1:T(8,128)(2,1)}), bf16[1,128,16,512]{3,2,0,1:T(8,128)(2,1)}, u32[]{:S(2)}, u32[]{:S(2)}) %all-to-all-start) | async-done | bytes 2097184 | tf_op jit(solution)/shard_map/all_to_all | solution.py:95
  51.4 10.9 %scatter_custom_fusion = bf16[1025,512]{1,0:T(8,128)(2,1)} fusion(s32[2048]{0:T(1024)S(1)} %bitcast.151, bf16[2048,512]{1,0:T(8,128)(2,1)} %bitcast.2, bf16[]{:T(256)} %constant.57.clone.1), kind=kCustom, calls=%fused_computation.93 | custom fusion | bytes 1050112 | tf_op jit(solution)/shard_map/scatter | solution.py:102
  63.6 3.7 all-gather.2.cloned.1.call-done
  67.4 2.7 gather_fusion
  71.1 6.8 %multiply_convert_fusion = (bf16[1152,2048]{1,0:T(8,128)(2,1)S(1)}, f32[1152,2048]{1,0:T(8,128)}) fusion(bf16[512,2048]{1,0:T(8,128)(2,1)S(1)} %copy-done, f32[1152]{0:T(1024)S(1)} %fusion.43, f32[1152]{0:T(1024)S(1)} %broadcast_multiply_fusion.1, bf16[128,512]{1,0:T(8,128)(2,1)S(1)} %select_select_fusion.1, bf16[1024,512]{1,0:T(8,128)(2,1)S(1)} %slice.121), kind=kOutput, calls=%fused_computation.15 | convolution fusion | flops 2431844352 | bytes 17441792 | tf_op jit(solution)/shard_map/jvp()/dot_general | solution.py:40
  99.6 7.4 %select_convert_fusion.1 = (bf16[8,512,512]{2,1,0:T(8,128)(2,1)S(1)}, f32[8,512,512]{2,1,0:T(8,128)}) fusion(pred[512,512]{1,0:T(8,128)(4,1)} %compare_and_fusion, bf16[512,8,64]{0,2,1:T(8,128)(2,1)} %bitcast.137, bf16[512,8,64]{0,2,1:T(8,128)(2,1)} %bitcast.139), kind=kOutput, calls=%fused_computation.20 | convolution fusion | flops 283115520 | bytes 13893632 | tf_op jit(solution)/shard_map/jvp(qhe,khe->hqk)/dot_general | solution.py:21
  110.1 9.8 %select_convert_fusion = (bf16[8,512,1024]{2,1,0:T(8,128)(2,1)S(1)}, f32[8,512,1024]{2,1,0:T(8,128)}) fusion(pred[512,1024]{1,0:T(8,128)(4,1)S(1)} %copy-done.35, bf16[512,8,64]{0,2,1:T(8,128)(2,1)S(1)} %bitcast.141, bf16[1024,8,64]{0,2,1:T(8,128)(2,1)S(1)} %bitcast.128), kind=kOutput, calls=%fused_computation.7 | convolution fusion | flops 566231040 | bytes 27262976 | tf_op jit(solution)/shard_map/jvp(qhe,khe->hqk)/dot_general | solution.py:21
  120.0 2.7 convolution_bitcast_fusion
  123.2 3.7 select_convert_fusion.2
  130.6 3.1 copy.104
  133.6 3.7 multiply_reduce_fusion
  137.3 3.8 fusion.57
  145.3 13.1 %fusion.2 = bf16[8,512,1024]{2,1,0:T(8,128)(2,1)S(1)} fusion(f32[8,512,1024]{2,1,0:T(8,128)} %get-tuple-element.40, pred[512,1024]{1,0:T(8,128)(4,1)} %fusion.23, bf16[8,64,512]{2,1,0:T(8,128)(2,1)} %bitcast.131, bf16[1024,8,64]{0,2,1:T(8,128)(2,1)} %bitcast.119), kind=kOutput, calls=%fused_computation.6 | convolution fusion | flops 595591168 | bytes 27262976 | tf_op jit(solution)/shard_map/transpose(jvp(hqk,khe->qhe))/dot_general | solution.py:25
  161.0 3.5 fusion.29
  166.6 7.3 %fusion.7 = bf16[8,512,512]{2,1,0:T(8,128)(2,1)S(1)} fusion(f32[8,512,512]{2,1,0:T(8,128)} %get-tuple-element.42, pred[512,512]{1,0:T(8,128)(4,1)} %compare_and_fusion, bf16[8,64,512]{2,1,0:T(8,128)(2,1)} %bitcast.143, bf16[512,8,64]{0,2,1:T(8,128)(2,1)} %bitcast.148), kind=kOutput, calls=%fused_computation.19 | convolution fusion | flops 297795584 | bytes 13893632 | tf_op jit(solution)/shard_map/transpose(jvp(hqk,khe->qhe))/dot_general | solution.py:25
  177.8 6.1 %fusion.26 = bf16[1024,8,64]{0,2,1:T(8,128)(2,1)} fusion(bf16[8,64,512]{2,1,0:T(8,128)(2,1)S(1)} %bitcast.132, bf16[8,512,1024]{2,1,0:T(8,128)(2,1)} %copy-done.1), kind=kOutput, calls=%fused_computation.65 | convolution fusion | flops 536870912 | bytes 9961472 | tf_op jit(solution)/shard_map/transpose(jvp(hqk,khe->qhe))/dot_general | solution.py:25
  190.0 3.1 fusion.25
  193.2 4.2 fusion.10
  203.4 2.8 fusion.36
  209.8 3.2 pad_add_fusion
  215.4 7.4 %fusion.3 = bf16[1152,2048]{1,0:T(8,128)(2,1)S(1)} fusion(f32[1152,2048]{1,0:T(8,128)} %get-tuple-element.36, bf16[1152,512]{1,0:T(8,128)(2,1)} %get-tuple-element.11, bf16[1152,512]{1,0:T(8,128)(2,1)} %copy.113, bf16[1152,512]{1,0:T(8,128)(2,1)} %copy.112, bf16[1152,512]{1,0:T(8,128)(2,1)} %copy.111), kind=kLoop, calls=%fused_computation.13 | loop fusion | flops 42467328 | bytes 18874368 | tf_op jit(solution)/shard_map/transpose(jvp(jit(silu)))/add_any | solution.py:40
  222.8 2.8 fusion.22
  232.1 3.4 fusion.28
  235.5 7.4 %fusion.16 = f32[512,2048]{1,0:T(8,128)} fusion(bf16[1152,2048]{1,0:T(8,128)(2,1)} %copy-done.13, f32[1152]{0:T(1024)S(1)} %copy-done.41, f32[1152]{0:T(1024)S(1)} %broadcast_multiply_fusion.1, bf16[128,512]{1,0:T(8,128)(2,1)S(1)} %select_select_fusion.1, bf16[1024,512]{1,0:T(8,128)(2,1)S(1)} %slice.121), kind=kOutput, calls=%fused_computation.39 | convolution fusion | flops 2421096448 | bytes 10101760 | tf_op jit(solution)/shard_map/transpose(jvp())/dot_general | solution.py:40
  244.9 9.2 %gather_fusion.1 = bf16[2048,512]{1,0:T(8,128)(2,1)} fusion(bf16[1024,512]{1,0:T(8,128)(2,1)S(1)} %split.32, s32[2048]{0:T(1024)S(1)} %broadcast_clamp_fusion), kind=kCustom, calls=%fused_computation.1 | custom fusion | bytes 4202496 | tf_op jit(solution)/shard_map/jit(_take)/gather | solution.py:119
  254.1 2.9 select_select_fusion
  257.0 9.0 %all-to-all-start.1 = ((bf16[128,1,16,512]{3,2,1,0:T(8,128)(2,1)}), bf16[128,1,16,512]{3,2,1,0:T(8,128)(2,1)}, u32[]{:S(2)}, u32[]{:S(2)}) async-start(bf16[128,1,16,512]{3,2,1,0:T(8,128)(2,1)} %select_select_fusion), calls=%async_computation.1 | async-start | bytes 4194304 | tf_op jit(solution)/shard_map/all_to_all | solution.py:121
  269.9 28.1 %all-to-all-done.1 = bf16[128,1,16,512]{3,2,1,0:T(8,128)(2,1)} async-done(((bf16[128,1,16,512]{3,2,1,0:T(8,128)(2,1)}), bf16[128,1,16,512]{3,2,1,0:T(8,128)(2,1)}, u32[]{:S(2)}, u32[]{:S(2)}) %all-to-all-start.1) | async-done | bytes 2097184 | tf_op jit(solution)/shard_map/all_to_all | solution.py:121
  298.0 19.0 %reduce-scatter.2.cloned.1.call-done = bf16[128,512]{1,0:T(8,128)(2,1)} async-done(((bf16[2048,512]{1,0:T(8,128)(2,1)}), bf16[128,512]{1,0:T(8,128)(2,1)}) %reduce-scatter.2.cloned.1.call-update) | async-done | bytes 131088 | tf_op jit(solution)/shard_map/reduce_scatter | solution.py:132
  318.6 162.3 %all-reduce.20.cloned.1.call-done = (f32[512,2048]{1,0:T(8,128)}, f32[512,512]{1,0:T(8,128)}) async-done(((f32[512,2048]{1,0:T(8,128)}, f32[512,512]{1,0:T(8,128)}), (f32[512,2048]{1,0:T(8,128)}, f32[512,512]{1,0:T(8,128)})) %all-reduce.20.cloned.1.call-update) | async-done | bytes 5242896 | tf_op jit(solution)/shard_map/psum | solution.py:143
  480.9 3.2 copy.121
  (201 shorter events, 84.0 us)
Async XLA Ops:
  7.2 63.9 %copy-start = (bf16[512,2048]{1,0:T(8,128)(2,1)S(1)}, bf16[512,2048]{1,0:T(8,128)(2,1)}, u32[]{:S(2)}) copy-start(bf16[512,2048]{1,0:T(8,128)(2,1)} %param.14) | copy-start | bytes 6291460
  7.2 12.8 %copy-start.52 = (s32[8,16]{1,0:T(8,128)S(1)}, s32[8,16]{1,0:T(8,128)}, u32[]{:S(2)}) copy-start(s32[8,16]{1,0:T(8,128)} %param.13) | copy-start | bytes 1540
  7.2 13.0 %copy-start.44 = (s32[1,128,16]{1,2,0:T(8,128)S(1)}, s32[1,128,16]{1,2,0:T(8,128)}, u32[]{:S(2)}) copy-start(s32[1,128,16]{1,2,0:T(8,128)} %param.10) | copy-start | bytes 24580
  7.2 13.2 %copy-start.55 = (s32[1,8]{1,0:T(1,128)S(1)}, s32[1,8]{1,0:T(1,128)}, u32[]{:S(2)}) copy-start(s32[1,8]{1,0:T(1,128)} %param.11) | copy-start | bytes 100
  7.2 60.2 %all-gather.2.cloned.1.call-start = ((), (), s32[]{:S(2)}) async-start(), calls=%async_computation.3 | async-start | bytes 2228224 | tf_op jit(solution)/shard_map/all_gather | solution.py:105
  7.9 43.5 %all-to-all-start = ((bf16[1,128,16,512]{3,2,0,1:T(8,128)(2,1)}), bf16[1,128,16,512]{3,2,0,1:T(8,128)(2,1)}, u32[]{:S(2)}, u32[]{:S(2)}) async-start(bf16[1,128,16,512]{3,2,0,1:T(8,128)(2,1)} %bitcast.147), calls=%async_computation | async-start | bytes 4194304 | tf_op jit(solution)/shard_map/all_to_all | solution.py:95
  19.9 297.1 %reduce-scatter.2.cloned.1.call-start = ((), (), s32[]{:S(2)}) async-start(), calls=%async_computation.4 | async-start | bytes 2228224 | tf_op jit(solution)/shard_map/reduce_scatter | solution.py:132
  20.1 31.4 %copy-start.53 = (s32[128]{0:T(128)}, s32[128]{0:T(128)S(1)}, u32[]{:S(2)}) copy-start(s32[128]{0:T(128)S(1)} %reshape.424) | copy-start | bytes 1540
  63.6 171.8 %copy-start.2 = (bf16[1024,512]{1,0:T(8,128)(2,1)}, bf16[1024,512]{1,0:T(8,128)(2,1)S(1)}, u32[]{:S(2)}) copy-start(bf16[1024,512]{1,0:T(8,128)(2,1)S(1)} %slice.121) | copy-start | bytes 3145732
  71.1 6.8 %copy-start.42 = (f32[1152]{0:T(1024)}, f32[1152]{0:T(1024)S(1)}, u32[]{:S(2)}) copy-start(f32[1152]{0:T(1024)S(1)} %fusion.20) | copy-start | bytes 13828
  71.1 6.8 %copy-start.40 = (f32[1152]{0:T(1024)}, f32[1152]{0:T(1024)S(1)}, u32[]{:S(2)}) copy-start(f32[1152]{0:T(1024)S(1)} %fusion.43) | copy-start | bytes 13828
  77.9 3.5 copy-start.7
  98.5 28.3 %copy-start.48 = (f32[128,8]{0,1:T(8,128)}, f32[128,8]{0,1:T(8,128)S(1)}, u32[]{:S(2)}) copy-start(f32[128,8]{0,1:T(8,128)S(1)} %fusion.48) | copy-start | bytes 12292
  99.6 7.5 %copy-start.32 = (bf16[512,512]{0,1:T(8,128)(2,1)S(1)}, bf16[512,512]{0,1:T(8,128)(2,1)}, u32[]{:S(2)}) copy-start(bf16[512,512]{0,1:T(8,128)(2,1)} %copy.95) | copy-start | bytes 1572868
  110.1 9.9 %copy-start.8 = (bf16[1024,512]{0,1:T(8,128)(2,1)S(1)}, bf16[1024,512]{0,1:T(8,128)(2,1)}, u32[]{:S(2)}) copy-start(bf16[1024,512]{0,1:T(8,128)(2,1)} %copy.98) | copy-start | bytes 3145732
  133.6 3.7 copy-start.50
  133.6 3.7 copy-start.4
  145.3 13.1 %copy-start.27 = (bf16[512,512]{0,1:T(8,128)(2,1)S(1)}, bf16[512,512]{0,1:T(8,128)(2,1)}, u32[]{:S(2)}) copy-start(bf16[512,512]{0,1:T(8,128)(2,1)} %copy.99) | copy-start | bytes 1572868
  166.6 7.4 %copy-start.24 = (bf16[512,512]{0,1:T(8,128)(2,1)S(1)}, bf16[512,512]{0,1:T(8,128)(2,1)}, u32[]{:S(2)}) copy-start(bf16[512,512]{0,1:T(8,128)(2,1)} %copy.96) | copy-start | bytes 1572868
  177.8 6.1 %copy-start.6 = (bf16[8,512,512]{2,1,0:T(8,128)(2,1)S(1)}, bf16[8,512,512]{2,1,0:T(8,128)(2,1)}, u32[]{:S(2)}) copy-start(bf16[8,512,512]{2,1,0:T(8,128)(2,1)} %copy-done.5) | copy-start | bytes 12582916
  177.8 6.1 %copy-start.28 = (bf16[512,512]{0,1:T(8,128)(2,1)S(1)}, bf16[512,512]{0,1:T(8,128)(2,1)}, u32[]{:S(2)}) copy-start(bf16[512,512]{0,1:T(8,128)(2,1)} %copy.110) | copy-start | bytes 1572868
  183.9 5.2 %copy-start.47 = (f32[128,8]{0,1:T(8,128)S(1)}, f32[128,8]{0,1:T(8,128)}, u32[]{:S(2)}) copy-start(f32[128,8]{0,1:T(8,128)} %copy-done.46) | copy-start | bytes 12292
  187.3 5.8 %copy-start.9 = (bf16[1024,512]{0,1:T(8,128)(2,1)S(1)}, bf16[1024,512]{0,1:T(8,128)(2,1)}, u32[]{:S(2)}) copy-start(bf16[1024,512]{0,1:T(8,128)(2,1)} %copy.98) | copy-start | bytes 3145732
  187.3 5.8 %copy-start.22 = (f32[128,512]{0,1:T(8,128)S(1)}, f32[128,512]{0,1:T(8,128)}, u32[]{:S(2)}) copy-start(f32[128,512]{0,1:T(8,128)} %copy.108) | copy-start | bytes 786436
  187.3 5.8 %copy-start.39 = (pred[128,1024]{1,0:T(8,128)(4,1)S(1)}, pred[128,1024]{1,0:T(8,128)(4,1)}, u32[]{:S(2)}) copy-start(pred[128,1024]{1,0:T(8,128)(4,1)} %broadcast_compare_fusion) | copy-start | bytes 393220
  193.1 4.2 copy-start.30
  197.4 3.7 copy-start.11
  199.5 3.9 copy-start.21
  206.2 3.6 copy-start.34
  231.7 249.2 %all-reduce.20.cloned.1.call-start = ((), (), s32[]{:S(2)}) async-start(), calls=%async_computation.5 | async-start | bytes 10485760 | tf_op jit(solution)/shard_map/psum | solution.py:143
  257.0 9.0 %copy-start.3 = (bf16[1024,512]{1,0:T(8,128)(2,1)S(1)}, bf16[1024,512]{1,0:T(8,128)(2,1)}, u32[]{:S(2)}) copy-start(bf16[1024,512]{1,0:T(8,128)(2,1)} %copy-done.2) | copy-start | bytes 3145732
  257.0 41.0 %all-to-all-start.1 = ((bf16[128,1,16,512]{3,2,1,0:T(8,128)(2,1)}), bf16[128,1,16,512]{3,2,1,0:T(8,128)(2,1)}, u32[]{:S(2)}, u32[]{:S(2)}) async-start(bf16[128,1,16,512]{3,2,1,0:T(8,128)(2,1)} %select_select_fusion), calls=%async_computation.1 | async-start | bytes 4194304 | tf_op jit(solution)/shard_map/all_to_all | solution.py:121
  (29 other events, 64.9 us)
Sparse Core Ops, SparseCore 0:
  10.2 57.1 all-gather.1
  231.8 85.0 reduce-scatter.1
  323.5 157.3 all-reduce.19
where the time goes:
time: 500 us; the launch traced here: 494 us
  waiting for transfers between devices  241 us (48%)
  matrix products  103 us (21%)
  local copies, waits for them, and re-layouts  78 us (16%)
  other arithmetic  36.7 us (7%)
  starting transfers between devices  21 us (4%)
  between operations  14.7 us (3%)
    psum x1, waiting for transfers between devices, local(): lax.psum((grad_proj.astype(jnp.float32), grad_out.astype(jnp.float32)), (...  162 us
    dot_general x9, matrix products, attend_block(): jnp.einsum('hqk,khe->qhe', weights, val_rows, preferred_element_type=jnp....  40.3 us
    dot_general x9, matrix products, attend_block(): jnp.einsum('qhe,khe->hqk', queries, key_rows, preferred_element_type=jnp....  34.1 us
    all_to_all x1, waiting for transfers between devices, local(): lax.all_to_all(slot_grads.reshape(peer_count, 1, capacity, feature), ('gr...  28.1 us
    all_to_all x1, waiting for transfers between devices, local(): lax.all_to_all(send_rows, ('grp', 'mem'), split_axis=1, concat_axis=0, ti...  26.9 us
    reduce_scatter x1, waiting for transfers between devices, local(): lax.psum_scatter(jnp.dot(onehot, tangent_rows, precision=lax.Precision.HI...  19 us
    dot_general x3, matrix products, sequence_layer(): jnp.dot(normed, w_proj, preferred_element_type=jnp.float32)  17 us
    unnamed x116, local copies, waits for them, and re-layouts  13.2 us
  transfers between devices with their start and end apart: 5, of which 5 were waited for; matrix products, arithmetic and copies ran while one was open for 9% of the time, Pallas kernels for 0%

commit v1 on v0

v1 whole, which is shorter than its diff:
```python
import jax
import jax.numpy as jnp
from jax import lax
from jax.experimental import pallas as pl
from jax.experimental.pallas import tpu as pltpu
from jax.sharding import PartitionSpec as P

HEADS = 8
EPS = 1e-05
BLK = 256
MASKED = -1e9
F32 = jnp.float32
BF16 = jnp.bfloat16
BOTH = ("grp", "mem")
NN = (((1,), (0,)), ((), ()))
NT = (((1,), (1,)), ((), ()))


def mm(left, right, dims=NN):
    return lax.dot_general(left, right, dims, preferred_element_type=F32)


def moments(values):
    centred = values - jnp.mean(values, axis=-1, keepdims=True)
    variance = jnp.mean(centred * centred, axis=-1, keepdims=True)
    return centred, lax.rsqrt(variance + EPS)


def layer_kernel(
    first_ref,
    arrived,
    pos_row,
    cand,
    tid_col,
    lo,
    hi,
    w_proj,
    w_out,
    g_hist,
    g_tgt,
    out_hist,
    out_tgt,
    normed_o,
    normed_t,
    mixed_t,
    rstd_o,
    d_pre,
    x_s,
    gate_s,
    q_s,
    km,
    vm,
    w_s,
    s_s,
    bias_s,
    a_acc,
    dq_acc,
    da_s,
    da_t,
    q_t,
    dk_t,
    dv_t,
):
    hist_rows = out_hist.shape[0]
    tgt_rows = out_tgt.shape[0]
    feature = out_hist.shape[1]
    blocks = hist_rows // BLK
    lane = lax.broadcasted_iota(jnp.int32, (1, 128), 1)
    low_half = jnp.where(lane < 64, 1.0, 0.0).astype(F32)
    halves = (low_half, 1.0 - low_half)

    def project(r0, size, table, hits):
        rows = pl.ds(r0, size)
        onehot = jnp.where(hits, 1.0, 0.0).astype(BF16)
        x = mm(onehot, table[...])
        x_s[rows, :] = x.astype(BF16)
        centred, rstd = moments(x)
        normed = centred * rstd
        rstd_o[rows, :] = rstd
        normed_t[:, rows] = normed.T.astype(BF16)
        normed = normed.astype(BF16)
        normed_o[rows, :] = normed
        for part in range(4):
            half = mm(normed, w_proj[:, part * feature : (part + 1) * feature]) * 0.5
            t = jnp.tanh(half)
            u = 1.0 + t
            act = half * u
            slope = 0.5 * u * (1.0 + half * (1.0 - t))
            d_pre[rows, part * feature : (part + 1) * feature] = slope.astype(BF16)
            if part == 0:
                gate_s[rows, :] = act.astype(BF16)
            elif part == 2:
                q_s[rows, :] = (act.astype(BF16) * 0.0625).astype(BF16)
            else:
                dest = vm if part == 1 else km
                for head in range(HEADS):
                    pair = act[:, (head // 2) * 128 : (head // 2 + 1) * 128]
                    dest[head, rows, :] = (pair * halves[head % 2]).astype(BF16)

    def project_hist(i, carry):
        r0 = pl.multiple_of(i * BLK, BLK)
        row = r0 + lax.broadcasted_iota(jnp.int32, (BLK, 1), 0)
        project(r0, BLK, arrived, pos_row[...] == row)
        return carry

    lax.fori_loop(0, blocks, project_hist, 0)
    col = lax.broadcasted_iota(jnp.int32, (1, cand.shape[0]), 1)
    project(hist_rows, tgt_rows, cand, tid_col[...] == col)
    dk_t[...] = jnp.zeros_like(dk_t)
    dv_t[...] = jnp.zeros_like(dv_t)

    def forward(r0, size, slot, k0, width, bias):
        rows, keys = pl.ds(r0, size), pl.ds(k0, width)
        bias_s[:size, :width] = bias
        for pair in range(HEADS // 2):
            cols = slice(pair * 128, (pair + 1) * 128)
            total = a_acc[:size, cols]
            for head in (2 * pair, 2 * pair + 1):
                half = mm(q_s[rows, cols], km[head, keys, :], NT) + bias_s[:size, :width]
                t = jnp.tanh(half)
                u = 1.0 + t
                weight = (half * u).astype(BF16)
                w_s[slot, head, :size, :width] = weight
                slope = 0.5 * u * (1.0 + half * (1.0 - t))
                s_s[slot, head, :size, :width] = slope.astype(BF16)
                total = total + mm(weight, vm[head, keys, :])
            a_acc[:size, cols] = total

    def backward(size, slot, k0, width):
        keys = pl.ds(k0, width)
        for pair in range(HEADS // 2):
            cols = slice(pair * 128, (pair + 1) * 128)
            total = dq_acc[:size, cols]
            for head in (2 * pair, 2 * pair + 1):
                d_weight = mm(da_s[:size, cols], vm[head, keys, :], NT)
                d_score = d_weight * s_s[slot, head, :size, :width].astype(F32)
                d_score = d_score.astype(BF16)
                total = total + mm(d_score, km[head, keys, :])
                own = slice(head * 64, (head + 1) * 64)
                dv_t[own, keys] += mm(da_t[own, :size], w_s[slot, head, :size, :width])
                dk_t[own, keys] += mm(q_t[own, :size], d_score)
            dq_acc[:size, cols] = total

    def middle(r0, size, out_ref, g_ref, o0):
        rows, own = pl.ds(r0, size), pl.ds(o0, size)
        centred, rstd = moments(a_acc[:size, :])
        normed = centred * rstd
        gate = gate_s[rows, :].astype(F32)
        mixed = normed * gate
        mixed_t[:, rows] = mixed.T.astype(BF16)
        update = mm(mixed.astype(BF16), w_out[...])
        out_ref[own, :] = (x_s[rows, :].astype(F32) + update).astype(BF16)
        d_mixed = mm(g_ref[own, :], w_out[...], NT)
        d_gate = d_mixed * normed * d_pre[rows, :feature].astype(F32)
        d_pre[rows, :feature] = d_gate.astype(BF16)
        d_normed = d_mixed * gate
        mean_d = jnp.mean(d_normed, axis=-1, keepdims=True)
        mean_dn = jnp.mean(d_normed * normed, axis=-1, keepdims=True)
        d_att = rstd * (d_normed - mean_d - normed * mean_dn)
        da_s[:size, :] = d_att.astype(BF16)
        da_t[:, :size] = d_att.T.astype(BF16)
        q_t[:, :size] = q_s[rows, :].astype(F32).T.astype(BF16)

    def finish(r0, size):
        rows, cols = pl.ds(r0, size), slice(2 * feature, 3 * feature)
        d_q = dq_acc[:size, :] * 0.125 * d_pre[rows, cols].astype(F32)
        d_pre[rows, cols] = d_q.astype(BF16)

    def bias_of(r0, size, k0):
        rows = pl.ds(r0, size)
        key = k0 + lax.broadcasted_iota(jnp.int32, (1, BLK), 1)
        allowed = (key >= lo[rows, :]) & (key <= hi[rows, :])
        return jnp.where(allowed, 0.0, MASKED).astype(F32)

    def hist_block(i, carry):
        r0 = pl.multiple_of(i * BLK, BLK)
        first = first_ref[i]
        a_acc[...] = jnp.zeros_like(a_acc)
        dq_acc[...] = jnp.zeros_like(dq_acc)

        def fwd(j, c):
            k0 = pl.multiple_of(j * BLK, BLK)
            forward(r0, BLK, j, k0, BLK, bias_of(r0, BLK, k0))
            return c

        def bwd(j, c):
            backward(BLK, j, pl.multiple_of(j * BLK, BLK), BLK)
            return c

        lax.fori_loop(first, i + 1, fwd, 0)
        middle(r0, BLK, out_hist, g_hist, r0)
        lax.fori_loop(first, i + 1, bwd, 0)
        finish(r0, BLK)
        return carry

    lax.fori_loop(0, blocks, hist_block, 0)

    a_acc[...] = jnp.zeros_like(a_acc)
    dq_acc[...] = jnp.zeros_like(dq_acc)

    def fwd_tgt(j, c):
        k0 = pl.multiple_of(j * BLK, BLK)
        forward(hist_rows, tgt_rows, j, k0, BLK, bias_of(hist_rows, tgt_rows, k0))
        return c

    def bwd_tgt(j, c):
        backward(tgt_rows, j, pl.multiple_of(j * BLK, BLK), BLK)
        return c

    lax.fori_loop(0, blocks, fwd_tgt, 0)
    same = lax.broadcasted_iota(jnp.int32, (tgt_rows, tgt_rows), 0) == lax.broadcasted_iota(
        jnp.int32, (tgt_rows, tgt_rows), 1
    )
    forward(
        hist_rows, tgt_rows, blocks, hist_rows, tgt_rows, jnp.where(same, 0.0, MASKED).astype(F32)
    )
    middle(hist_rows, tgt_rows, out_tgt, g_tgt, 0)
    lax.fori_loop(0, blocks, bwd_tgt, 0)
    backward(tgt_rows, blocks, hist_rows, tgt_rows)
    finish(hist_rows, tgt_rows)

    def spread(r0, size):
        rows = pl.ds(r0, size)
        vals, keys = slice(feature, 2 * feature), slice(3 * feature, 4 * feature)
        d_val = dv_t[:, rows].T * d_pre[rows, vals].astype(F32)
        d_pre[rows, vals] = d_val.astype(BF16)
        d_key = dk_t[:, rows].T * 2.0 * d_pre[rows, keys].astype(F32)
        d_pre[rows, keys] = d_key.astype(BF16)

    def spread_hist(i, carry):
        spread(pl.multiple_of(i * BLK, BLK), BLK)
        return carry

    lax.fori_loop(0, blocks, spread_hist, 0)
    spread(hist_rows, tgt_rows)


def weights_kernel(normed_t, mixed_t, d_pre, g_hist, g_tgt, d_proj, d_out):
    hist_rows = g_hist.shape[0]
    for part in range(d_proj.shape[1] // 512):
        cols = slice(part * 512, (part + 1) * 512)
        d_proj[:, cols] = mm(normed_t[...], d_pre[:, cols]).astype(BF16)
    total = mm(mixed_t[:, :hist_rows], g_hist[...])
    total = total + mm(mixed_t[:, hist_rows:], g_tgt[...])
    d_out[...] = total.astype(BF16)


def rows_kernel(
    d_pre, w_proj, normed, rstd, g_hist, g_tgt, pos_col, slot_grads, d_tgt, d_hist
):
    hist_rows = g_hist.shape[0]
    tgt_rows = g_tgt.shape[0]

    def back(r0, size, g_ref, out_ref, o0):
        rows, own = pl.ds(r0, size), pl.ds(o0, size)
        d_normed = mm(d_pre[rows, :], w_proj[...], NT)
        unit = normed[rows, :].astype(F32)
        mean_d = jnp.mean(d_normed, axis=-1, keepdims=True)
        mean_dn = jnp.mean(d_normed * unit, axis=-1, keepdims=True)
        d_x = rstd[rows, :] * (d_normed - mean_d - unit * mean_dn)
        out_ref[own, :] = (d_x + g_ref[own, :].astype(F32)).astype(BF16)

    back(hist_rows, tgt_rows, g_tgt, d_tgt, 0)

    def back_hist(i, carry):
        r0 = pl.multiple_of(i * BLK, BLK)
        back(r0, BLK, g_hist, d_hist, r0)
        return carry

    lax.fori_loop(0, hist_rows // BLK, back_hist, 0)

    def pick(i, carry):
        r0 = pl.multiple_of(i * BLK, BLK)
        row = lax.broadcasted_iota(jnp.int32, (1, hist_rows), 1)
        onehot = jnp.where(pos_col[pl.ds(r0, BLK), :] == row, 1.0, 0.0).astype(BF16)
        slot_grads[pl.ds(r0, BLK), :] = mm(onehot, d_hist[...]).astype(BF16)
        return carry

    lax.fori_loop(0, slot_grads.shape[0] // BLK, pick, 0)


def cand_kernel(own_ids, picked, rows, out):
    hits = own_ids[...] == picked[...]
    out[...] = mm(jnp.where(hits, 1.0, 0.0).astype(BF16), rows[...])


VMEM = pl.BlockSpec(memory_space=pltpu.VMEM)
SMEM = pl.BlockSpec(memory_space=pltpu.SMEM)


def params(mib):
    return pltpu.CompilerParams(vmem_limit_bytes=mib << 20)


AXES = {"z": (4, 32), "c": (2, 16), "x": (4, 4), "y": (4, 1)}


def local(
    send_rows, slot_pos, lengths, candidates, target_ids, w_proj, w_out, g_hist, g_tgt
):
    peers, capacity, feature = send_rows.shape[1:]
    slots = peers * capacity
    hist_rows, tgt_rows = g_hist.shape[0], g_tgt.shape[0]
    all_rows = hist_rows + tgt_rows
    users, tgt_each = target_ids.shape
    table = lax.all_gather(candidates, "mem", axis=0, tiled=True)
    arrived = lax.all_to_all(send_rows, BOTH, split_axis=1, concat_axis=0, tiled=True)
    arrived = arrived.reshape(slots, feature)

    pos_row = slot_pos.reshape(1, slots)
    pos_col = slot_pos.reshape(slots, 1)
    ends = jnp.cumsum(lengths[0])
    starts = ends - lengths[0]
    row = jnp.arange(hist_rows)[:, None]
    hist_lo = jnp.max(jnp.where(row >= starts[None, :], starts[None, :], 0), axis=1)
    lo = jnp.concatenate([hist_lo, jnp.repeat(starts, tgt_each)]).astype(jnp.int32)[:, None]
    hi = jnp.concatenate([jnp.arange(hist_rows), jnp.repeat(ends - 1, tgt_each)])
    hi = hi.astype(jnp.int32)[:, None]
    first = (hist_lo[::BLK] // BLK).astype(jnp.int32)

    sds = jax.ShapeDtypeStruct
    out_hist, out_tgt, normed, normed_t, mixed_t, rstd, d_pre = pl.pallas_call(
        layer_kernel,
        out_shape=(
            sds((hist_rows, feature), BF16),
            sds((tgt_rows, feature), BF16),
            sds((all_rows, feature), BF16),
            sds((feature, all_rows), BF16),
            sds((feature, all_rows), BF16),
            sds((all_rows, 1), F32),
            sds((all_rows, 4 * feature), BF16),
        ),
        in_specs=[SMEM] + [VMEM] * 10,
        out_specs=(VMEM,) * 7,
        scratch_shapes=[
            pltpu.VMEM((all_rows, feature), BF16),
            pltpu.VMEM((all_rows, feature), BF16),
            pltpu.VMEM((all_rows, feature), BF16),
            pltpu.VMEM((HEADS, all_rows, 128), BF16),
            pltpu.VMEM((HEADS, all_rows, 128), BF16),
            pltpu.VMEM((hist_rows // BLK + 1, HEADS, BLK, BLK), BF16),
            pltpu.VMEM((hist_rows // BLK + 1, HEADS, BLK, BLK), BF16),
            pltpu.VMEM((BLK, BLK), F32),
            pltpu.VMEM((BLK, feature), F32),
            pltpu.VMEM((BLK, feature), F32),
            pltpu.VMEM((BLK, feature), BF16),
            pltpu.VMEM((feature, BLK), BF16),
            pltpu.VMEM((feature, BLK), BF16),
            pltpu.VMEM((feature, all_rows), F32),
            pltpu.VMEM((feature, all_rows), F32),
        ],
        compiler_params=params(58),
        name="layer",
    )(
        first,
        arrived,
        pos_row,
        table,
        target_ids.reshape(tgt_rows, 1),
        lo,
        hi,
        w_proj,
        w_out,
        g_hist,
        g_tgt,
    )

    d_proj, d_out = pl.pallas_call(
        weights_kernel,
        out_shape=(sds(w_proj.shape, BF16), sds(w_out.shape, BF16)),
        in_specs=[VMEM] * 5,
        out_specs=(VMEM, VMEM),
        compiler_params=params(40),
        name="weights",
    )(normed_t, mixed_t, d_pre, g_hist, g_tgt)

    slot_grads, d_tgt = pl.pallas_call(
        rows_kernel,
        out_shape=(sds((slots, feature), BF16), sds((tgt_rows, feature), BF16)),
        in_specs=[VMEM] * 7,
        out_specs=(VMEM, VMEM),
        scratch_shapes=[pltpu.VMEM((hist_rows, feature), BF16)],
        compiler_params=params(40),
        name="rows",
    )(d_pre, w_proj, normed, rstd, g_hist, g_tgt, pos_col)

    sum_proj, sum_out = reduce_weights(d_proj, d_out)

    returned = lax.all_to_all(
        slot_grads.reshape(peers, 1, capacity, feature),
        BOTH,
        split_axis=0,
        concat_axis=1,
        tiled=True,
    )

    picked = lax.all_gather(target_ids.reshape(1, tgt_rows), "mem", axis=1, tiled=True)
    tgt_grads = lax.all_gather(d_tgt, "mem", axis=0, tiled=True)
    mine = lax.axis_index("mem") * candidates.shape[0] + jnp.arange(
        candidates.shape[0], dtype=jnp.int32
    )
    d_cand = pl.pallas_call(
        cand_kernel,
        out_shape=sds(candidates.shape, F32),
        in_specs=[VMEM] * 3,
        out_specs=VMEM,
        name="cand",
    )(mine.astype(jnp.int32)[:, None], picked, tgt_grads)
    return (out_hist, out_tgt, returned, d_cand, sum_proj, sum_out)


def reduce_weights(d_proj, d_out):
    both = jnp.concatenate([d_proj.reshape(2048, 512), d_out], axis=0).reshape(128, 16, 1280 // 2)
    both = lax.all_to_all(both, BOTH, split_axis=0, concat_axis=0, tiled=True)
    total = jnp.sum(both.astype(F32), axis=0).astype(BF16)
    gathered = lax.all_gather(total, "mem", axis=0, tiled=True)
    gathered = lax.all_gather(gathered, "grp", axis=0, tiled=True)
    gathered = gathered.reshape(2560, 512).astype(F32)
    return gathered[:2048].reshape(512, 2048), gathered[2048:]


def solution(mesh):
    placed = (
        P(BOTH, None, None, None),
        P(BOTH, None, None),
        P(BOTH, None),
        P(BOTH, None),
        P(BOTH, None),
        P(),
        P(),
        P(BOTH, None),
        P(BOTH, None),
    )
    return jax.shard_map(
        local,
        mesh=mesh,
        in_specs=placed,
        out_specs=(
            P(BOTH, None),
            P(BOTH, None),
            P(BOTH, None, None, None),
            P(BOTH, None),
            P(),
            P(),
        ),
        check_vma=False,
    )
```

time: 500 us -> 314 us (0.63)
  waiting for transfers between devices: 241 us -> 42.7 us
  blocking collectives: 0 us -> 110 us
  matrix products: 103 us -> 0 us
  Pallas kernels: 0 us -> 78 us
  local copies, waits for them, and re-layouts: 78 us -> 41.2 us
  other arithmetic: 36.7 us -> 3.61 us
    psum x1 -> x0, waiting for transfers between devices: 162 us -> none  [local(): lax.psum((grad_proj.astype(jnp.float32), grad_out.astype(jnp.float32)), (...]
    dot_general x25 -> x0, matrix products: 103 us -> none  [the longest x9 40.3 us: attend_block(): jnp.einsum('hqk,khe->qhe', weights, val_rows, preferred_element_type=jnp....]
    pallas_call x0 -> x4, Pallas kernels: none -> 78 us  [the longest x1 61.6 us: local(): pl.pallas_call(layer_kernel, out_shape=(sds((hist_rows, feature), BF16),...]
    all_gather x0 -> x2, blocking collectives: none -> 57.5 us  [the longest x1 37.9 us: local(): lax.all_gather(target_ids.reshape(1, tgt_rows), 'mem', axis=1, tiled=True)]
    all_to_all x0 -> x1, blocking collectives: none -> 52.1 us  [reduce_weights(): both = lax.all_to_all(both, BOTH, split_axis=0, concat_axis=0, tiled=True)]
    all_to_all x2, waiting for transfers between devices: 55 us -> 26.1 us  [the longest x1 26.1 us: local(): lax.all_to_all(send_rows, BOTH, split_axis=1, concat_axis=0, tiled=True)]
    reduce_scatter x1 -> x0, waiting for transfers between devices: 19 us -> none  [local(): lax.psum_scatter(jnp.dot(onehot, tangent_rows, precision=lax.Precision.HI...]
    add_any x6 -> x0, other arithmetic: 15.2 us -> none  [the longest x1 7.37 us: sequence_layer(): jax.nn.silu(jnp.dot(normed, w_proj, preferred_element_type=jnp.float32))]
  transfers between devices with their start and end apart: 5 -> 5, of which waited for: 5 -> 2; matrix products, arithmetic and copies ran while one was open for 9% -> 5% of each run, Pallas kernels for 0% -> 2%
where the time goes in v1:
time: 314 us; the launch traced here: 311 us
  blocking collectives  110 us (35%)
  Pallas kernels  78 us (25%)
  waiting for transfers between devices  42.7 us (14%)
  local copies, waits for them, and re-layouts  41.2 us (13%)
  starting transfers between devices  22.1 us (7%)
  between operations  13.9 us (4%)
  other arithmetic  3.61 us (1%)
    pallas_call x1, Pallas kernels, local(): pl.pallas_call(layer_kernel, out_shape=(sds((hist_rows, feature), BF16),...  61.6 us
    all_to_all x1, blocking collectives, reduce_weights(): both = lax.all_to_all(both, BOTH, split_axis=0, concat_axis=0, tiled=True)  52.1 us
    all_gather x1, blocking collectives, local(): lax.all_gather(target_ids.reshape(1, tgt_rows), 'mem', axis=1, tiled=True)  37.9 us
    all_to_all x1, waiting for transfers between devices, local(): lax.all_to_all(send_rows, BOTH, split_axis=1, concat_axis=0, tiled=True)  26.1 us
    all_gather x1, blocking collectives, reduce_weights(): gathered = lax.all_gather(total, 'mem', axis=0, tiled=True)  19.5 us
    all_gather x1, waiting for transfers between devices, local(): table = lax.all_gather(candidates, 'mem', axis=0, tiled=True)  15.9 us
    all_to_all x1, starting transfers between devices, local(): lax.all_to_all(send_rows, BOTH, split_axis=1, concat_axis=0, tiled=True)  12 us
    unnamed x30, local copies, waits for them, and re-layouts  11.8 us
  transfers between devices with their start and end apart: 5, of which 2 were waited for; matrix products, arithmetic and copies ran while one was open for 5% of the time, Pallas kernels for 2%

profile of v1, /device:TPU:1, one launch (start us, length us, event | category | flops | bytes accessed | tf_op | source)
XLA Modules:
  0.0 311.2 jit_solution(1766833159294341486)
XLA Ops:
  7.2 0.7 all-gather.4.cloned.1.call-update
  7.9 12.0 %all-to-all-start = ((bf16[1,128,16,512]{3,2,0,1:T(8,128)(2,1)}), bf16[1,128,16,512]{3,2,0,1:T(8,128)(2,1)}, u32[]{:S(2)}, u32[]{:S(2)}) async-start(bf16[1,128,16,512]{3,2,0,1:T(8,128)(2,1)} %bitcast.19), calls=%async_computation | async-start | bytes 4194304 | tf_op jit(solution)/shard_map/all_to_all | solution.py:307
  20.1 0.7 reshape.75.pos_row
  22.0 0.7 reshape.87.tid_col
  22.8 1.0 broadcast_in_dim.32.hi
  23.8 1.0 broadcast_in_dim.31.lo
  25.4 26.1 %all-to-all-done = bf16[1,128,16,512]{3,2,0,1:T(8,128)(2,1)} async-done(((bf16[1,128,16,512]{3,2,0,1:T(8,128)(2,1)}), bf16[1,128,16,512]{3,2,0,1:T(8,128)(2,1)}, u32[]{:S(2)}, u32[]{:S(2)}) %all-to-all-start) | async-done | bytes 2097184 | tf_op jit(solution)/shard_map/all_to_all | solution.py:307
  51.4 15.9 %all-gather.4.cloned.1.call-done.cand = bf16[2048,512]{1,0:T(8,128)(2,1)} async-done(((bf16[128,512]{1,0:T(8,128)(2,1)}), bf16[2048,512]{1,0:T(8,128)(2,1)}) %all-gather.4.cloned.1.call-update) | async-done | bytes 2097168 | tf_op jit(solution)/shard_map/all_gather | solution.py:306
  67.3 61.6 %layer.1 = (bf16[1024,512]{1,0:T(8,128)(2,1)}, bf16[128,512]{1,0:T(8,128)(2,1)}, bf16[1152,512]{1,0:T(8,128)(2,1)}, bf16[512,1152]{1,0:T(8,128)(2,1)}, bf16[512,...) custom-call(s32[4]{0:T(128)} %and_select_fusion.first_ref, bf16[2048,512]{1,0:T(8,128)(2,1)} %bitcast.4.arrived, ...), custom_call_target="tpu_custom_call" | custom-call | tf_op jit(solution)/shard_map/layer/pallas_call | solution.py:322
  129.0 2.3 copy-done
  131.3 1.3 copy-done.7
  132.6 1.1 copy-done.8
  133.6 10.1 %rows.1 = (bf16[2048,512]{1,0:T(8,128)(2,1)}, bf16[128,512]{1,0:T(8,128)(2,1)}) custom-call(bf16[1152,2048]{1,0:T(8,128)(2,1)S(1)} %copy-done, bf16[512,2048]{1,0:T(8,128)(2,1)S(1)} %copy-done.3, bf16[1152,512]{1,0:T(8,128)(2,1)S(1)} %copy-done.7, f32[1152,1]{1,0:T(8,128)S(1)} %copy-done.8, bf16[1024,512]{1,0:T(8,128)(2,1)S(1)} %copy-done.2, ...), custom_call_target="tpu_custom_call" | custom-call | tf_op jit(solution)/shard_map/rows/pallas_call | solution.py:377
  144.0 2.3 copy-done.1
  146.3 1.3 copy-done.5
  147.6 1.3 copy-done.6
  148.8 3.5 %weights.1 = (bf16[512,2048]{1,0:T(8,128)(2,1)S(1)}, bf16[512,512]{1,0:T(8,128)(2,1)S(1)}) custom-call(bf16[512,1152]{1,0:T(8,128)(2,1)S(1)} %copy-done.5, bf16[512,1152]{1,0:T(8,128)(2,1)S(1)} %copy-done.6, bf16[1152,2048]{1,0:T(8,128)(2,1)S(1)} %copy-done.1, bf16[1024,512]{1,0:T(8,128)(2,1)S(1)} %copy-done.2, bf16[128,512]{1,0:T(8,128)(2,1)S(1)} %copy-done.4), custom_call_target="tpu_custom_call" | custom-call | tf_op jit(solution)/shard_map/weights/pallas_call | solution.py:368
  152.4 0.8 copy-done.9
  153.2 2.5 reshape.83
  155.7 1.8 pad_maximum_fusion
  157.5 3.5 %reshape.84 = bf16[128,16,640]{2,1,0:T(8,128)(2,1)} reshape(bf16[2560,512]{1,0:T(8,128)(2,1)S(1)} %pad_maximum_fusion) | data formatting | bytes 5242880 | tf_op jit(solution)/shard_map/reshape | solution.py:413
  161.0 52.1 %all_to_all.26 = bf16[128,16,640]{2,1,0:T(8,128)(2,1)S(1)} all-to-all(bf16[128,16,640]{2,1,0:T(8,128)(2,1)} %reshape.84), channel_id=1, replica_groups=mesh['grp'=8,'mem'=16] {'grp','mem'}, dimensions={0} | all-to-all | bytes 5242880 | tf_op jit(solution)/shard_map/all_to_all | solution.py:414
  213.6 19.5 %all_gather.18 = bf16[256,640]{1,0:T(8,128)(2,1)} all-gather(bf16[16,640]{1,0:T(8,128)(2,1)S(1)} %reduce_sum.12), channel_id=1, replica_groups=mesh['grp'=8,'mem'=16] {'mem'}, dimensions={0}, use_global_device_ids=true | all-gather | bytes 348160 | tf_op jit(solution)/shard_map/all_gather | solution.py:416
  233.1 9.9 %all-to-all-start.1 = ((bf16[128,1,16,512]{3,2,1,0:T(8,128)(2,1)}), bf16[128,1,16,512]{3,2,1,0:T(8,128)(2,1)S(1)}, u32[]{:S(2)}, u32[]{:S(2)}) async-start(bf16[128,1,16,512]{3,2,1,0:T(8,128)(2,1)} %bitcast.8), calls=%async_computation.1 | async-start | bytes 4194304 | tf_op jit(solution)/shard_map/all_to_all | solution.py:389
  243.1 37.9 %all_gather.16.picked = s32[1,2048]{1,0:T(1,128)} all-gather(s32[1,128]{1,0:T(1,128)S(1)} %reshape.82), channel_id=1, replica_groups=mesh['grp'=8,'mem'=16] {'mem'}, dimensions={1}, use_global_device_ids=true | all-gather | bytes 8704 | tf_op jit(solution)/shard_map/all_gather | solution.py:397
  281.1 0.6 iota_add_fusion.own_ids
  281.7 2.8 cand.1
  284.5 6.3 %reshape.86 = f32[2560,512]{1,0:T(8,128)} reshape(bf16[2048,640]{1,0:T(8,128)(2,1)} %all-gather.8.cloned.1.call-done) | data formatting | bytes 7864320 | tf_op jit(solution)/shard_map/convert_element_type | solution.py:418
  290.8 2.3 slice.13
  293.1 4.7 %slice.12 = f32[2048,512]{1,0:T(8,128)} slice(f32[2560,512]{1,0:T(8,128)} %reshape.86), slice={[0:2048], [0:512]} | slice | bytes 8388608 | tf_op jit(solution)/shard_map/slice | solution.py:419
  297.7 5.6 %reshape.85 = f32[512,2048]{1,0:T(8,128)} reshape(f32[2048,512]{1,0:T(8,128)} %slice.12) | data formatting | bytes 8388608 | tf_op jit(solution)/shard_map/reshape | solution.py:419
  303.3 1.3 copy.41
  (46 shorter events, 2.7 us)
Async XLA Ops:
  7.2 12.8 %copy-start.12 = (s32[1,128,16]{1,2,0:T(8,128)S(1)}, s32[1,128,16]{1,2,0:T(8,128)}, u32[]{:S(2)}) copy-start(s32[1,128,16]{1,2,0:T(8,128)} %param.10) | copy-start | bytes 24580
  7.2 60.2 %all-gather.4.cloned.1.call-start = ((), (), s32[]{:S(2)}) async-start(), calls=%async_computation.3 | async-start | bytes 2228224 | tf_op jit(solution)/shard_map/all_gather | solution.py:306
  7.9 13.4 %copy-start.13 = (s32[1,8]{1,0:T(1,128)S(1)}, s32[1,8]{1,0:T(1,128)}, u32[]{:S(2)}) copy-start(s32[1,8]{1,0:T(1,128)} %param.11) | copy-start | bytes 100
  7.9 14.1 %copy-start.11 = (s32[8,16]{1,0:T(8,128)S(1)}, s32[8,16]{1,0:T(8,128)}, u32[]{:S(2)}) copy-start(s32[8,16]{1,0:T(8,128)} %param.13) | copy-start | bytes 1540
  7.9 43.5 %all-to-all-start = ((bf16[1,128,16,512]{3,2,0,1:T(8,128)(2,1)}), bf16[1,128,16,512]{3,2,0,1:T(8,128)(2,1)}, u32[]{:S(2)}, u32[]{:S(2)}) async-start(bf16[1,128,16,512]{3,2,0,1:T(8,128)(2,1)} %bitcast.19), calls=%async_computation | async-start | bytes 4194304 | tf_op jit(solution)/shard_map/all_to_all | solution.py:307
  19.9 261.8 %all-gather.6.cloned.1.call-start = ((), (), s32[]{:S(2)}) async-start(), calls=%async_computation.4 | async-start | bytes 2228224 | tf_op jit(solution)/shard_map/all_gather | solution.py:398
  67.3 61.6 %copy-start.2 = (bf16[1024,512]{1,0:T(8,128)(2,1)S(1)}, bf16[1024,512]{1,0:T(8,128)(2,1)}, u32[]{:S(2)}) copy-start(bf16[1024,512]{1,0:T(8,128)(2,1)} %g_hist.5) | copy-start | bytes 3145732
  67.3 61.6 %copy-start.3 = (bf16[512,2048]{1,0:T(8,128)(2,1)S(1)}, bf16[512,2048]{1,0:T(8,128)(2,1)}, u32[]{:S(2)}) copy-start(bf16[512,2048]{1,0:T(8,128)(2,1)} %w_proj.3) | copy-start | bytes 6291460
  67.3 61.6 %copy-start.4 = (bf16[128,512]{1,0:T(8,128)(2,1)S(1)}, bf16[128,512]{1,0:T(8,128)(2,1)}, u32[]{:S(2)}) copy-start(bf16[128,512]{1,0:T(8,128)(2,1)} %g_tgt.5) | copy-start | bytes 393220
  129.0 2.3 copy-start
  131.3 1.3 copy-start.7
  132.6 1.1 copy-start.8
  143.7 140.8 %all-gather.8.cloned.1.call-start = ((), (), s32[]{:S(2)}) async-start(), calls=%async_computation.5 | async-start | bytes 2949120 | tf_op jit(solution)/shard_map/all_gather | solution.py:417
  144.0 2.3 copy-start.1
  146.3 1.3 copy-start.5
  147.6 1.3 copy-start.6
  152.4 0.8 copy-start.9
  153.2 2.5 copy-start.10
  233.1 48.6 %all-to-all-start.1 = ((bf16[128,1,16,512]{3,2,1,0:T(8,128)(2,1)}), bf16[128,1,16,512]{3,2,1,0:T(8,128)(2,1)S(1)}, u32[]{:S(2)}, u32[]{:S(2)}) async-start(bf16[128,1,16,512]{3,2,1,0:T(8,128)(2,1)} %bitcast.8), calls=%async_computation.1 | async-start | bytes 4194304 | tf_op jit(solution)/shard_map/all_to_all | solution.py:389
Sparse Core Ops, SparseCore 0:
  10.2 57.1 all-gather.3
  143.9 64.3 all-gather.5
  233.3 48.6 all-gather.7

commit v2 on v1

v2 whole, which is shorter than its diff:
```python
import jax
import jax.numpy as jnp
from jax import lax
from jax.experimental import pallas as pl
from jax.experimental.pallas import tpu as pltpu
from jax.sharding import PartitionSpec as P

HEADS = 8
EPS = 1e-05
BLK = 256
MASKED = -1e9
F32 = jnp.float32
BF16 = jnp.bfloat16
BOTH = ("grp", "mem")
NN = (((1,), (0,)), ((), ()))
NT = (((1,), (1,)), ((), ()))


def mm(left, right, dims=NN):
    return lax.dot_general(left, right, dims, preferred_element_type=F32)


def moments(values):
    centred = values - jnp.mean(values, axis=-1, keepdims=True)
    variance = jnp.mean(centred * centred, axis=-1, keepdims=True)
    return centred, lax.rsqrt(variance + EPS)


def head_masks():
    lane = lax.broadcasted_iota(jnp.int32, (1, 128), 1)
    low_half = jnp.where(lane < 64, 1.0, 0.0).astype(F32)
    return (low_half, 1.0 - low_half)


def silu_parts(half):
    t = jnp.tanh(half)
    u = 1.0 + t
    return half * u, 0.5 * u * (1.0 + half * (1.0 - t))


def one_hot(hits):
    return jnp.where(hits, 1.0, 0.0).astype(BF16)


def split_heads(act, dest, rows):
    halves = head_masks()
    for head in range(HEADS):
        pair = act[:, (head // 2) * 128 : (head // 2 + 1) * 128]
        dest[head, rows, :] = (pair * halves[head % 2]).astype(BF16)


def score_bias(lo, hi, k0):
    key = k0 + lax.broadcasted_iota(jnp.int32, (1, BLK), 1)
    allowed = (key >= lo) & (key <= hi)
    return jnp.where(allowed, 0.0, MASKED).astype(F32)


def forward(q_ref, rows, size, km, vm, keys, width, w_s, s_s, slot, bias_s, a_acc):
    for pair in range(HEADS // 2):
        cols = slice(pair * 128, (pair + 1) * 128)
        total = a_acc[:size, cols]
        for head in (2 * pair, 2 * pair + 1):
            half = mm(q_ref[rows, cols], km[head, keys, :], NT) + bias_s[:size, :width]
            weight, slope = silu_parts(half)
            weight = weight.astype(BF16)
            w_s[slot, head, :size, :width] = weight
            s_s[slot, head, :size, :width] = slope.astype(BF16)
            total = total + mm(weight, vm[head, keys, :])
        a_acc[:size, cols] = total


def backward(size, km, vm, keys, width, w_s, s_s, slot, da_s, da_t, q_t, dq_acc, dk_t, dv_t):
    for pair in range(HEADS // 2):
        cols = slice(pair * 128, (pair + 1) * 128)
        total = dq_acc[:size, cols]
        for head in (2 * pair, 2 * pair + 1):
            d_weight = mm(da_s[:size, cols], vm[head, keys, :], NT)
            d_score = d_weight * s_s[slot, head, :size, :width].astype(F32)
            d_score = d_score.astype(BF16)
            total = total + mm(d_score, km[head, keys, :])
            own = slice(head * 64, (head + 1) * 64)
            dv_t[own, keys] += mm(da_t[own, :size], w_s[slot, head, :size, :width])
            dk_t[own, keys] += mm(q_t[own, :size], d_score)
        dq_acc[:size, cols] = total


def middle(attended, x, gate, g, w_out):
    centred, rstd = moments(attended)
    normed = centred * rstd
    mixed = normed * gate
    out = (x + mm(mixed.astype(BF16), w_out)).astype(BF16)
    d_mixed = mm(g, w_out, NT)
    d_normed = d_mixed * gate
    mean_d = jnp.mean(d_normed, axis=-1, keepdims=True)
    mean_dn = jnp.mean(d_normed * normed, axis=-1, keepdims=True)
    d_att = rstd * (d_normed - mean_d - normed * mean_dn)
    return out, mixed, d_mixed * normed, d_att


def hist_kernel(
    first_ref,
    arrived,
    pos_row,
    lo,
    hi,
    w_proj,
    w_out,
    g_hist,
    out_hist,
    normed_o,
    rstd_o,
    normed_t,
    mixed_t,
    km,
    vm,
    dk_t,
    dv_t,
    d_gq,
    sl_vk,
    x_s,
    gate_s,
    q_s,
    w_s,
    s_s,
    bias_s,
    a_acc,
    dq_acc,
    da_s,
    da_t,
    q_t,
):
    hist_rows, feature = out_hist.shape
    blocks = hist_rows // BLK
    first_cols, last_cols = slice(0, feature), slice(feature, 2 * feature)

    def project(i, carry):
        r0 = pl.multiple_of(i * BLK, BLK)
        rows = pl.ds(r0, BLK)
        row = r0 + lax.broadcasted_iota(jnp.int32, (BLK, 1), 0)
        x = mm(one_hot(pos_row[...] == row), arrived[...])
        x_s[rows, :] = x.astype(BF16)
        centred, rstd = moments(x)
        normed = centred * rstd
        rstd_o[rows, :] = rstd
        normed_t[:, rows] = normed.T.astype(BF16)
        normed = normed.astype(BF16)
        normed_o[rows, :] = normed
        for part in range(4):
            half = mm(normed, w_proj[:, part * feature : (part + 1) * feature]) * 0.5
            act, slope = silu_parts(half)
            slope = slope.astype(BF16)
            if part == 0:
                gate_s[rows, :] = act.astype(BF16)
                d_gq[rows, first_cols] = slope
            elif part == 1:
                split_heads(act, vm, rows)
                sl_vk[rows, first_cols] = slope
            elif part == 2:
                q_s[rows, :] = (act.astype(BF16) * 0.0625).astype(BF16)
                d_gq[rows, last_cols] = slope
            else:
                split_heads(act, km, rows)
                sl_vk[rows, last_cols] = slope
        return carry

    lax.fori_loop(0, blocks, project, 0)
    dk_t[...] = jnp.zeros_like(dk_t)
    dv_t[...] = jnp.zeros_like(dv_t)

    def hist_block(i, carry):
        r0 = pl.multiple_of(i * BLK, BLK)
        rows = pl.ds(r0, BLK)
        first = first_ref[i]
        a_acc[...] = jnp.zeros_like(a_acc)
        dq_acc[...] = jnp.zeros_like(dq_acc)

        def fwd(j, c):
            k0 = pl.multiple_of(j * BLK, BLK)
            keys = pl.ds(k0, BLK)
            bias_s[...] = score_bias(lo[rows, :], hi[rows, :], k0)
            forward(q_s, rows, BLK, km, vm, keys, BLK, w_s, s_s, j, bias_s, a_acc)
            return c

        def bwd(j, c):
            keys = pl.ds(pl.multiple_of(j * BLK, BLK), BLK)
            backward(
                BLK, km, vm, keys, BLK, w_s, s_s, j, da_s, da_t, q_t, dq_acc, dk_t, dv_t
            )
            return c

        lax.fori_loop(first, i + 1, fwd, 0)
        out, mixed, d_gate, d_att = middle(
            a_acc[...], x_s[rows, :].astype(F32), gate_s[rows, :].astype(F32), g_hist[rows, :], w_out[...]
        )
        out_hist[rows, :] = out
        mixed_t[:, rows] = mixed.T.astype(BF16)
        d_gq[rows, first_cols] = (d_gate * d_gq[rows, first_cols].astype(F32)).astype(BF16)
        da_s[...] = d_att.astype(BF16)
        da_t[...] = d_att.T.astype(BF16)
        q_t[...] = q_s[rows, :].astype(F32).T.astype(BF16)
        lax.fori_loop(first, i + 1, bwd, 0)
        d_q = dq_acc[...] * 0.125 * d_gq[rows, last_cols].astype(F32)
        d_gq[rows, last_cols] = d_q.astype(BF16)
        return carry

    lax.fori_loop(0, blocks, hist_block, 0)


def tgt_kernel(
    core_ref,
    cand,
    tid_col,
    tid_row,
    lo,
    hi,
    w_proj,
    w_out,
    g_tgt,
    km,
    vm,
    dk_in,
    dv_in,
    d_gq,
    sl_vk,
    normed_t,
    mixed_t,
    g_hist,
    out_tgt,
    d_tgt,
    d_vk,
    keep,
    give,
    gate_s,
    q_s,
    km_own,
    vm_own,
    d_pre,
    w_s,
    s_s,
    bias_s,
    a_acc,
    dq_acc,
    da_s,
    da_t,
    q_t,
    dk_t,
    dv_t,
    dk_own,
    dv_own,
    tgt_t,
):
    tgt_rows, feature = out_tgt.shape
    hist_rows = g_hist.shape[0]
    blocks = hist_rows // BLK
    every = slice(0, tgt_rows)
    part_cols = [slice(part * feature, (part + 1) * feature) for part in range(4)]
    col = lax.broadcasted_iota(jnp.int32, (1, cand.shape[0]), 1)
    x = mm(one_hot(tid_col[...] == col), cand[...])
    centred, rstd = moments(x)
    unit = centred * rstd
    normed = unit.astype(BF16)
    tgt_t[0] = unit.T.astype(BF16)
    for part in range(4):
        half = mm(normed, w_proj[:, part_cols[part]]) * 0.5
        act, slope = silu_parts(half)
        d_pre[:, part_cols[part]] = slope.astype(BF16)
        if part == 0:
            gate_s[...] = act.astype(BF16)
        elif part == 1:
            split_heads(act, vm_own, every)
        elif part == 2:
            q_s[...] = (act.astype(BF16) * 0.0625).astype(BF16)
        else:
            split_heads(act, km_own, every)

    a_acc[...] = jnp.zeros_like(a_acc)
    dq_acc[...] = jnp.zeros_like(dq_acc)
    dk_own[...] = jnp.zeros_like(dk_own)
    dv_own[...] = jnp.zeros_like(dv_own)
    dk_t[...] = dk_in[...]
    dv_t[...] = dv_in[...]

    def fwd(j, c):
        k0 = pl.multiple_of(j * BLK, BLK)
        keys = pl.ds(k0, BLK)
        bias_s[...] = score_bias(lo[...], hi[...], k0)
        forward(q_s, every, tgt_rows, km, vm, keys, BLK, w_s, s_s, j, bias_s, a_acc)
        return c

    def bwd(j, c):
        keys = pl.ds(pl.multiple_of(j * BLK, BLK), BLK)
        backward(
            tgt_rows, km, vm, keys, BLK, w_s, s_s, j, da_s, da_t, q_t, dq_acc, dk_t, dv_t
        )
        return c

    lax.fori_loop(0, blocks, fwd, 0)
    same = lax.broadcasted_iota(jnp.int32, (tgt_rows, tgt_rows), 0) == lax.broadcasted_iota(
        jnp.int32, (tgt_rows, tgt_rows), 1
    )
    bias_s[:, :tgt_rows] = jnp.where(same, 0.0, MASKED).astype(F32)
    forward(
        q_s, every, tgt_rows, km_own, vm_own, every, tgt_rows, w_s, s_s, blocks, bias_s, a_acc
    )
    out, mixed, d_gate, d_att = middle(
        a_acc[...], x, gate_s[...].astype(F32), g_tgt[...], w_out[...]
    )
    out_tgt[...] = out
    tgt_t[1] = mixed.T.astype(BF16)
    d_pre[:, part_cols[0]] = (d_gate * d_pre[:, part_cols[0]].astype(F32)).astype(BF16)
    da_s[...] = d_att.astype(BF16)
    da_t[...] = d_att.T.astype(BF16)
    q_t[...] = q_s[...].astype(F32).T.astype(BF16)
    lax.fori_loop(0, blocks, bwd, 0)
    backward(
        tgt_rows, km_own, vm_own, every, tgt_rows, w_s, s_s, blocks,
        da_s, da_t, q_t, dq_acc, dk_own, dv_own,
    )
    grads = (None, dv_own[...].T, dq_acc[...] * 0.125, dk_own[...].T * 2.0)
    for part in (1, 2, 3):
        d_part = grads[part] * d_pre[:, part_cols[part]].astype(F32)
        d_pre[:, part_cols[part]] = d_part.astype(BF16)

    d_normed = mm(d_pre[...], w_proj[...], NT)
    mean_d = jnp.mean(d_normed, axis=-1, keepdims=True)
    mean_dn = jnp.mean(d_normed * unit, axis=-1, keepdims=True)
    d_x = rstd * (d_normed - mean_d - unit * mean_dn) + g_tgt[...].astype(F32)
    d_tgt[every, :] = d_x.astype(BF16)
    ids = tid_row[...]
    high = lax.shift_right_logical(ids, 6)
    low = ids - high * 64
    d_tgt[tgt_rows:, :] = jnp.zeros((d_tgt.shape[0] - tgt_rows, feature), BF16)
    wide = (d_tgt.shape[0] - tgt_rows, tgt_rows)
    d_tgt[tgt_rows:, :tgt_rows] = jnp.broadcast_to(high.astype(F32), wide).astype(BF16)
    d_tgt[tgt_rows:, tgt_rows : 2 * tgt_rows] = jnp.broadcast_to(low.astype(F32), wide).astype(BF16)

    def spread(i, carry):
        rows = pl.ds(pl.multiple_of(i * BLK, BLK), BLK)
        vals, keys = slice(0, feature), slice(feature, 2 * feature)
        d_vk[rows, vals] = (dv_t[:, rows].T * sl_vk[rows, vals].astype(F32)).astype(BF16)
        d_vk[rows, keys] = (dk_t[:, rows].T * 2.0 * sl_vk[rows, keys].astype(F32)).astype(BF16)
        return carry

    lax.fori_loop(0, blocks, spread, 0)

    core = core_ref[0]
    half_rows = feature // 2
    for dest, half in ((give, 1 - core), (keep, core)):
        rows = pl.ds(pl.multiple_of(half * half_rows, half_rows), half_rows)
        for part in range(5):
            if part < 4:
                source = (d_gq, d_vk)[part % 2]
                cols = slice((part // 2) * feature, (part // 2 + 1) * feature)
                total = mm(normed_t[rows, :], source[:, cols])
                total = total + mm(tgt_t[0, rows, :], d_pre[:, part_cols[part]])
            else:
                total = mm(mixed_t[rows, :], g_hist[...]) + mm(tgt_t[1, rows, :], g_tgt[...])
            for group, dest_cols, cols in segments(part, feature):
                piece = total[:, cols].reshape(16, 16, cols.stop - cols.start)
                dest[:, group, :, dest_cols] = piece.astype(BF16)


def segments(part, feature):
    found, begin = [], part * feature
    while begin < (part + 1) * feature:
        group = begin // 640
        end = min((part + 1) * feature, (group + 1) * 640)
        found.append(
            (group, slice(begin - group * 640, end - group * 640), slice(begin - part * feature, end - part * feature))
        )
        begin = end
    return found


def rows_kernel(d_gq, d_vk, w_proj, normed, rstd, g_hist, pos_col, slot_grads, d_hist):
    hist_rows, feature = g_hist.shape

    def back(i, carry):
        rows = pl.ds(pl.multiple_of(i * BLK, BLK), BLK)
        d_normed = jnp.zeros((BLK, feature), F32)
        for part in range(4):
            cols = slice((part // 2) * feature, (part // 2 + 1) * feature)
            source = (d_gq, d_vk)[part % 2]
            weights = w_proj[:, part * feature : (part + 1) * feature]
            d_normed = d_normed + mm(source[rows, cols], weights, NT)
        unit = normed[rows, :].astype(F32)
        mean_d = jnp.mean(d_normed, axis=-1, keepdims=True)
        mean_dn = jnp.mean(d_normed * unit, axis=-1, keepdims=True)
        d_x = rstd[rows, :] * (d_normed - mean_d - unit * mean_dn)
        d_hist[rows, :] = (d_x + g_hist[rows, :].astype(F32)).astype(BF16)
        return carry

    lax.fori_loop(0, hist_rows // BLK, back, 0)

    def pick(i, carry):
        rows = pl.ds(pl.multiple_of(i * BLK, BLK), BLK)
        row = lax.broadcasted_iota(jnp.int32, (1, hist_rows), 1)
        onehot = one_hot(pos_col[rows, :] == row)
        slot_grads[rows, :] = mm(onehot, d_hist[...]).astype(BF16)
        return carry

    lax.fori_loop(0, slot_grads.shape[0] // BLK, pick, 0)


def cand_kernel(first_ref, rows, out):
    count, feature = out.shape
    own = first_ref[0] + lax.broadcasted_iota(jnp.int32, (count, 1), 0)
    total = jnp.zeros((count, feature), F32)
    for peer in range(rows.shape[0]):
        high = rows[peer, count : count + 16, :count].astype(F32)[:1]
        low = rows[peer, count : count + 16, count : 2 * count].astype(F32)[:1]
        ids = (high * 64.0 + low).astype(jnp.int32)
        total = total + mm(one_hot(own == ids), rows[peer, :count, :])
    out[...] = total


def sums_kernel(core_ref, own, other, d_proj, d_out):
    half_rows, feature = d_proj.shape[0] // 2, d_out.shape[1]
    for source, half in ((own, core_ref[0]), (other, 1 - core_ref[0])):
        rows = pl.ds(pl.multiple_of(half * half_rows, half_rows), half_rows)
        for part in range(5):
            for group, source_cols, cols in segments(part, feature):
                piece = source[:, group, :, source_cols].astype(F32)
                piece = piece.reshape(half_rows, cols.stop - cols.start)
                if part < 4:
                    d_proj[rows, part * feature + cols.start : part * feature + cols.stop] = piece
                else:
                    d_out[rows, cols] = piece


VMEM = pl.BlockSpec(memory_space=pltpu.VMEM)
SMEM = pl.BlockSpec(memory_space=pltpu.SMEM)


def params(mib):
    return pltpu.CompilerParams(vmem_limit_bytes=mib << 20)


def cost(flops, nbytes):
    return pl.CostEstimate(flops=flops, bytes_accessed=nbytes, transcendentals=0)


def local(
    send_rows, slot_pos, lengths, candidates, target_ids, w_proj, w_out, g_hist, g_tgt
):
    peers, capacity, feature = send_rows.shape[1:]
    slots = peers * capacity
    hist_rows, tgt_rows = g_hist.shape[0], g_tgt.shape[0]
    blocks = hist_rows // BLK
    each = target_ids.shape[1]
    table = lax.all_gather(candidates, "mem", axis=0, tiled=True)
    arrived = lax.all_to_all(send_rows, BOTH, split_axis=1, concat_axis=0, tiled=True)
    arrived = arrived.reshape(slots, feature)

    pos_row = slot_pos.reshape(1, slots)
    pos_col = slot_pos.reshape(slots, 1)
    ends = jnp.cumsum(lengths[0])
    starts = ends - lengths[0]
    row = jnp.arange(hist_rows, dtype=jnp.int32)[:, None]
    hist_lo = jnp.max(jnp.where(row >= starts[None, :], starts[None, :], 0), axis=1)
    first = (hist_lo[::BLK] // BLK).astype(jnp.int32)
    tgt_lo = jnp.repeat(starts, each).astype(jnp.int32)[:, None]
    tgt_hi = jnp.repeat(ends - 1, each).astype(jnp.int32)[:, None]
    core = lax.rem(lax.axis_index("grp"), 2).astype(jnp.int32)[None]

    sds = jax.ShapeDtypeStruct
    heads_shape = (HEADS, hist_rows, 128)
    out_hist, normed, rstd, normed_t, mixed_t, km, vm, dk_t, dv_t, d_gq, sl_vk = pl.pallas_call(
        hist_kernel,
        out_shape=(
            sds((hist_rows, feature), BF16),
            sds((hist_rows, feature), BF16),
            sds((hist_rows, 1), F32),
            sds((feature, hist_rows), BF16),
            sds((feature, hist_rows), BF16),
            sds(heads_shape, BF16),
            sds(heads_shape, BF16),
            sds((feature, hist_rows), F32),
            sds((feature, hist_rows), F32),
            sds((hist_rows, 2 * feature), BF16),
            sds((hist_rows, 2 * feature), BF16),
        ),
        in_specs=[SMEM] + [VMEM] * 7,
        out_specs=(VMEM,) * 11,
        scratch_shapes=[
            pltpu.VMEM((hist_rows, feature), BF16),
            pltpu.VMEM((hist_rows, feature), BF16),
            pltpu.VMEM((hist_rows, feature), BF16),
            pltpu.VMEM((blocks, HEADS, BLK, BLK), BF16),
            pltpu.VMEM((blocks, HEADS, BLK, BLK), BF16),
            pltpu.VMEM((BLK, BLK), F32),
            pltpu.VMEM((BLK, feature), F32),
            pltpu.VMEM((BLK, feature), F32),
            pltpu.VMEM((BLK, feature), BF16),
            pltpu.VMEM((feature, BLK), BF16),
            pltpu.VMEM((feature, BLK), BF16),
        ],
        compiler_params=params(HIST_MIB),
        cost_estimate=cost(16 << 30, 24 << 20),
        name="hist",
    )(first, arrived, pos_row, hist_lo.astype(jnp.int32)[:, None], row, w_proj, w_out, g_hist)

    pieces = (16, 4, 16, 640)
    out_tgt, d_tgt, d_vk, keep, give = pl.pallas_call(
        tgt_kernel,
        out_shape=(
            sds((tgt_rows, feature), BF16),
            sds((tgt_rows + 16, feature), BF16),
            sds((hist_rows, 2 * feature), BF16),
            sds(pieces, BF16),
            sds(pieces, BF16),
        ),
        in_specs=[SMEM] + [VMEM] * 17,
        out_specs=(VMEM,) * 5,
        scratch_shapes=[
            pltpu.VMEM((tgt_rows, feature), BF16),
            pltpu.VMEM((tgt_rows, feature), BF16),
            pltpu.VMEM((HEADS, tgt_rows, 128), BF16),
            pltpu.VMEM((HEADS, tgt_rows, 128), BF16),
            pltpu.VMEM((tgt_rows, 4 * feature), BF16),
            pltpu.VMEM((blocks + 1, HEADS, tgt_rows, BLK), BF16),
            pltpu.VMEM((blocks + 1, HEADS, tgt_rows, BLK), BF16),
            pltpu.VMEM((tgt_rows, BLK), F32),
            pltpu.VMEM((tgt_rows, feature), F32),
            pltpu.VMEM((tgt_rows, feature), F32),
            pltpu.VMEM((tgt_rows, feature), BF16),
            pltpu.VMEM((feature, tgt_rows), BF16),
            pltpu.VMEM((feature, tgt_rows), BF16),
            pltpu.VMEM((feature, hist_rows), F32),
            pltpu.VMEM((feature, hist_rows), F32),
            pltpu.VMEM((feature, tgt_rows), F32),
            pltpu.VMEM((feature, tgt_rows), F32),
            pltpu.VMEM((2, feature, tgt_rows), BF16),
        ],
        compiler_params=params(TGT_MIB),
        cost_estimate=cost(6 << 30, 28 << 20),
        name="tgt",
    )(
        core,
        table,
        target_ids.reshape(tgt_rows, 1),
        target_ids.reshape(1, tgt_rows),
        tgt_lo,
        tgt_hi,
        w_proj,
        w_out,
        g_tgt,
        km,
        vm,
        dk_t,
        dv_t,
        d_gq,
        sl_vk,
        normed_t,
        mixed_t,
        g_hist,
    )

    swap = core_swap()
    swapped = lax.ppermute(give, BOTH, swap)
    chip_sum = (keep.astype(F32) + swapped.astype(F32)).astype(BF16)
    chip_sum = chip_sum.reshape(64, 1, 16, 640)
    scattered = lax.all_to_all(
        chip_sum, BOTH, split_axis=0, concat_axis=1, tiled=True, axis_index_groups=same_core()
    )
    slot_grads = pl.pallas_call(
        rows_kernel,
        out_shape=sds((slots, feature), BF16),
        in_specs=[VMEM] * 7,
        out_specs=VMEM,
        scratch_shapes=[pltpu.VMEM((hist_rows, feature), BF16)],
        compiler_params=params(ROWS_MIB),
        cost_estimate=cost(5 << 30, 16 << 20),
        name="rows",
    )(d_gq, d_vk, w_proj, normed, rstd, g_hist, pos_col)
    total = jnp.sum(scattered.reshape(64, 16, 640).astype(F32), axis=0).astype(BF16)

    returned = lax.all_to_all(
        slot_grads.reshape(peers, 1, capacity, feature),
        BOTH,
        split_axis=0,
        concat_axis=1,
        tiled=True,
    )
    own = lax.all_to_all(
        jnp.broadcast_to(total[None, None], (64, 1, 16, 640)),
        BOTH,
        split_axis=0,
        concat_axis=1,
        tiled=True,
        axis_index_groups=same_core(),
    ).reshape(pieces)
    other = lax.ppermute(own, BOTH, swap)
    sum_proj, sum_out = pl.pallas_call(
        sums_kernel,
        out_shape=(sds(w_proj.shape, F32), sds(w_out.shape, F32)),
        in_specs=[SMEM, VMEM, VMEM],
        out_specs=(VMEM, VMEM),
        compiler_params=params(16),
        name="sums",
    )(core, own, other)

    tgt_grads = lax.all_gather(d_tgt, "mem", axis=0, tiled=False)
    mine = (lax.axis_index("mem") * candidates.shape[0]).astype(jnp.int32)[None]
    d_cand = pl.pallas_call(
        cand_kernel,
        out_shape=sds(candidates.shape, F32),
        in_specs=[SMEM, VMEM],
        out_specs=VMEM,
        compiler_params=params(16),
        name="cand",
    )(mine, tgt_grads)
    return (out_hist, out_tgt, returned, d_cand, sum_proj, sum_out)


HIST_MIB, TGT_MIB, ROWS_MIB = 44, 44, 24


def core_swap():
    return [(i, i + 16 if (i // 16) % 2 == 0 else i - 16) for i in range(128)]


def same_core():
    return [[i for i in range(128) if (i // 16) % 2 == core] for core in (0, 1)]


def solution(mesh):
    placed = (
        P(BOTH, None, None, None),
        P(BOTH, None, None),
        P(BOTH, None),
        P(BOTH, None),
        P(BOTH, None),
        P(),
        P(),
        P(BOTH, None),
        P(BOTH, None),
    )
    return jax.shard_map(
        local,
        mesh=mesh,
        in_specs=placed,
        out_specs=(
            P(BOTH, None),
            P(BOTH, None),
            P(BOTH, None, None, None),
            P(BOTH, None),
            P(),
            P(),
        ),
        check_vma=False,
    )
```

time: 314 us -> 248 us (0.79)
  blocking collectives: 110 us -> 0 us
  waiting for transfers between devices: 42.7 us -> 87.2 us
  starting transfers between devices: 22.1 us -> 43.1 us
  local copies, waits for them, and re-layouts: 41.2 us -> 22.1 us
    all_gather x2 -> x0, blocking collectives: 57.5 us -> none  [the longest x1 37.9 us: local(): lax.all_gather(target_ids.reshape(1, tgt_rows), 'mem', axis=1, tiled=True)]
    all_to_all x1 -> x0, blocking collectives: 52.1 us -> none  [reduce_weights(): both = lax.all_to_all(both, BOTH, split_axis=0, concat_axis=0, tiled=True)]
    all_to_all x1, waiting for transfers between devices: 0.01 us -> 28.2 us  [local(): lax.all_to_all(slot_grads.reshape(peers, 1, capacity, feature), BOTH, spl...]
    all_to_all x0 -> x2, waiting for transfers between devices: none -> 24.9 us  [the longest x1 19.7 us: local(): lax.all_to_all(chip_sum, BOTH, split_axis=0, concat_axis=1, tiled=True, a...]
    all_gather x1, waiting for transfers between devices: 15.9 us -> 0.01 us  [local(): table = lax.all_gather(candidates, 'mem', axis=0, tiled=True)]
    reshape x5 -> x0, local copies, waits for them, and re-layouts: 11.9 us -> none  [the longest x1 5.61 us: reduce_weights(): return (gathered[:2048].reshape(512, 2048), gathered[2048:])]
    all_to_all x0 -> x2, starting transfers between devices: none -> 10 us  [the longest x1 5.36 us: local(): lax.all_to_all(jnp.broadcast_to(total[None, None], (64, 1, 16, 640)), BOT...]
    ppermute x0 -> x2, starting transfers between devices: none -> 8.7 us  [the longest x1 7.48 us: local(): swapped = lax.ppermute(give, BOTH, swap)]
  transfers between devices with their start and end apart: 5 -> 8, of which waited for: 2 -> 5; matrix products, arithmetic and copies ran while one was open for 5% -> 1% of each run, Pallas kernels for 2% -> 20%
where the time goes in v2:
time: 248 us
  waiting for transfers between devices  87.2 us (35%)
  Pallas kernels  78.8 us (32%)
  starting transfers between devices  43.1 us (17%)
  local copies, waits for them, and re-layouts  22.1 us (9%)
  between operations  14.3 us (6%)
    pallas_call x1, Pallas kernels, local(): pl.pallas_call(hist_kernel, out_shape=(sds((hist_rows, feature), BF16), s...  38.5 us
    all_to_all x1, waiting for transfers between devices, local(): lax.all_to_all(send_rows, BOTH, split_axis=1, concat_axis=0, tiled=True)  30.2 us
    all_to_all x1, waiting for transfers between devices, local(): lax.all_to_all(slot_grads.reshape(peers, 1, capacity, feature), BOTH, spl...  28.2 us
    pallas_call x1, Pallas kernels, local(): pl.pallas_call(tgt_kernel, out_shape=(sds((tgt_rows, feature), BF16), sds...  27.2 us
    all_to_all x1, waiting for transfers between devices, local(): lax.all_to_all(chip_sum, BOTH, split_axis=0, concat_axis=1, tiled=True, a...  19.7 us
    unnamed x42, local copies, waits for them, and re-layouts  19.5 us
    all_to_all x1, starting transfers between devices, local(): lax.all_to_all(slot_grads.reshape(peers, 1, capacity, feature), BOTH, spl...  12.4 us
    all_to_all x1, starting transfers between devices, local(): lax.all_to_all(send_rows, BOTH, split_axis=1, concat_axis=0, tiled=True)  12 us
  transfers between devices with their start and end apart: 8, of which 5 were waited for; matrix products, arithmetic and copies ran while one was open for 1% of the time, Pallas kernels for 20%

profile of v2, /device:TPU:1, one launch (start us, length us, event | category | flops | bytes accessed | tf_op | source)
XLA Modules:
  0.0 247.5 jit_solution(14170496987281398191)
XLA Ops:
  8.0 12.0 %all-to-all-start = ((bf16[1,128,16,512]{3,2,0,1:T(8,128)(2,1)}), bf16[1,128,16,512]{3,2,0,1:T(8,128)(2,1)}, u32[]{:S(2)}, u32[]{:S(2)}) async-start(bf16[1,128,16,512]{3,2,0,1:T(8,128)(2,1)} %bitcast.30), calls=%async_computation | async-start | bytes 4194304 | tf_op jit(solution)/shard_map/all_to_all | solution.py:452
  21.3 30.2 %all-to-all-done = bf16[1,128,16,512]{3,2,0,1:T(8,128)(2,1)} async-done(((bf16[1,128,16,512]{3,2,0,1:T(8,128)(2,1)}), bf16[1,128,16,512]{3,2,0,1:T(8,128)(2,1)}, u32[]{:S(2)}, u32[]{:S(2)}) %all-to-all-start) | async-done | bytes 2097184 | tf_op jit(solution)/shard_map/all_to_all | solution.py:452
  51.5 38.5 %hist.1 = (bf16[1024,512]{1,0:T(8,128)(2,1)}, bf16[1024,512]{1,0:T(8,128)(2,1)S(1)}, f32[1024,1]{1,0:T(8,128)S(1)}, bf16[512,1024]{1,0:T(8,128)(2,1)S(1)}, bf16[...) custom-call(s32[4]{0:T(128)S(1)} %and_select_fusion.first_ref, ...), custom_call_target="tpu_custom_call" | custom-call | flops 17179869184 | bytes 25165824 | tf_op jit(solution)/shard_map/hist/pallas_call | solution.py:468
  90.0 1.3 copy-done.8
  91.3 1.0 copy-done.9
  92.2 1.0 copy-done.11
  93.3 1.0 copy-done.13
  94.3 0.8 copy-done.15
  95.1 1.2 copy-done.10
  96.3 1.2 copy-done.12
  97.6 27.2 %tgt.1 = (bf16[128,512]{1,0:T(8,128)(2,1)}, bf16[144,512]{1,0:T(8,128)(2,1)}, bf16[1024,1024]{1,0:T(8,128)(2,1)S(1)}, bf16[16,4,16,640]{3,2,1,0:T(8,128)(2,1)S(1)}, bf16[16,4,16,640]{3,2,1,0:T(8,128)(2,1)S(1)}) custom-call(s32[1]{0:T(128)} %bitcast.6.core_ref, bf16[2048,512]{1,0:T(8,128)(2,1)} %all-gather.4.cloned.1.call-done.cand, ...), custom_call_target="tpu_custom_call" | custom-call | flops 6442450944 | bytes 29360128 | tf_op jit(solution)/shard_map/tgt/pallas_call | solution.py:504
  124.7 7.5 %collective-permute-start = (bf16[16,4,16,640]{3,2,1,0:T(8,128)(2,1)S(1)}, bf16[16,4,16,640]{3,2,1,0:T(8,128)(2,1)S(1)}, u32[]{:S(2)}, u32[]{:S(2)}) collective-permute-start(bf16[16,4,16,640]{3,2,1,0:T(8,128)(2,1)S(1)} %get-tuple-element.39), channel_id=1, source_target_pairs={{0,16},{1,17},{2,18},{3,19},{4,20},{5,21},{6,22},{7,23},{8,24},{9,... | collective-permute-start | bytes 3932168 | tf_op jit(solution)/shard_map/ppermute | solution.py:560
  132.2 2.7 %collective-permute-done = bf16[16,4,16,640]{3,2,1,0:T(8,128)(2,1)S(1)} collective-permute-done((bf16[16,4,16,640]{3,2,1,0:T(8,128)(2,1)S(1)}, bf16[16,4,16,640]{3,2,1,0:T(8,128)(2,1)S(1)}, u32[]{:S(2)}, u32[]{:S(2)}) %collective-permute-start) | collective-permute-done | bytes 1310752 | tf_op jit(solution)/shard_map/ppermute | solution.py:560
  134.9 1.5 add_convert_fusion
  136.3 4.7 %all-to-all-start.2 = ((bf16[64,1,16,640]{3,2,1,0:T(8,128)(2,1)}), bf16[64,1,16,640]{3,2,1,0:T(8,128)(2,1)S(1)}, u32[]{:S(2)}, u32[]{:S(2)}) async-start(bf16[64,1,16,640]{3,2,1,0:T(8,128)(2,1)} %bitcast.29), calls=%async_computation.2 | async-start | bytes 2621440 | tf_op jit(solution)/shard_map/all_to_all | solution.py:563
  141.8 19.7 %all-to-all-done.2 = bf16[64,1,16,640]{3,2,1,0:T(8,128)(2,1)S(1)} async-done(((bf16[64,1,16,640]{3,2,1,0:T(8,128)(2,1)}), bf16[64,1,16,640]{3,2,1,0:T(8,128)(2,1)S(1)}, u32[]{:S(2)}, u32[]{:S(2)}) %all-to-all-start.2) | async-done | bytes 1310752 | tf_op jit(solution)/shard_map/all_to_all | solution.py:563
  161.7 1.2 broadcast_in_dim.40
  162.9 5.4 %all-to-all-start.3 = ((bf16[64,1,16,640]{3,2,1,0:T(8,128)(2,1)}), bf16[64,1,16,640]{3,2,1,0:T(8,128)(2,1)S(1)}, u32[]{:S(2)}, u32[]{:S(2)}) async-start(bf16[64,1,16,640]{3,2,1,0:T(8,128)(2,1)} %broadcast_in_dim.40), calls=%async_computation.3 | async-start | bytes 2621440 | tf_op jit(solution)/shard_map/all_to_all | solution.py:585
  168.8 1.6 copy-done.1
  170.4 1.6 copy-done.5
  172.0 1.6 copy-done.7
  173.6 1.2 copy-done.14
  174.8 1.0 copy-done.16
  175.9 9.1 %rows.1 = bf16[2048,512]{1,0:T(8,128)(2,1)} custom-call(bf16[1024,1024]{1,0:T(8,128)(2,1)S(1)} %copy-done.5, bf16[1024,1024]{1,0:T(8,128)(2,1)S(1)} %copy-done.7, bf16[512,2048]{1,0:T(8,128)(2,1)S(1)} %copy-done.1, bf16[1024,512]{1,0:T(8,128)(2,1)S(1)} %copy-done.14, f32[1024,1]{1,0:T(8,128)S(1)} %copy-done.16, bf16[1024,512]{1,0:T(8,128)(2,1)S(1)} %copy-done.2, ...), custom_call_target="tpu_custom_call" | custom-call | flops 5368709120 | bytes 16777216 | tf_op jit(solution)/shard_map/rows/pallas_call | solution.py:566
  185.0 5.1 %all-to-all-done.3 = bf16[64,1,16,640]{3,2,1,0:T(8,128)(2,1)S(1)} async-done(((bf16[64,1,16,640]{3,2,1,0:T(8,128)(2,1)}), bf16[64,1,16,640]{3,2,1,0:T(8,128)(2,1)S(1)}, u32[]{:S(2)}, u32[]{:S(2)}) %all-to-all-start.3) | async-done | bytes 1310752 | tf_op jit(solution)/shard_map/all_to_all | solution.py:585
  190.1 12.4 %all-to-all-start.1 = ((bf16[128,1,16,512]{3,2,1,0:T(8,128)(2,1)}), bf16[128,1,16,512]{3,2,1,0:T(8,128)(2,1)}, u32[]{:S(2)}, u32[]{:S(2)}) async-start(bf16[128,1,16,512]{3,2,1,0:T(8,128)(2,1)} %bitcast.10), calls=%async_computation.1 | async-start | bytes 4194304 | tf_op jit(solution)/shard_map/all_to_all | solution.py:578
  202.5 1.2 collective-permute-start.1
  203.7 28.2 %all-to-all-done.1 = bf16[128,1,16,512]{3,2,1,0:T(8,128)(2,1)} async-done(((bf16[128,1,16,512]{3,2,1,0:T(8,128)(2,1)}), bf16[128,1,16,512]{3,2,1,0:T(8,128)(2,1)}, u32[]{:S(2)}, u32[]{:S(2)}) %all-to-all-start.1) | async-done | bytes 2097184 | tf_op jit(solution)/shard_map/all_to_all | solution.py:578
  231.9 1.7 copy-done
  233.5 1.4 cand.1
  234.9 2.7 %sums.1 = (f32[512,2048]{1,0:T(8,128)}, f32[512,512]{1,0:T(8,128)}) custom-call(s32[1]{0:T(128)} %bitcast.6.core_ref, bf16[16,4,16,640]{3,2,1,0:T(8,128)(2,1)S(1)} %bitcast.27, bf16[16,4,16,640]{3,2,1,0:T(8,128)(2,1)S(1)} %collective-permute-done.1.other), custom_call_target="tpu_custom_call" | custom-call | tf_op jit(solution)/shard_map/sums/pallas_call | solution.py:594
  237.6 3.1 %copy.48 = bf16[1,128,16,512]{3,2,1,0:T(8,128)(2,1)} copy(bf16[1,128,16,512]{3,2,1,0:T(8,128)(2,1)} %bitcast.11) | data formatting | bytes 4194304
  (52 shorter events, 3.6 us)
Async XLA Ops:
  7.2 87.9 %all-gather.4.cloned.1.call-start = ((), (), s32[]{:S(2)}) async-start(), calls=%async_computation.4 | async-start | bytes 2228224 | tf_op jit(solution)/shard_map/all_gather | solution.py:451
  7.9 12.0 %copy-start.17 = (s32[8,16]{1,0:T(8,128)S(1)}, s32[8,16]{1,0:T(8,128)}, u32[]{:S(2)}) copy-start(s32[8,16]{1,0:T(8,128)} %param.13) | copy-start | bytes 1540
  7.9 12.2 %copy-start.19 = (s32[1,8]{1,0:T(1,128)S(1)}, s32[1,8]{1,0:T(1,128)}, u32[]{:S(2)}) copy-start(s32[1,8]{1,0:T(1,128)} %param.11) | copy-start | bytes 100
  7.9 12.8 %copy-start.18 = (s32[1,128,16]{1,2,0:T(8,128)S(1)}, s32[1,128,16]{1,2,0:T(8,128)}, u32[]{:S(2)}) copy-start(s32[1,128,16]{1,2,0:T(8,128)} %param.10) | copy-start | bytes 24580
  7.9 43.5 %copy-start.2 = (bf16[1024,512]{1,0:T(8,128)(2,1)S(1)}, bf16[1024,512]{1,0:T(8,128)(2,1)}, u32[]{:S(2)}) copy-start(bf16[1024,512]{1,0:T(8,128)(2,1)} %g_hist.5) | copy-start | bytes 3145732
  7.9 43.5 %copy-start.3 = (bf16[512,512]{1,0:T(8,128)(2,1)S(1)}, bf16[512,512]{1,0:T(8,128)(2,1)}, u32[]{:S(2)}) copy-start(bf16[512,512]{1,0:T(8,128)(2,1)} %w_out.3) | copy-start | bytes 1572868
  8.0 43.5 %all-to-all-start = ((bf16[1,128,16,512]{3,2,0,1:T(8,128)(2,1)}), bf16[1,128,16,512]{3,2,0,1:T(8,128)(2,1)}, u32[]{:S(2)}, u32[]{:S(2)}) async-start(bf16[1,128,16,512]{3,2,0,1:T(8,128)(2,1)} %bitcast.30), calls=%async_computation | async-start | bytes 4194304 | tf_op jit(solution)/shard_map/all_to_all | solution.py:452
  51.5 43.6 %copy-start.4 = (bf16[128,512]{1,0:T(8,128)(2,1)S(1)}, bf16[128,512]{1,0:T(8,128)(2,1)}, u32[]{:S(2)}) copy-start(bf16[128,512]{1,0:T(8,128)(2,1)} %g_tgt.1) | copy-start | bytes 393220
  90.0 1.3 copy-start.8
  91.3 1.0 copy-start.9
  92.2 1.0 copy-start.11
  93.3 1.0 copy-start.13
  94.3 0.8 copy-start.15
  95.1 1.2 copy-start.10
  96.3 1.2 copy-start.12
  124.7 11.6 %copy-start.6 = (bf16[1024,1024]{1,0:T(8,128)(2,1)}, bf16[1024,1024]{1,0:T(8,128)(2,1)S(1)}, u32[]{:S(2)}) copy-start(bf16[1024,1024]{1,0:T(8,128)(2,1)S(1)} %get-tuple-element.34.d_vk) | copy-start | bytes 6291460
  124.7 10.1 %collective-permute-start = (bf16[16,4,16,640]{3,2,1,0:T(8,128)(2,1)S(1)}, bf16[16,4,16,640]{3,2,1,0:T(8,128)(2,1)S(1)}, u32[]{:S(2)}, u32[]{:S(2)}) collective-permute-start(bf16[16,4,16,640]{3,2,1,0:T(8,128)(2,1)S(1)} %get-tuple-element.39), channel_id=1, source_target_pairs={{0,16},{1,17},{2,18},{3,19},{4,20},{5,21},{6,22},{7,23},{8,24},{9,... | collective-permute-start | bytes 3932168 | tf_op jit(solution)/shard_map/ppermute | solution.py:560
  136.3 25.2 %all-to-all-start.2 = ((bf16[64,1,16,640]{3,2,1,0:T(8,128)(2,1)}), bf16[64,1,16,640]{3,2,1,0:T(8,128)(2,1)S(1)}, u32[]{:S(2)}, u32[]{:S(2)}) async-start(bf16[64,1,16,640]{3,2,1,0:T(8,128)(2,1)} %bitcast.29), calls=%async_computation.2 | async-start | bytes 2621440 | tf_op jit(solution)/shard_map/all_to_all | solution.py:563
  141.0 90.9 %all-gather.6.cloned.1.call-start = ((), (), s32[]{:S(2)}) async-start(), calls=%async_computation.5 | async-start | bytes 2506752 | tf_op jit(solution)/shard_map/all_gather | solution.py:603
  162.9 27.2 %all-to-all-start.3 = ((bf16[64,1,16,640]{3,2,1,0:T(8,128)(2,1)}), bf16[64,1,16,640]{3,2,1,0:T(8,128)(2,1)S(1)}, u32[]{:S(2)}, u32[]{:S(2)}) async-start(bf16[64,1,16,640]{3,2,1,0:T(8,128)(2,1)} %broadcast_in_dim.40), calls=%async_computation.3 | async-start | bytes 2621440 | tf_op jit(solution)/shard_map/all_to_all | solution.py:585
  168.8 1.6 copy-start.1
  170.4 1.6 copy-start.5
  172.0 1.6 copy-start.7
  173.6 1.2 copy-start.14
  174.8 1.0 copy-start.16
  190.1 41.8 %all-to-all-start.1 = ((bf16[128,1,16,512]{3,2,1,0:T(8,128)(2,1)}), bf16[128,1,16,512]{3,2,1,0:T(8,128)(2,1)}, u32[]{:S(2)}, u32[]{:S(2)}) async-start(bf16[128,1,16,512]{3,2,1,0:T(8,128)(2,1)} %bitcast.10), calls=%async_computation.1 | async-start | bytes 4194304 | tf_op jit(solution)/shard_map/all_to_all | solution.py:578
  202.5 32.5 %collective-permute-start.1 = (bf16[16,4,16,640]{3,2,1,0:T(8,128)(2,1)S(1)}, bf16[16,4,16,640]{3,2,1,0:T(8,128)(2,1)S(1)}, u32[]{:S(2)}, u32[]{:S(2)}) collective-permute-start(bf16[16,4,16,640]{3,2,1,0:T(8,128)(2,1)S(1)} %bitcast.26), channel_id=1, source_target_pairs={{0,16},{1,17},{2,18},{3,19},{4,20},{5,21},{6,22},{7,23},{8,24},{9,... | collective-permute-start | bytes 3932168 | tf_op jit(solution)/shard_map/ppermute | solution.py:593
  231.9 1.7 copy-start
Sparse Core Ops, SparseCore 0:
  10.1 57.2 all-gather.3
  144.6 51.8 all-gather.5

commit v3 on v2

v3 whole, which is shorter than its diff:
```python
import jax
import jax.numpy as jnp
from jax import lax
from jax.experimental import pallas as pl
from jax.experimental.pallas import tpu as pltpu
from jax.sharding import PartitionSpec as P

HEADS = 8
EPS = 1e-05
BLK = 256
MASKED = -1e9
F32 = jnp.float32
BF16 = jnp.bfloat16
BOTH = ("grp", "mem")
NN = (((1,), (0,)), ((), ()))
NT = (((1,), (1,)), ((), ()))


def mm(left, right, dims=NN):
    return lax.dot_general(left, right, dims, preferred_element_type=F32)


def moments(values):
    centred = values - jnp.mean(values, axis=-1, keepdims=True)
    variance = jnp.mean(centred * centred, axis=-1, keepdims=True)
    return centred, lax.rsqrt(variance + EPS)


def head_masks():
    lane = lax.broadcasted_iota(jnp.int32, (1, 128), 1)
    low_half = jnp.where(lane < 64, 1.0, 0.0).astype(F32)
    return (low_half, 1.0 - low_half)


def silu_parts(half):
    t = jnp.tanh(half)
    u = 1.0 + t
    return half * u, 0.5 * u * (1.0 + half * (1.0 - t))


def one_hot(hits):
    return jnp.where(hits, 1.0, 0.0).astype(BF16)


def split_heads(act, dest, rows):
    halves = head_masks()
    for head in range(HEADS):
        pair = act[:, (head // 2) * 128 : (head // 2 + 1) * 128]
        dest[head, rows, :] = (pair * halves[head % 2]).astype(BF16)


def score_bias(lo, hi, k0):
    key = k0 + lax.broadcasted_iota(jnp.int32, (1, BLK), 1)
    allowed = (key >= lo) & (key <= hi)
    return jnp.where(allowed, 0.0, MASKED).astype(F32)


def forward(q_ref, rows, size, km, vm, keys, width, w_s, s_s, slot, bias_s, a_acc):
    for pair in range(HEADS // 2):
        cols = slice(pair * 128, (pair + 1) * 128)
        total = a_acc[:size, cols]
        for head in (2 * pair, 2 * pair + 1):
            half = mm(q_ref[rows, cols], km[head, keys, :], NT) + bias_s[:size, :width]
            weight, slope = silu_parts(half)
            weight = weight.astype(BF16)
            w_s[slot, head, :size, :width] = weight
            s_s[slot, head, :size, :width] = slope.astype(BF16)
            total = total + mm(weight, vm[head, keys, :])
        a_acc[:size, cols] = total


def backward(size, km, vm, keys, width, w_s, s_s, slot, da_s, da_t, q_t, dq_acc, dk_t, dv_t):
    for pair in range(HEADS // 2):
        cols = slice(pair * 128, (pair + 1) * 128)
        total = dq_acc[:size, cols]
        for head in (2 * pair, 2 * pair + 1):
            d_weight = mm(da_s[:size, cols], vm[head, keys, :], NT)
            d_score = d_weight * s_s[slot, head, :size, :width].astype(F32)
            d_score = d_score.astype(BF16)
            total = total + mm(d_score, km[head, keys, :])
            own = slice(head * 64, (head + 1) * 64)
            dv_t[own, keys] += mm(da_t[own, :size], w_s[slot, head, :size, :width])
            dk_t[own, keys] += mm(q_t[own, :size], d_score)
        dq_acc[:size, cols] = total


def middle(attended, x, gate, g, w_out):
    centred, rstd = moments(attended)
    normed = centred * rstd
    mixed = normed * gate
    out = (x + mm(mixed.astype(BF16), w_out)).astype(BF16)
    d_mixed = mm(g, w_out, NT)
    d_normed = d_mixed * gate
    mean_d = jnp.mean(d_normed, axis=-1, keepdims=True)
    mean_dn = jnp.mean(d_normed * normed, axis=-1, keepdims=True)
    d_att = rstd * (d_normed - mean_d - normed * mean_dn)
    return out, mixed, d_mixed * normed, d_att


def project_kernel(
    arrived, pos_row, w_proj, x_o, normed_o, rstd_o, normed_t, gate_qry, km, vm, slopes
):
    size, feature = x_o.shape
    every = slice(0, size)
    row = pl.program_id(0) * size + lax.broadcasted_iota(jnp.int32, (size, 1), 0)
    x = mm(one_hot(pos_row[...] == row), arrived[...])
    x_o[...] = x.astype(BF16)
    centred, rstd = moments(x)
    normed = centred * rstd
    rstd_o[...] = rstd
    normed_t[...] = normed.T.astype(BF16)
    normed = normed.astype(BF16)
    normed_o[...] = normed
    for part in range(4):
        cols = slice(part * feature, (part + 1) * feature)
        act, slope = silu_parts(mm(normed, w_proj[:, cols]) * 0.5)
        slopes[:, cols] = slope.astype(BF16)
        if part == 0:
            gate_qry[:, :feature] = act.astype(BF16)
        elif part == 1:
            split_heads(act, vm, every)
        elif part == 2:
            gate_qry[:, feature:] = (act.astype(BF16) * 0.0625).astype(BF16)
        else:
            split_heads(act, km, every)


def fetch(pairs, sems):
    copies = [pltpu.make_async_copy(src, dst, sems.at[i]) for i, (src, dst) in enumerate(pairs)]
    for copy in copies:
        copy.start()
    return copies


def tgt_kernel(
    cand,
    tid_col,
    tid_row,
    lo,
    hi,
    w_proj,
    w_out,
    g_tgt,
    km_in,
    vm_in,
    out_tgt,
    d_tgt,
    dk_t,
    dv_t,
    tgt_t,
    d_pre,
    km,
    vm,
    sems,
    gate_s,
    q_s,
    km_own,
    vm_own,
    w_s,
    s_s,
    bias_s,
    a_acc,
    dq_acc,
    da_s,
    da_t,
    q_t,
    dk_own,
    dv_own,
):
    copies = fetch([(km_in, km), (vm_in, vm)], sems)
    tgt_rows, feature = out_tgt.shape
    blocks = km.shape[1] // BLK
    every = slice(0, tgt_rows)
    part_cols = [slice(part * feature, (part + 1) * feature) for part in range(4)]
    col = lax.broadcasted_iota(jnp.int32, (1, cand.shape[0]), 1)
    x = mm(one_hot(tid_col[...] == col), cand[...])
    centred, rstd = moments(x)
    unit = centred * rstd
    normed = unit.astype(BF16)
    tgt_t[0] = unit.T.astype(BF16)
    for part in range(4):
        half = mm(normed, w_proj[:, part_cols[part]]) * 0.5
        act, slope = silu_parts(half)
        d_pre[:, part_cols[part]] = slope.astype(BF16)
        if part == 0:
            gate_s[...] = act.astype(BF16)
        elif part == 1:
            split_heads(act, vm_own, every)
        elif part == 2:
            q_s[...] = (act.astype(BF16) * 0.0625).astype(BF16)
        else:
            split_heads(act, km_own, every)

    a_acc[...] = jnp.zeros_like(a_acc)
    dq_acc[...] = jnp.zeros_like(dq_acc)
    dk_own[...] = jnp.zeros_like(dk_own)
    dv_own[...] = jnp.zeros_like(dv_own)
    dk_t[...] = jnp.zeros_like(dk_t)
    dv_t[...] = jnp.zeros_like(dv_t)
    for copy in copies:
        copy.wait()

    def fwd(j, c):
        k0 = pl.multiple_of(j * BLK, BLK)
        keys = pl.ds(k0, BLK)
        bias_s[...] = score_bias(lo[...], hi[...], k0)
        forward(q_s, every, tgt_rows, km, vm, keys, BLK, w_s, s_s, j, bias_s, a_acc)
        return c

    def bwd(j, c):
        keys = pl.ds(pl.multiple_of(j * BLK, BLK), BLK)
        backward(
            tgt_rows, km, vm, keys, BLK, w_s, s_s, j, da_s, da_t, q_t, dq_acc, dk_t, dv_t
        )
        return c

    lax.fori_loop(0, blocks, fwd, 0)
    same = lax.broadcasted_iota(jnp.int32, (tgt_rows, tgt_rows), 0) == lax.broadcasted_iota(
        jnp.int32, (tgt_rows, tgt_rows), 1
    )
    bias_s[:, :tgt_rows] = jnp.where(same, 0.0, MASKED).astype(F32)
    forward(
        q_s, every, tgt_rows, km_own, vm_own, every, tgt_rows, w_s, s_s, blocks, bias_s, a_acc
    )
    out, mixed, d_gate, d_att = middle(
        a_acc[...], x, gate_s[...].astype(F32), g_tgt[...], w_out[...]
    )
    out_tgt[...] = out
    tgt_t[1] = mixed.T.astype(BF16)
    d_pre[:, part_cols[0]] = (d_gate * d_pre[:, part_cols[0]].astype(F32)).astype(BF16)
    da_s[...] = d_att.astype(BF16)
    da_t[...] = d_att.T.astype(BF16)
    q_t[...] = q_s[...].astype(F32).T.astype(BF16)
    lax.fori_loop(0, blocks, bwd, 0)
    backward(
        tgt_rows, km_own, vm_own, every, tgt_rows, w_s, s_s, blocks,
        da_s, da_t, q_t, dq_acc, dk_own, dv_own,
    )
    grads = (None, dv_own[...].T, dq_acc[...] * 0.125, dk_own[...].T * 2.0)
    for part in (1, 2, 3):
        d_part = grads[part] * d_pre[:, part_cols[part]].astype(F32)
        d_pre[:, part_cols[part]] = d_part.astype(BF16)

    d_normed = mm(d_pre[...], w_proj[...], NT)
    mean_d = jnp.mean(d_normed, axis=-1, keepdims=True)
    mean_dn = jnp.mean(d_normed * unit, axis=-1, keepdims=True)
    d_x = rstd * (d_normed - mean_d - unit * mean_dn) + g_tgt[...].astype(F32)
    d_tgt[every, :] = d_x.astype(BF16)
    ids = tid_row[...]
    high = lax.shift_right_logical(ids, 6)
    low = ids - high * 64
    d_tgt[tgt_rows:, :] = jnp.zeros((d_tgt.shape[0] - tgt_rows, feature), BF16)
    wide = (d_tgt.shape[0] - tgt_rows, tgt_rows)
    d_tgt[tgt_rows:, :tgt_rows] = jnp.broadcast_to(high.astype(F32), wide).astype(BF16)
    d_tgt[tgt_rows:, tgt_rows : 2 * tgt_rows] = jnp.broadcast_to(low.astype(F32), wide).astype(BF16)


def hist_kernel(
    core_ref,
    first_ref,
    lo,
    hi,
    w_out,
    g_hist,
    g_tgt,
    tgt_t,
    tgt_pre,
    gate_qry_in,
    km_in,
    vm_in,
    x_in,
    slopes_in,
    dv_in,
    dk_in,
    normed_t_in,
    out_hist,
    keep,
    give,
    d_pre_o,
    gate_qry,
    km,
    vm,
    x_s,
    d_pre,
    dv_t,
    dk_t,
    normed_t,
    mixed_t,
    sems,
    w_s,
    s_s,
    bias_s,
    a_acc,
    dq_acc,
    da_s,
    da_t,
    q_t,
):
    copies = fetch(
        [
            (gate_qry_in, gate_qry),
            (km_in, km),
            (vm_in, vm),
            (x_in, x_s),
            (slopes_in, d_pre),
            (dv_in, dv_t),
            (dk_in, dk_t),
            (normed_t_in, normed_t),
        ],
        sems,
    )
    hist_rows, feature = out_hist.shape
    blocks = hist_rows // BLK
    part_cols = [slice(part * feature, (part + 1) * feature) for part in range(4)]
    qry = slice(feature, 2 * feature)
    q_ref = gate_qry.at[:, qry]
    for copy in copies[:3]:
        copy.wait()

    def hist_block(i, carry):
        r0 = pl.multiple_of(i * BLK, BLK)
        rows = pl.ds(r0, BLK)
        first = first_ref[i]
        a_acc[...] = jnp.zeros_like(a_acc)
        dq_acc[...] = jnp.zeros_like(dq_acc)

        def fwd(j, c):
            k0 = pl.multiple_of(j * BLK, BLK)
            keys = pl.ds(k0, BLK)
            bias_s[...] = score_bias(lo[rows, :], hi[rows, :], k0)
            forward(q_ref, rows, BLK, km, vm, keys, BLK, w_s, s_s, j, bias_s, a_acc)
            return c

        def bwd(j, c):
            keys = pl.ds(pl.multiple_of(j * BLK, BLK), BLK)
            backward(
                BLK, km, vm, keys, BLK, w_s, s_s, j, da_s, da_t, q_t, dq_acc, dk_t, dv_t
            )
            return c

        lax.fori_loop(first, i + 1, fwd, 0)

        @pl.when(i == 0)
        def _():
            for copy in copies[3:]:
                copy.wait()

        out, mixed, d_gate, d_att = middle(
            a_acc[...],
            x_s[rows, :].astype(F32),
            gate_qry[rows, :feature].astype(F32),
            g_hist[rows, :],
            w_out[...],
        )
        out_hist[rows, :] = out
        mixed_t[:, rows] = mixed.T.astype(BF16)
        d_pre[rows, part_cols[0]] = (d_gate * d_pre[rows, part_cols[0]].astype(F32)).astype(BF16)
        da_s[...] = d_att.astype(BF16)
        da_t[...] = d_att.T.astype(BF16)
        q_t[...] = gate_qry[rows, qry].astype(F32).T.astype(BF16)
        lax.fori_loop(first, i + 1, bwd, 0)
        d_q = dq_acc[...] * 0.125 * d_pre[rows, part_cols[2]].astype(F32)
        d_pre[rows, part_cols[2]] = d_q.astype(BF16)
        return carry

    lax.fori_loop(0, blocks, hist_block, 0)

    def spread(i, carry):
        rows = pl.ds(pl.multiple_of(i * BLK, BLK), BLK)
        vals, keys = part_cols[1], part_cols[3]
        d_pre[rows, vals] = (dv_t[:, rows].T * d_pre[rows, vals].astype(F32)).astype(BF16)
        d_pre[rows, keys] = (dk_t[:, rows].T * 2.0 * d_pre[rows, keys].astype(F32)).astype(BF16)
        return carry

    lax.fori_loop(0, blocks, spread, 0)
    sent = pltpu.make_async_copy(d_pre, d_pre_o, sems.at[len(copies)])
    sent.start()

    core = core_ref[0]
    half_rows = feature // 2
    for dest, half in ((give, 1 - core), (keep, core)):
        rows = pl.ds(pl.multiple_of(half * half_rows, half_rows), half_rows)
        for part in range(5):
            if part < 4:
                total = mm(normed_t[rows, :], d_pre[:, part_cols[part]])
                total = total + mm(tgt_t[0, rows, :], tgt_pre[:, part_cols[part]])
            else:
                total = mm(mixed_t[rows, :], g_hist[...]) + mm(tgt_t[1, rows, :], g_tgt[...])
            for group, dest_cols, cols in segments(part, feature):
                piece = total[:, cols].reshape(16, 16, cols.stop - cols.start)
                dest[:, group, :, dest_cols] = piece.astype(BF16)
    sent.wait()


def segments(part, feature):
    found, begin = [], part * feature
    while begin < (part + 1) * feature:
        group = begin // 640
        end = min((part + 1) * feature, (group + 1) * 640)
        found.append(
            (group, slice(begin - group * 640, end - group * 640), slice(begin - part * feature, end - part * feature))
        )
        begin = end
    return found


def rows_kernel(d_pre, w_proj, normed, rstd, g_hist, pos_col, slot_grads, d_hist):
    hist_rows, feature = g_hist.shape

    def back(i, carry):
        rows = pl.ds(pl.multiple_of(i * BLK, BLK), BLK)
        d_normed = mm(d_pre[rows, :], w_proj[...], NT)
        unit = normed[rows, :].astype(F32)
        mean_d = jnp.mean(d_normed, axis=-1, keepdims=True)
        mean_dn = jnp.mean(d_normed * unit, axis=-1, keepdims=True)
        d_x = rstd[rows, :] * (d_normed - mean_d - unit * mean_dn)
        d_hist[rows, :] = (d_x + g_hist[rows, :].astype(F32)).astype(BF16)
        return carry

    lax.fori_loop(0, hist_rows // BLK, back, 0)

    def pick(i, carry):
        rows = pl.ds(pl.multiple_of(i * BLK, BLK), BLK)
        row = lax.broadcasted_iota(jnp.int32, (1, hist_rows), 1)
        onehot = one_hot(pos_col[rows, :] == row)
        slot_grads[rows, :] = mm(onehot, d_hist[...]).astype(BF16)
        return carry

    lax.fori_loop(0, slot_grads.shape[0] // BLK, pick, 0)


def cand_kernel(first_ref, rows, out):
    count, feature = out.shape
    own = first_ref[0] + lax.broadcasted_iota(jnp.int32, (count, 1), 0)
    total = jnp.zeros((count, feature), F32)
    for peer in range(rows.shape[0]):
        high = rows[peer, count : count + 16, :count].astype(F32)[:1]
        low = rows[peer, count : count + 16, count : 2 * count].astype(F32)[:1]
        ids = (high * 64.0 + low).astype(jnp.int32)
        total = total + mm(one_hot(own == ids), rows[peer, :count, :])
    out[...] = total


def reduce_kernel(pieces, slot_grads, copies):
    del slot_grads
    total = jnp.sum(pieces[...].astype(F32), axis=0).astype(BF16)
    for peer in range(copies.shape[0]):
        copies[peer] = total


def sums_kernel(pieces, d_proj, d_out):
    quarter, feature = d_out.shape
    for part in range(5):
        for group, source_cols, cols in segments(part, feature):
            piece = pieces[0, :, group, :, source_cols].astype(F32)
            piece = piece.reshape(quarter, cols.stop - cols.start)
            if part < 4:
                base = part * feature
                d_proj[:, base + cols.start : base + cols.stop] = piece
            else:
                d_out[:, cols] = piece


VMEM = pl.BlockSpec(memory_space=pltpu.VMEM)
SMEM = pl.BlockSpec(memory_space=pltpu.SMEM)
ANY = pl.BlockSpec(memory_space=pl.ANY)


def params(mib):
    return pltpu.CompilerParams(vmem_limit_bytes=mib << 20)


def cost(flops, nbytes):
    return pl.CostEstimate(flops=flops, bytes_accessed=nbytes, transcendentals=0)


def local(
    send_rows, slot_pos, lengths, candidates, target_ids, w_proj, w_out, g_hist, g_tgt
):
    peers, capacity, feature = send_rows.shape[1:]
    slots = peers * capacity
    hist_rows, tgt_rows = g_hist.shape[0], g_tgt.shape[0]
    blocks = hist_rows // BLK
    each = target_ids.shape[1]
    table = lax.all_gather(candidates, "mem", axis=0, tiled=True)
    arrived = lax.all_to_all(send_rows, BOTH, split_axis=1, concat_axis=0, tiled=True)
    arrived = arrived.reshape(slots, feature)

    pos_row = slot_pos.reshape(1, slots)
    pos_col = slot_pos.reshape(slots, 1)
    ends = jnp.cumsum(lengths[0])
    starts = ends - lengths[0]
    row = jnp.arange(hist_rows, dtype=jnp.int32)[:, None]
    hist_lo = jnp.max(jnp.where(row >= starts[None, :], starts[None, :], 0), axis=1)
    first = (hist_lo[::BLK] // BLK).astype(jnp.int32)
    tgt_lo = jnp.repeat(starts, each).astype(jnp.int32)[:, None]
    tgt_hi = jnp.repeat(ends - 1, each).astype(jnp.int32)[:, None]
    core = lax.rem(lax.axis_index("grp"), 2).astype(jnp.int32)[None]

    sds = jax.ShapeDtypeStruct

    def by_rows(width):
        return pl.BlockSpec((BLK, width), lambda i: (i, 0))

    def whole(*shape):
        return pl.BlockSpec(shape, lambda i: (0,) * len(shape))

    per_head = pl.BlockSpec((HEADS, BLK, 128), lambda i: (0, i, 0))
    x_hist, normed, rstd, normed_t, gate_qry, km, vm, slopes = pl.pallas_call(
        project_kernel,
        grid=(blocks,),
        out_shape=(
            sds((hist_rows, feature), BF16),
            sds((hist_rows, feature), BF16),
            sds((hist_rows, 1), F32),
            sds((feature, hist_rows), BF16),
            sds((hist_rows, 2 * feature), BF16),
            sds((HEADS, hist_rows, 128), BF16),
            sds((HEADS, hist_rows, 128), BF16),
            sds((hist_rows, 4 * feature), BF16),
        ),
        in_specs=[whole(slots, feature), whole(1, slots), whole(feature, 4 * feature)],
        out_specs=(
            by_rows(feature),
            by_rows(feature),
            by_rows(1),
            pl.BlockSpec((feature, BLK), lambda i: (0, i)),
            by_rows(2 * feature),
            per_head,
            per_head,
            by_rows(4 * feature),
        ),
        compiler_params=params(56),
        cost_estimate=cost(5 << 30, 20 << 20),
        name="project",
    )(arrived, pos_row, w_proj)

    scratch = pltpu.VMEM
    out_tgt, d_tgt, dk_t, dv_t, tgt_t, tgt_pre = pl.pallas_call(
        tgt_kernel,
        out_shape=(
            sds((tgt_rows, feature), BF16),
            sds((tgt_rows + 16, feature), BF16),
            sds((feature, hist_rows), F32),
            sds((feature, hist_rows), F32),
            sds((2, feature, tgt_rows), BF16),
            sds((tgt_rows, 4 * feature), BF16),
        ),
        in_specs=[VMEM] * 8 + [ANY] * 2,
        out_specs=(VMEM,) * 6,
        scratch_shapes=[
            scratch((HEADS, hist_rows, 128), BF16),
            scratch((HEADS, hist_rows, 128), BF16),
            pltpu.SemaphoreType.DMA((2,)),
            scratch((tgt_rows, feature), BF16),
            scratch((tgt_rows, feature), BF16),
            scratch((HEADS, tgt_rows, 128), BF16),
            scratch((HEADS, tgt_rows, 128), BF16),
            scratch((blocks + 1, HEADS, tgt_rows, BLK), BF16),
            scratch((blocks + 1, HEADS, tgt_rows, BLK), BF16),
            scratch((tgt_rows, BLK), F32),
            scratch((tgt_rows, feature), F32),
            scratch((tgt_rows, feature), F32),
            scratch((tgt_rows, feature), BF16),
            scratch((feature, tgt_rows), BF16),
            scratch((feature, tgt_rows), BF16),
            scratch((feature, tgt_rows), F32),
            scratch((feature, tgt_rows), F32),
        ],
        compiler_params=params(56),
        cost_estimate=cost(6 << 30, 16 << 20),
        name="tgt",
    )(
        table,
        target_ids.reshape(tgt_rows, 1),
        target_ids.reshape(1, tgt_rows),
        tgt_lo,
        tgt_hi,
        w_proj,
        w_out,
        g_tgt,
        km,
        vm,
    )
    tgt_grads = lax.all_gather(d_tgt, "mem", axis=0, tiled=False)

    pieces = (16, 4, 16, 640)
    out_hist, keep, give, d_pre = pl.pallas_call(
        hist_kernel,
        out_shape=(
            sds((hist_rows, feature), BF16),
            sds(pieces, BF16),
            sds(pieces, BF16),
            sds((hist_rows, 4 * feature), BF16),
        ),
        in_specs=[SMEM] * 2 + [VMEM] * 7 + [ANY] * 8,
        out_specs=(VMEM, VMEM, VMEM, ANY),
        scratch_shapes=[
            scratch((hist_rows, 2 * feature), BF16),
            scratch((HEADS, hist_rows, 128), BF16),
            scratch((HEADS, hist_rows, 128), BF16),
            scratch((hist_rows, feature), BF16),
            scratch((hist_rows, 4 * feature), BF16),
            scratch((feature, hist_rows), F32),
            scratch((feature, hist_rows), F32),
            scratch((feature, hist_rows), BF16),
            scratch((feature, hist_rows), BF16),
            pltpu.SemaphoreType.DMA((9,)),
            scratch((blocks, HEADS, BLK, BLK), BF16),
            scratch((blocks, HEADS, BLK, BLK), BF16),
            scratch((BLK, BLK), F32),
            scratch((BLK, feature), F32),
            scratch((BLK, feature), F32),
            scratch((BLK, feature), BF16),
            scratch((feature, BLK), BF16),
            scratch((feature, BLK), BF16),
        ],
        compiler_params=params(56),
        cost_estimate=cost(18 << 30, 24 << 20),
        name="hist",
    )(
        core,
        first,
        hist_lo.astype(jnp.int32)[:, None],
        row,
        w_out,
        g_hist,
        g_tgt,
        tgt_t,
        tgt_pre,
        gate_qry,
        km,
        vm,
        x_hist,
        slopes,
        dv_t,
        dk_t,
        normed_t,
    )

    swapped = lax.ppermute(give, BOTH, core_swap())
    chip_sum = (keep.astype(F32) + swapped.astype(F32)).astype(BF16)
    chip_sum = chip_sum.reshape(64, 1, 16, 640)
    scattered = lax.all_to_all(
        chip_sum, BOTH, split_axis=0, concat_axis=1, tiled=True, axis_index_groups=same_core()
    )
    slot_grads = pl.pallas_call(
        rows_kernel,
        out_shape=sds((slots, feature), BF16),
        in_specs=[VMEM] * 6,
        out_specs=VMEM,
        scratch_shapes=[scratch((hist_rows, feature), BF16)],
        compiler_params=params(56),
        cost_estimate=cost(5 << 30, 16 << 20),
        name="rows",
    )(d_pre, w_proj, normed, rstd, g_hist, pos_col)
    copies = pl.pallas_call(
        reduce_kernel,
        out_shape=sds((16, 16, 640), BF16),
        in_specs=[VMEM, ANY],
        out_specs=VMEM,
        compiler_params=params(56),
        name="reduce",
    )(scattered.reshape(64, 16, 640), slot_grads)
    level = lax.all_to_all(
        copies.reshape(16, 1, 16, 640), "mem", split_axis=0, concat_axis=1, tiled=True
    ).reshape(256, 640)
    everything = lax.all_gather(level, "grp", axis=0, tiled=True)

    returned = lax.all_to_all(
        slot_grads.reshape(peers, 1, capacity, feature),
        BOTH,
        split_axis=0,
        concat_axis=1,
        tiled=True,
    )
    sum_proj, sum_out = pl.pallas_call(
        sums_kernel,
        out_shape=(sds(w_proj.shape, F32), sds(w_out.shape, F32)),
        grid=(2, 4),
        in_specs=[pl.BlockSpec((1, 4, 4, 16, 640), lambda c, z: (2 * z + c, 0, 0, 0, 0))],
        out_specs=(
            pl.BlockSpec((64, 4 * feature), lambda c, z: (4 * c + z, 0)),
            pl.BlockSpec((64, feature), lambda c, z: (4 * c + z, 0)),
        ),
        compiler_params=params(56),
        name="sums",
    )(everything.reshape(8, 4, 4, 16, 640))

    mine = (lax.axis_index("mem") * candidates.shape[0]).astype(jnp.int32)[None]
    d_cand = pl.pallas_call(
        cand_kernel,
        out_shape=sds(candidates.shape, F32),
        in_specs=[SMEM, VMEM],
        out_specs=VMEM,
        compiler_params=params(56),
        name="cand",
    )(mine, tgt_grads)
    return (out_hist, out_tgt, returned, d_cand, sum_proj, sum_out)


def core_swap():
    return [(i, i + 16 if (i // 16) % 2 == 0 else i - 16) for i in range(128)]


def same_core():
    return [[i for i in range(128) if (i // 16) % 2 == core] for core in (0, 1)]


def solution(mesh):
    placed = (
        P(BOTH, None, None, None),
        P(BOTH, None, None),
        P(BOTH, None),
        P(BOTH, None),
        P(BOTH, None),
        P(),
        P(),
        P(BOTH, None),
        P(BOTH, None),
    )
    return jax.shard_map(
        local,
        mesh=mesh,
        in_specs=placed,
        out_specs=(
            P(BOTH, None),
            P(BOTH, None),
            P(BOTH, None, None, None),
            P(BOTH, None),
            P(),
            P(),
        ),
        check_vma=False,
    )
```

time: 248 us -> 243 us (0.980)
  Pallas kernels: 78.8 us -> 100 us
  starting transfers between devices: 43.1 us -> 28.2 us
  waiting for transfers between devices: 87.2 us -> 73.2 us
  blocking collectives: 0 us -> 11.9 us
  local copies, waits for them, and re-layouts: 22.1 us -> 10.9 us
    unnamed x42 -> x12, local copies, waits for them, and re-layouts: 19.5 us -> 3.8 us
    pallas_call x0 -> x2, Pallas kernels: none -> 14.9 us  [the longest x1 12.7 us: local(): pl.pallas_call(project_kernel, grid=(blocks,), out_shape=(sds((hist_rows,...]
    all_to_all x1, waiting for transfers between devices: 19.7 us -> 5.63 us  [local(): lax.all_to_all(chip_sum, BOTH, split_axis=0, concat_axis=1, tiled=True, a...]
    all_to_all x0 -> x1, blocking collectives: none -> 11.9 us  [local(): lax.all_to_all(copies.reshape(16, 1, 16, 640), 'mem', split_axis=0, conca...]
    ppermute x2 -> x1, starting transfers between devices: 8.7 us -> 1.59 us  [local(): swapped = lax.ppermute(give, BOTH, core_swap())]
    pallas_call x1, Pallas kernels: 27.2 us -> 20.2 us  [local(): pl.pallas_call(tgt_kernel, out_shape=(sds((tgt_rows, feature), BF16), sds...]
    all_gather x0 -> x1, waiting for transfers between devices: none -> 5.97 us  [local(): everything = lax.all_gather(level, 'grp', axis=0, tiled=True)]
    all_to_all x1, starting transfers between devices: 12.4 us -> 6.84 us  [local(): lax.all_to_all(slot_grads.reshape(peers, 1, capacity, feature), BOTH, spl...]
  transfers between devices with their start and end apart: 8 -> 7, of which waited for: 5 -> 6; matrix products, arithmetic and copies ran while one was open for 1% -> 4% of each run, Pallas kernels for 20% -> 30%
where the time goes in v3:
time: 243 us; the launch traced here: 242 us
  Pallas kernels  100 us (41%)
  waiting for transfers between devices  73.2 us (30%)
  starting transfers between devices  28.2 us (12%)
  between operations  13.8 us (6%)
  blocking collectives  11.9 us (5%)
  local copies, waits for them, and re-layouts  10.9 us (4%)
  other arithmetic  3.64 us (1%)
    pallas_call x1, Pallas kernels, local(): pl.pallas_call(hist_kernel, out_shape=(sds((hist_rows, feature), BF16), s...  42.6 us
    all_to_all x1, waiting for transfers between devices, local(): lax.all_to_all(slot_grads.reshape(peers, 1, capacity, feature), BOTH, spl...  29.9 us
    all_to_all x1, waiting for transfers between devices, local(): lax.all_to_all(send_rows, BOTH, split_axis=1, concat_axis=0, tiled=True)  26.1 us
    pallas_call x1, Pallas kernels, local(): pl.pallas_call(tgt_kernel, out_shape=(sds((tgt_rows, feature), BF16), sds...  20.2 us
    pallas_call x1, Pallas kernels, local(): pl.pallas_call(rows_kernel, out_shape=sds((slots, feature), BF16), in_spe...  12.9 us
    pallas_call x1, Pallas kernels, local(): pl.pallas_call(project_kernel, grid=(blocks,), out_shape=(sds((hist_rows,...  12.7 us
    all_to_all x1, blocking collectives, local(): lax.all_to_all(copies.reshape(16, 1, 16, 640), 'mem', split_axis=0, conca...  11.9 us
    all_to_all x1, starting transfers between devices, local(): lax.all_to_all(send_rows, BOTH, split_axis=1, concat_axis=0, tiled=True)  11.5 us
  transfers between devices with their start and end apart: 7, of which 6 were waited for; matrix products, arithmetic and copies ran while one was open for 4% of the time, Pallas kernels for 30%

profile of v3, /device:TPU:1, one launch (start us, length us, event | category | flops | bytes accessed | tf_op | source)
XLA Modules:
  0.0 241.8 jit_solution(8627587172512580641)
XLA Ops:
  7.2 0.7 all-gather.5.cloned.1.call-update
  7.9 11.5 %all-to-all-start = ((bf16[1,128,16,512]{3,2,0,1:T(8,128)(2,1)}), bf16[1,128,16,512]{3,2,0,1:T(8,128)(2,1)S(1)}, u32[]{:S(2)}, u32[]{:S(2)}) async-start(bf16[1,128,16,512]{3,2,0,1:T(8,128)(2,1)} %bitcast.35), calls=%async_computation | async-start | bytes 4194304 | tf_op jit(solution)/shard_map/all_to_all | solution.py:486
  19.5 0.7 reshape.85.tid_col
  20.2 0.6 reshape.73.tid_row
  20.9 0.7 reshape.76.pos_row
  21.9 0.7 broadcast_in_dim_reshape.8.lo
  22.7 0.7 broadcast_in_dim_reshape.9.hi
  23.6 1.0 copy.43.lo
  24.6 0.6 and_select_fusion.first_ref
  25.2 26.1 %all-to-all-done = bf16[1,128,16,512]{3,2,0,1:T(8,128)(2,1)S(1)} async-done(((bf16[1,128,16,512]{3,2,0,1:T(8,128)(2,1)}), bf16[1,128,16,512]{3,2,0,1:T(8,128)(2,1)S(1)}, u32[]{:S(2)}, u32[]{:S(2)}) %all-to-all-start) | async-done | bytes 2097184 | tf_op jit(solution)/shard_map/all_to_all | solution.py:486
  51.3 1.3 copy-done.1
  52.6 12.7 %project.1 = (bf16[1024,512]{1,0:T(8,128)(2,1)}, bf16[1024,512]{1,0:T(8,128)(2,1)}, f32[1024,1]{1,0:T(8,128)}, bf16[512,1024]{1,0:T(8,128)(2,1)}, bf16[1024,1024...) custom-call(bf16[2048,512]{1,0:T(8,128)(2,1)} %bitcast.36, ...), custom_call_target="tpu_custom_call" | custom-call | flops 5368709120 | bytes 20971520 | tf_op jit(solution)/shard_map/project/pallas_call | solution.py:509
  65.3 2.0 all-gather.5.cloned.1.call-done.cand
  67.3 20.2 %tgt.1 = (bf16[128,512]{1,0:T(8,128)(2,1)}, bf16[144,512]{1,0:T(8,128)(2,1)}, f32[512,1024]{1,0:T(8,128)}, f32[512,1024]{1,0:T(8,128)}, bf16[2,512,128]{2,1,0:T(8,128)(2,1)}, /*index=5*/bf16[128,2048]{1,0:T(8,128)(2,1)}) custom-call(bf16[2048,512]{1,0:T(8,128)(2,1)} %all-gather.5.cloned.1.call-done.cand, s32[128,1]{1,0:T(8,128)} %reshape.85.tid_col, ...), custom_call_target="tpu_custom_call" | custom-call | flops 6442450944 | bytes 16777216 | tf_op jit(solution)/shard_map/tgt/pallas_call | solution.py:539
  87.6 0.9 iota.6.hi
  88.4 42.6 %hist.1 = (bf16[1024,512]{1,0:T(8,128)(2,1)}, bf16[16,4,16,640]{3,2,1,0:T(8,128)(2,1)}, bf16[16,4,16,640]{3,2,1,0:T(8,128)(2,1)}, bf16[1024,2048]{1,0:T(8,128)(2,1)}) custom-call(s32[1]{0:T(128)} %bitcast.core_ref, s32[4]{0:T(128)} %and_select_fusion.first_ref, s32[1024,1]{1,0:T(8,128)} %copy.43.lo, s32[1024,1]{1,0:T(8,128)} %iota.6.hi, ...), custom_call_target="tpu_custom_call" | custom-call | flops 19327352832 | bytes 25165824 | tf_op jit(solution)/shard_map/hist/pallas_call | solution.py:588
  131.0 1.6 collective-permute-start
  132.6 2.9 %collective-permute-done = bf16[16,4,16,640]{3,2,1,0:T(8,128)(2,1)S(1)} collective-permute-done((bf16[16,4,16,640]{3,2,1,0:T(8,128)(2,1)}, bf16[16,4,16,640]{3,2,1,0:T(8,128)(2,1)S(1)}, u32[]{:S(2)}, u32[]{:S(2)}) %collective-permute-start) | collective-permute-done | bytes 1310752 | tf_op jit(solution)/shard_map/ppermute | solution.py:641
  135.5 2.8 %add_convert_fusion = bf16[16,4,16,640]{3,2,1,0:T(8,128)(2,1)} fusion(bf16[16,4,16,640]{3,2,1,0:T(8,128)(2,1)S(1)} %collective-permute-done, bf16[16,4,16,640]{3,2,1,0:T(8,128)(2,1)} %get-tuple-element.42), kind=kLoop, calls=%fused_computation | loop fusion | flops 2621440 | bytes 3932160 | tf_op jit(solution)/shard_map/convert_element_type | solution.py:642
  138.3 8.2 %all-to-all-start.2 = ((bf16[64,1,16,640]{3,2,1,0:T(8,128)(2,1)}), bf16[64,1,16,640]{3,2,1,0:T(8,128)(2,1)S(1)}, u32[]{:S(2)}, u32[]{:S(2)}) async-start(bf16[64,1,16,640]{3,2,1,0:T(8,128)(2,1)} %bitcast.15), calls=%async_computation.2 | async-start | bytes 2621440 | tf_op jit(solution)/shard_map/all_to_all | solution.py:644
  146.5 1.6 reshape.86.pos_col
  148.1 12.9 %rows.1.slot_grads = bf16[2048,512]{1,0:T(8,128)(2,1)} custom-call(bf16[1024,2048]{1,0:T(8,128)(2,1)} %get-tuple-element.38.d_pre, bf16[512,2048]{1,0:T(8,128)(2,1)} %w_proj.5, bf16[1024,512]{1,0:T(8,128)(2,1)} %get-tuple-element.39.normed, f32[1024,1]{1,0:T(8,128)} %get-tuple-element.40.rstd, bf16[1024,512]{1,0:T(8,128)(2,1)} %g_hist.3, ...), custom_call_target="tpu_custom_call" | custom-call | flops 5368709120 | bytes 16777216 | tf_op jit(solution)/shard_map/rows/pallas_call | solution.py:647
  161.0 5.6 %all-to-all-done.2 = bf16[64,1,16,640]{3,2,1,0:T(8,128)(2,1)S(1)} async-done(((bf16[64,1,16,640]{3,2,1,0:T(8,128)(2,1)}), bf16[64,1,16,640]{3,2,1,0:T(8,128)(2,1)S(1)}, u32[]{:S(2)}, u32[]{:S(2)}) %all-to-all-start.2) | async-done | bytes 1310752 | tf_op jit(solution)/shard_map/all_to_all | solution.py:644
  166.6 1.1 copy-done
  167.7 2.2 reduce.1
  169.9 11.9 %all_to_all.19 = bf16[16,1,16,640]{3,2,1,0:T(8,128)(2,1)} all-to-all(bf16[16,1,16,640]{3,2,1,0:T(8,128)(2,1)} %bitcast.37), channel_id=1, replica_groups=mesh['grp'=8,'mem'=16] {'mem'}, dimensions={0} | all-to-all | bytes 655360 | tf_op jit(solution)/shard_map/all_to_all | solution.py:665
  181.8 6.8 %all-to-all-start.1 = ((bf16[128,1,16,512]{3,2,1,0:T(8,128)(2,1)}), bf16[128,1,16,512]{3,2,1,0:T(8,128)(2,1)S(1)}, u32[]{:S(2)}, u32[]{:S(2)}) async-start(bf16[128,1,16,512]{3,2,1,0:T(8,128)(2,1)} %bitcast.10), calls=%async_computation.1 | async-start | bytes 4194304 | tf_op jit(solution)/shard_map/all_to_all | solution.py:670
  188.7 29.9 %all-to-all-done.1 = bf16[128,1,16,512]{3,2,1,0:T(8,128)(2,1)S(1)} async-done(((bf16[128,1,16,512]{3,2,1,0:T(8,128)(2,1)}), bf16[128,1,16,512]{3,2,1,0:T(8,128)(2,1)S(1)}, u32[]{:S(2)}, u32[]{:S(2)}) %all-to-all-start.1) | async-done | bytes 2097184 | tf_op jit(solution)/shard_map/all_to_all | solution.py:670
  218.6 3.1 %cand.1 = f32[128,512]{1,0:T(8,128)} custom-call(s32[1]{0:T(128)} %bitcast.12.first_ref, bf16[16,144,512]{2,1,0:T(8,128)(2,1)} %bitcast.34), custom_call_target="tpu_custom_call" | custom-call | tf_op jit(solution)/shard_map/cand/pallas_call | solution.py:691
  221.7 6.0 %all-gather.7.cloned.1.call-done = bf16[2048,640]{1,0:T(8,128)(2,1)} async-done(((bf16[256,640]{1,0:T(8,128)(2,1)}), bf16[2048,640]{1,0:T(8,128)(2,1)}) %all-gather.7.cloned.1.call-update) | async-done | bytes 2621456 | tf_op jit(solution)/shard_map/all_gather | solution.py:668
  227.6 6.3 %sums.1 = (f32[512,2048]{1,0:T(8,128)}, f32[512,512]{1,0:T(8,128)}) custom-call(bf16[8,4,4,16,640]{4,3,2,1,0:T(8,128)(2,1)} %bitcast.33), custom_call_target="tpu_custom_call" | custom-call | tf_op jit(solution)/shard_map/sums/pallas_call | solution.py:677
  233.9 1.3 copy.50
  (22 shorter events, 0.8 us)
Async XLA Ops:
  7.2 60.1 %all-gather.5.cloned.1.call-start = ((), (), s32[]{:S(2)}) async-start(), calls=%async_computation.4 | async-start | bytes 2228224 | tf_op jit(solution)/shard_map/all_gather | solution.py:485
  7.9 11.6 %copy-start.2 = (s32[8,16]{1,0:T(8,128)S(1)}, s32[8,16]{1,0:T(8,128)}, u32[]{:S(2)}) copy-start(s32[8,16]{1,0:T(8,128)} %param.13) | copy-start | bytes 1540
  7.9 12.9 %copy-start.3 = (s32[1,128,16]{1,2,0:T(8,128)S(1)}, s32[1,128,16]{1,2,0:T(8,128)}, u32[]{:S(2)}) copy-start(s32[1,128,16]{1,2,0:T(8,128)} %param.10) | copy-start | bytes 24580
  7.9 13.7 %copy-start.4 = (s32[1,8]{1,0:T(1,128)S(1)}, s32[1,8]{1,0:T(1,128)}, u32[]{:S(2)}) copy-start(s32[1,8]{1,0:T(1,128)} %param.11) | copy-start | bytes 100
  7.9 43.4 %all-to-all-start = ((bf16[1,128,16,512]{3,2,0,1:T(8,128)(2,1)}), bf16[1,128,16,512]{3,2,0,1:T(8,128)(2,1)S(1)}, u32[]{:S(2)}, u32[]{:S(2)}) async-start(bf16[1,128,16,512]{3,2,0,1:T(8,128)(2,1)} %bitcast.35), calls=%async_computation | async-start | bytes 4194304 | tf_op jit(solution)/shard_map/all_to_all | solution.py:486
  19.4 199.1 %all-gather.9.cloned.1.call-start = ((), (), s32[]{:S(2)}) async-start(), calls=%async_computation.6 | async-start | bytes 2506752 | tf_op jit(solution)/shard_map/all_gather | solution.py:585
  51.3 1.3 copy-start.1
  131.0 4.5 %collective-permute-start = (bf16[16,4,16,640]{3,2,1,0:T(8,128)(2,1)}, bf16[16,4,16,640]{3,2,1,0:T(8,128)(2,1)S(1)}, u32[]{:S(2)}, u32[]{:S(2)}) collective-permute-start(bf16[16,4,16,640]{3,2,1,0:T(8,128)(2,1)} %get-tuple-element.43), channel_id=1, source_target_pairs={{0,16},{1,17},{2,18},{3,19},{4,20},{5,21},{6,22},{7,23},{8,24},{9,... | collective-permute-start | bytes 3932168 | tf_op jit(solution)/shard_map/ppermute | solution.py:641
  138.3 28.4 %all-to-all-start.2 = ((bf16[64,1,16,640]{3,2,1,0:T(8,128)(2,1)}), bf16[64,1,16,640]{3,2,1,0:T(8,128)(2,1)S(1)}, u32[]{:S(2)}, u32[]{:S(2)}) async-start(bf16[64,1,16,640]{3,2,1,0:T(8,128)(2,1)} %bitcast.15), calls=%async_computation.2 | async-start | bytes 2621440 | tf_op jit(solution)/shard_map/all_to_all | solution.py:644
  146.5 81.2 %all-gather.7.cloned.1.call-start = ((), (), s32[]{:S(2)}) async-start(), calls=%async_computation.5 | async-start | bytes 2949120 | tf_op jit(solution)/shard_map/all_gather | solution.py:668
  166.6 1.1 copy-start
  181.8 36.7 %all-to-all-start.1 = ((bf16[128,1,16,512]{3,2,1,0:T(8,128)(2,1)}), bf16[128,1,16,512]{3,2,1,0:T(8,128)(2,1)S(1)}, u32[]{:S(2)}, u32[]{:S(2)}) async-start(bf16[128,1,16,512]{3,2,1,0:T(8,128)(2,1)} %bitcast.10), calls=%async_computation.1 | async-start | bytes 4194304 | tf_op jit(solution)/shard_map/all_to_all | solution.py:670
Sparse Core Ops, SparseCore 0:
  10.1 57.1 all-gather.4
  87.7 44.7 all-gather.8
  181.9 45.6 all-gather.6

commit v4 on v3

--- a/solution.py
+++ b/solution.py
@@ -6,6 +6,7 @@
 from jax.sharding import PartitionSpec as P
 
 HEADS = 8
+PAIRS = HEADS // 2
 EPS = 1e-05
 BLK = 256
 MASKED = -1e9
@@ -42,46 +43,54 @@
     return jnp.where(hits, 1.0, 0.0).astype(BF16)
 
 
-def split_heads(act, dest, rows):
-    halves = head_masks()
-    for head in range(HEADS):
-        pair = act[:, (head // 2) * 128 : (head // 2 + 1) * 128]
-        dest[head, rows, :] = (pair * halves[head % 2]).astype(BF16)
-
-
 def score_bias(lo, hi, k0):
     key = k0 + lax.broadcasted_iota(jnp.int32, (1, BLK), 1)
     allowed = (key >= lo) & (key <= hi)
     return jnp.where(allowed, 0.0, MASKED).astype(F32)
 
 
-def forward(q_ref, rows, size, km, vm, keys, width, w_s, s_s, slot, bias_s, a_acc):
-    for pair in range(HEADS // 2):
+def stack_heads(rows, dest, size):
+    for pair in range(PAIRS):
+        both = rows[:, pair * 128 : (pair + 1) * 128]
+        for place, keep in enumerate(head_masks()):
+            dest[pair, place * size : (place + 1) * size, :] = (both * keep).astype(BF16)
+
+
+def stack_columns(rows_t, dest, size):
+    for head in range(HEADS):
+        pair, place = head // 2, head % 2
+        own = rows_t[head * 64 : (head + 1) * 64, :].astype(BF16)
+        dest[pair, place * 64 : (place + 1) * 64, place * size : (place + 1) * size] = own
+
+
+def merge_heads(acc, size):
+    first, second = head_masks()
+    return jnp.concatenate(
+        [acc[pair, :size, :] * first + acc[pair, size:, :] * second for pair in range(PAIRS)],
+        axis=1,
+    )
+
+
+def forward(q_st, k_ref, v_ref, keys, w_s, s_s, slot, bias, a_acc):
+    size, width = bias.shape
+    for pair in range(PAIRS):
         cols = slice(pair * 128, (pair + 1) * 128)
-        total = a_acc[:size, cols]
-        for head in (2 * pair, 2 * pair + 1):
-            half = mm(q_ref[rows, cols], km[head, keys, :], NT) + bias_s[:size, :width]
-            weight, slope = silu_parts(half)
-            weight = weight.astype(BF16)
-            w_s[slot, head, :size, :width] = weight
-            s_s[slot, head, :size, :width] = slope.astype(BF16)
-            total = total + mm(weight, vm[head, keys, :])
-        a_acc[:size, cols] = total
-
-
-def backward(size, km, vm, keys, width, w_s, s_s, slot, da_s, da_t, q_t, dq_acc, dk_t, dv_t):
-    for pair in range(HEADS // 2):
+        half = mm(q_st[pair], k_ref[keys, cols], NT).reshape(2, size, width)
+        weight, slope = silu_parts((half + bias[...][None]).reshape(2 * size, width))
+        weight = weight.astype(BF16)
+        w_s[slot, pair, :, :width] = weight
+        s_s[slot, pair, :, :width] = slope.astype(BF16)
+        a_acc[pair] += mm(weight, v_ref[keys, cols])
+
+
+def backward(q_t, k_ref, v_ref, keys, width, w_s, s_s, slot, da_st, da_t, dq_acc, dk_t, dv_t):
+    for pair in range(PAIRS):
         cols = slice(pair * 128, (pair + 1) * 128)
-        total = dq_acc[:size, cols]
-        for head in (2 * pair, 2 * pair + 1):
-            d_weight = mm(da_s[:size, cols], vm[head, keys, :], NT)
-            d_score = d_weight * s_s[slot, head, :size, :width].astype(F32)
-            d_score = d_score.astype(BF16)
-            total = total + mm(d_score, km[head, keys, :])
-            own = slice(head * 64, (head + 1) * 64)
-            dv_t[own, keys] += mm(da_t[own, :size], w_s[slot, head, :size, :width])
-            dk_t[own, keys] += mm(q_t[own, :size], d_score)
-        dq_acc[:size, cols] = total
+        d_weight = mm(da_st[pair], v_ref[keys, cols], NT)
+        d_score = (d_weight * s_s[slot, pair, :, :width].astype(F32)).astype(BF16)
+        dq_acc[pair] += mm(d_score, k_ref[keys, cols])
+        dv_t[cols, keys] += mm(da_t[pair], w_s[slot, pair, :, :width])
+        dk_t[cols, keys] += mm(q_t[pair], d_score)
 
 
 def middle(attended, x, gate, g, w_out):
@@ -98,10 +107,9 @@
 
 
 def project_kernel(
-    arrived, pos_row, w_proj, x_o, normed_o, rstd_o, normed_t, gate_qry, km, vm, slopes
+    arrived, pos_row, w_proj, x_o, normed_o, rstd_o, normed_t, acts, slopes
 ):
     size, feature = x_o.shape
-    every = slice(0, size)
     row = pl.program_id(0) * size + lax.broadcasted_iota(jnp.int32, (size, 1), 0)
     x = mm(one_hot(pos_row[...] == row), arrived[...])
     x_o[...] = x.astype(BF16)
@@ -115,14 +123,8 @@
         cols = slice(part * feature, (part + 1) * feature)
         act, slope = silu_parts(mm(normed, w_proj[:, cols]) * 0.5)
         slopes[:, cols] = slope.astype(BF16)
-        if part == 0:
-            gate_qry[:, :feature] = act.astype(BF16)
-        elif part == 1:
-            split_heads(act, vm, every)
-        elif part == 2:
-            gate_qry[:, feature:] = (act.astype(BF16) * 0.0625).astype(BF16)
-        else:
-            split_heads(act, km, every)
+        act = act.astype(BF16)
+        acts[:, cols] = (act * 0.0625).astype(BF16) if part == 2 else act
 
 
 def fetch(pairs, sems):
@@ -141,35 +143,36 @@
     w_proj,
     w_out,
     g_tgt,
-    km_in,
-    vm_in,
+    acts_in,
     out_tgt,
     d_tgt,
     dk_t,
     dv_t,
     tgt_t,
     d_pre,
-    km,
-    vm,
+    k_s,
+    v_s,
     sems,
-    gate_s,
-    q_s,
-    km_own,
-    vm_own,
+    acts,
     w_s,
     s_s,
     bias_s,
+    own_bias,
     a_acc,
     dq_acc,
-    da_s,
+    q_st,
+    da_st,
+    q_t,
     da_t,
-    q_t,
     dk_own,
     dv_own,
 ):
-    copies = fetch([(km_in, km), (vm_in, vm)], sems)
-    tgt_rows, feature = out_tgt.shape
-    blocks = km.shape[1] // BLK
+    feature = out_tgt.shape[1]
+    copies = fetch(
+        [(acts_in.at[:, 3 * feature :], k_s), (acts_in.at[:, feature : 2 * feature], v_s)], sems
+    )
+    tgt_rows = out_tgt.shape[0]
+    blocks = k_s.shape[0] // BLK
     every = slice(0, tgt_rows)
     part_cols = [slice(part * feature, (part + 1) * feature) for part in range(4)]
     col = lax.broadcasted_iota(jnp.int32, (1, cand.shape[0]), 1)
@@ -182,14 +185,13 @@
         half = mm(normed, w_proj[:, part_cols[part]]) * 0.5
         act, slope = silu_parts(half)
         d_pre[:, part_cols[part]] = slope.astype(BF16)
-        if part == 0:
-            gate_s[...] = act.astype(BF16)
-        elif part == 1:
-            split_heads(act, vm_own, every)
-        elif part == 2:
-            q_s[...] = (act.astype(BF16) * 0.0625).astype(BF16)
-        else:
-            split_heads(act, km_own, every)
+        act = act.astype(BF16)
+        acts[:, part_cols[part]] = (act * 0.0625).astype(BF16) if part == 2 else act
+    qry = acts[:, part_cols[2]].astype(F32)
+    q_t[...] = jnp.zeros_like(q_t)
+    da_t[...] = jnp.zeros_like(da_t)
+    stack_heads(qry, q_st, tgt_rows)
+    stack_columns(qry.T, q_t, tgt_rows)
 
     a_acc[...] = jnp.zeros_like(a_acc)
     dq_acc[...] = jnp.zeros_like(dq_acc)
@@ -202,41 +204,35 @@
 
     def fwd(j, c):
         k0 = pl.multiple_of(j * BLK, BLK)
-        keys = pl.ds(k0, BLK)
         bias_s[...] = score_bias(lo[...], hi[...], k0)
-        forward(q_s, every, tgt_rows, km, vm, keys, BLK, w_s, s_s, j, bias_s, a_acc)
+        forward(q_st, k_s, v_s, pl.ds(k0, BLK), w_s, s_s, j, bias_s, a_acc)
         return c
 
     def bwd(j, c):
         keys = pl.ds(pl.multiple_of(j * BLK, BLK), BLK)
-        backward(
-            tgt_rows, km, vm, keys, BLK, w_s, s_s, j, da_s, da_t, q_t, dq_acc, dk_t, dv_t
-        )
+        backward(q_t, k_s, v_s, keys, BLK, w_s, s_s, j, da_st, da_t, dq_acc, dk_t, dv_t)
         return c
 
     lax.fori_loop(0, blocks, fwd, 0)
     same = lax.broadcasted_iota(jnp.int32, (tgt_rows, tgt_rows), 0) == lax.broadcasted_iota(
         jnp.int32, (tgt_rows, tgt_rows), 1
     )
-    bias_s[:, :tgt_rows] = jnp.where(same, 0.0, MASKED).astype(F32)
-    forward(
-        q_s, every, tgt_rows, km_own, vm_own, every, tgt_rows, w_s, s_s, blocks, bias_s, a_acc
-    )
-    out, mixed, d_gate, d_att = middle(
-        a_acc[...], x, gate_s[...].astype(F32), g_tgt[...], w_out[...]
-    )
+    own_bias[...] = jnp.where(same, 0.0, MASKED).astype(F32)
+    k_own, v_own = acts.at[:, part_cols[3]], acts.at[:, part_cols[1]]
+    forward(q_st, k_own, v_own, every, w_s, s_s, blocks, own_bias, a_acc)
+    gate = acts[:, part_cols[0]].astype(F32)
+    out, mixed, d_gate, d_att = middle(merge_heads(a_acc, tgt_rows), x, gate, g_tgt[...], w_out[...])
     out_tgt[...] = out
     tgt_t[1] = mixed.T.astype(BF16)
     d_pre[:, part_cols[0]] = (d_gate * d_pre[:, part_cols[0]].astype(F32)).astype(BF16)
-    da_s[...] = d_att.astype(BF16)
-    da_t[...] = d_att.T.astype(BF16)
-    q_t[...] = q_s[...].astype(F32).T.astype(BF16)
+    stack_heads(d_att, da_st, tgt_rows)
+    stack_columns(d_att.T, da_t, tgt_rows)
     lax.fori_loop(0, blocks, bwd, 0)
     backward(
-        tgt_rows, km_own, vm_own, every, tgt_rows, w_s, s_s, blocks,
-        da_s, da_t, q_t, dq_acc, dk_own, dv_own,
-    )
-    grads = (None, dv_own[...].T, dq_acc[...] * 0.125, dk_own[...].T * 2.0)
+        q_t, k_own, v_own, every, tgt_rows, w_s, s_s, blocks, da_st, da_t, dq_acc, dk_own, dv_own
+    )
+    d_q = merge_heads(dq_acc, tgt_rows) * 0.125
+    grads = (None, dv_own[...].T, d_q, dk_own[...].T * 2.0)
     for part in (1, 2, 3):
         d_part = grads[part] * d_pre[:, part_cols[part]].astype(F32)
         d_pre[:, part_cols[part]] = d_part.astype(BF16)
@@ -265,9 +261,7 @@
     g_tgt,
     tgt_t,
     tgt_pre,
-    gate_qry_in,
-    km_in,
-    vm_in,
+    acts_in,
     x_in,
     slopes_in,
     dv_in,
@@ -277,9 +271,7 @@
     keep,
     give,
     d_pre_o,
-    gate_qry,
-    km,
-    vm,
+    acts,
     x_s,
     d_pre,
     dv_t,
@@ -292,15 +284,20 @@
     bias_s,
     a_acc,
     dq_acc,
-    da_s,
+    q_st,
+    da_st,
+    q_t,
     da_t,
-    q_t,
 ):
+    hist_rows, feature = out_hist.shape
+    blocks = hist_rows // BLK
+    part_cols = [slice(part * feature, (part + 1) * feature) for part in range(4)]
+    later = slice(2 * feature, 4 * feature)
     copies = fetch(
         [
-            (gate_qry_in, gate_qry),
-            (km_in, km),
-            (vm_in, vm),
+            (acts_in.at[:, later], acts.at[:, later]),
+            (acts_in.at[:, part_cols[1]], acts.at[:, part_cols[1]]),
+            (acts_in.at[:, part_cols[0]], acts.at[:, part_cols[0]]),
             (x_in, x_s),
             (slopes_in, d_pre),
             (dv_in, dv_t),
@@ -309,12 +306,10 @@
         ],
         sems,
     )
-    hist_rows, feature = out_hist.shape
-    blocks = hist_rows // BLK
-    part_cols = [slice(part * feature, (part + 1) * feature) for part in range(4)]
-    qry = slice(feature, 2 * feature)
-    q_ref = gate_qry.at[:, qry]
-    for copy in copies[:3]:
+    k_ref, v_ref = acts.at[:, part_cols[3]], acts.at[:, part_cols[1]]
+    q_t[...] = jnp.zeros_like(q_t)
+    da_t[...] = jnp.zeros_like(da_t)
+    for copy in copies[:2]:
         copy.wait()
 
     def hist_block(i, carry):
@@ -324,42 +319,42 @@
         a_acc[...] = jnp.zeros_like(a_acc)
         dq_acc[...] = jnp.zeros_like(dq_acc)
 
+        qry = acts[rows, part_cols[2]].astype(F32)
+        stack_heads(qry, q_st, BLK)
+        stack_columns(qry.T, q_t, BLK)
+
         def fwd(j, c):
             k0 = pl.multiple_of(j * BLK, BLK)
-            keys = pl.ds(k0, BLK)
             bias_s[...] = score_bias(lo[rows, :], hi[rows, :], k0)
-            forward(q_ref, rows, BLK, km, vm, keys, BLK, w_s, s_s, j, bias_s, a_acc)
+            forward(q_st, k_ref, v_ref, pl.ds(k0, BLK), w_s, s_s, j, bias_s, a_acc)
             return c
 
         def bwd(j, c):
             keys = pl.ds(pl.multiple_of(j * BLK, BLK), BLK)
-            backward(
-                BLK, km, vm, keys, BLK, w_s, s_s, j, da_s, da_t, q_t, dq_acc, dk_t, dv_t
-            )
+            backward(q_t, k_ref, v_ref, keys, BLK, w_s, s_s, j, da_st, da_t, dq_acc, dk_t, dv_t)
             return c
 
         lax.fori_loop(first, i + 1, fwd, 0)
 
         @pl.when(i == 0)
         def _():
-            for copy in copies[3:]:
+            for copy in copies[2:]:
                 copy.wait()
 
         out, mixed, d_gate, d_att = middle(
-            a_acc[...],
+            merge_heads(a_acc, BLK),
             x_s[rows, :].astype(F32),
-            gate_qry[rows, :feature].astype(F32),
+            acts[rows, part_cols[0]].astype(F32),
             g_hist[rows, :],
             w_out[...],
         )
         out_hist[rows, :] = out
         mixed_t[:, rows] = mixed.T.astype(BF16)
         d_pre[rows, part_cols[0]] = (d_gate * d_pre[rows, part_cols[0]].astype(F32)).astype(BF16)
-        da_s[...] = d_att.astype(BF16)
-        da_t[...] = d_att.T.astype(BF16)
-        q_t[...] = gate_qry[rows, qry].astype(F32).T.astype(BF16)
+        stack_heads(d_att, da_st, BLK)
+        stack_columns(d_att.T, da_t, BLK)
         lax.fori_loop(first, i + 1, bwd, 0)
-        d_q = dq_acc[...] * 0.125 * d_pre[rows, part_cols[2]].astype(F32)
+        d_q = merge_heads(dq_acc, BLK) * 0.125 * d_pre[rows, part_cols[2]].astype(F32)
         d_pre[rows, part_cols[2]] = d_q.astype(BF16)
         return carry
 
@@ -449,16 +444,21 @@
 
 
 def sums_kernel(pieces, d_proj, d_out):
-    quarter, feature = d_out.shape
-    for part in range(5):
-        for group, source_cols, cols in segments(part, feature):
-            piece = pieces[0, :, group, :, source_cols].astype(F32)
-            piece = piece.reshape(quarter, cols.stop - cols.start)
-            if part < 4:
-                base = part * feature
-                d_proj[:, base + cols.start : base + cols.stop] = piece
-            else:
-                d_out[:, cols] = piece
+    feature = d_out.shape[1]
+    quarter = d_out.shape[0] // 8
+    for level in range(4):
+        for core in range(2):
+            first = (core * 4 + level) * quarter
+            rows = slice(first, first + quarter)
+            for part in range(5):
+                for group, source_cols, cols in segments(part, feature):
+                    piece = pieces[level * 2 + core, :, group, :, source_cols].astype(F32)
+                    piece = piece.reshape(quarter, cols.stop - cols.start)
+                    if part < 4:
+                        base = part * feature
+                        d_proj[rows, base + cols.start : base + cols.stop] = piece
+                    else:
+                        d_out[rows, cols] = piece
 
 
 VMEM = pl.BlockSpec(memory_space=pltpu.VMEM)
@@ -505,8 +505,7 @@
     def whole(*shape):
         return pl.BlockSpec(shape, lambda i: (0,) * len(shape))
 
-    per_head = pl.BlockSpec((HEADS, BLK, 128), lambda i: (0, i, 0))
-    x_hist, normed, rstd, normed_t, gate_qry, km, vm, slopes = pl.pallas_call(
+    x_hist, normed, rstd, normed_t, acts, slopes = pl.pallas_call(
         project_kernel,
         grid=(blocks,),
         out_shape=(
@@ -514,9 +513,7 @@
             sds((hist_rows, feature), BF16),
             sds((hist_rows, 1), F32),
             sds((feature, hist_rows), BF16),
-            sds((hist_rows, 2 * feature), BF16),
-            sds((HEADS, hist_rows, 128), BF16),
-            sds((HEADS, hist_rows, 128), BF16),
+            sds((hist_rows, 4 * feature), BF16),
             sds((hist_rows, 4 * feature), BF16),
         ),
         in_specs=[whole(slots, feature), whole(1, slots), whole(feature, 4 * feature)],
@@ -525,9 +522,7 @@
             by_rows(feature),
             by_rows(1),
             pl.BlockSpec((feature, BLK), lambda i: (0, i)),
-            by_rows(2 * feature),
-            per_head,
-            per_head,
+            by_rows(4 * feature),
             by_rows(4 * feature),
         ),
         compiler_params=params(56),
@@ -546,24 +541,23 @@
             sds((2, feature, tgt_rows), BF16),
             sds((tgt_rows, 4 * feature), BF16),
         ),
-        in_specs=[VMEM] * 8 + [ANY] * 2,
+        in_specs=[VMEM] * 8 + [ANY],
         out_specs=(VMEM,) * 6,
         scratch_shapes=[
-            scratch((HEADS, hist_rows, 128), BF16),
-            scratch((HEADS, hist_rows, 128), BF16),
+            scratch((hist_rows, feature), BF16),
+            scratch((hist_rows, feature), BF16),
             pltpu.SemaphoreType.DMA((2,)),
-            scratch((tgt_rows, feature), BF16),
-            scratch((tgt_rows, feature), BF16),
-            scratch((HEADS, tgt_rows, 128), BF16),
-            scratch((HEADS, tgt_rows, 128), BF16),
-            scratch((blocks + 1, HEADS, tgt_rows, BLK), BF16),
-            scratch((blocks + 1, HEADS, tgt_rows, BLK), BF16),
+            scratch((tgt_rows, 4 * feature), BF16),
+            scratch((blocks + 1, PAIRS, 2 * tgt_rows, BLK), BF16),
+            scratch((blocks + 1, PAIRS, 2 * tgt_rows, BLK), BF16),
             scratch((tgt_rows, BLK), F32),
-            scratch((tgt_rows, feature), F32),
-            scratch((tgt_rows, feature), F32),
-            scratch((tgt_rows, feature), BF16),
-            scratch((feature, tgt_rows), BF16),
-            scratch((feature, tgt_rows), BF16),
+            scratch((tgt_rows, tgt_rows), F32),
+            scratch((PAIRS, 2 * tgt_rows, 128), F32),
+            scratch((PAIRS, 2 * tgt_rows, 128), F32),
+            scratch((PAIRS, 2 * tgt_rows, 128), BF16),
+            scratch((PAIRS, 2 * tgt_rows, 128), BF16),
+            scratch((PAIRS, 128, 2 * tgt_rows), BF16),
+            scratch((PAIRS, 128, 2 * tgt_rows), BF16),
             scratch((feature, tgt_rows), F32),
             scratch((feature, tgt_rows), F32),
         ],
@@ -579,8 +573,7 @@
         w_proj,
         w_out,
         g_tgt,
-        km,
-        vm,
+        acts,
     )
     tgt_grads = lax.all_gather(d_tgt, "mem", axis=0, tiled=False)
 
@@ -593,12 +586,10 @@
             sds(pieces, BF16),
             sds((hist_rows, 4 * feature), BF16),
         ),
-        in_specs=[SMEM] * 2 + [VMEM] * 7 + [ANY] * 8,
+        in_specs=[SMEM] * 2 + [VMEM] * 7 + [ANY] * 6,
         out_specs=(VMEM, VMEM, VMEM, ANY),
         scratch_shapes=[
-            scratch((hist_rows, 2 * feature), BF16),
-            scratch((HEADS, hist_rows, 128), BF16),
-            scratch((HEADS, hist_rows, 128), BF16),
+            scratch((hist_rows, 4 * feature), BF16),
             scratch((hist_rows, feature), BF16),
             scratch((hist_rows, 4 * feature), BF16),
             scratch((feature, hist_rows), F32),
@@ -606,14 +597,15 @@
             scratch((feature, hist_rows), BF16),
             scratch((feature, hist_rows), BF16),
             pltpu.SemaphoreType.DMA((9,)),
-            scratch((blocks, HEADS, BLK, BLK), BF16),
-            scratch((blocks, HEADS, BLK, BLK), BF16),
+            scratch((blocks, PAIRS, 2 * BLK, BLK), BF16),
+            scratch((blocks, PAIRS, 2 * BLK, BLK), BF16),
             scratch((BLK, BLK), F32),
-            scratch((BLK, feature), F32),
-            scratch((BLK, feature), F32),
-            scratch((BLK, feature), BF16),
-            scratch((feature, BLK), BF16),
-            scratch((feature, BLK), BF16),
+            scratch((PAIRS, 2 * BLK, 128), F32),
+            scratch((PAIRS, 2 * BLK, 128), F32),
+            scratch((PAIRS, 2 * BLK, 128), BF16),
+            scratch((PAIRS, 2 * BLK, 128), BF16),
+            scratch((PAIRS, 128, 2 * BLK), BF16),
+            scratch((PAIRS, 128, 2 * BLK), BF16),
         ],
         compiler_params=params(56),
         cost_estimate=cost(18 << 30, 24 << 20),
@@ -628,9 +620,7 @@
         g_tgt,
         tgt_t,
         tgt_pre,
-        gate_qry,
-        km,
-        vm,
+        acts,
         x_hist,
         slopes,
         dv_t,
@@ -677,13 +667,9 @@
     sum_proj, sum_out = pl.pallas_call(
         sums_kernel,
         out_shape=(sds(w_proj.shape, F32), sds(w_out.shape, F32)),
-        grid=(2, 4),
-        in_specs=[pl.BlockSpec((1, 4, 4, 16, 640), lambda c, z: (2 * z + c, 0, 0, 0, 0))],
-        out_specs=(
-            pl.BlockSpec((64, 4 * feature), lambda c, z: (4 * c + z, 0)),
-            pl.BlockSpec((64, feature), lambda c, z: (4 * c + z, 0)),
-        ),
-        compiler_params=params(56),
+        in_specs=[VMEM],
+        out_specs=(VMEM, VMEM),
+        compiler_params=params(16),
         name="sums",
     )(everything.reshape(8, 4, 4, 16, 640))
 

time: 243 us -> 228 us (0.938)
  Pallas kernels: 100 us -> 83.3 us
    pallas_call x1, Pallas kernels: 42.6 us -> 35.5 us  [local(): pl.pallas_call(hist_kernel, out_shape=(sds((hist_rows, feature), BF16), s...]
    pallas_call x1, Pallas kernels: 20.2 us -> 14.6 us  [local(): pl.pallas_call(tgt_kernel, out_shape=(sds((tgt_rows, feature), BF16), sds...]
    pallas_call x1, Pallas kernels: 6.28 us -> 2.69 us  [local(): pl.pallas_call(sums_kernel, out_shape=(sds(w_proj.shape, F32), sds(w_out....]
    unnamed x12 -> x14, local copies, waits for them, and re-layouts: 3.8 us -> 5.54 us
  transfers between devices with their start and end apart: 7 -> 7, of which waited for: 6 -> 6; matrix products, arithmetic and copies ran while one was open for 4% -> 5% of each run, Pallas kernels for 30% -> 29%
where the time goes in v4:
time: 228 us; the launch traced here: 227 us
  Pallas kernels  83.3 us (37%)
  waiting for transfers between devices  74.1 us (32%)
  starting transfers between devices  27.9 us (12%)
  between operations  13.9 us (6%)
  local copies, waits for them, and re-layouts  12.6 us (6%)
  blocking collectives  11.9 us (5%)
  other arithmetic  3.65 us (2%)
    pallas_call x1, Pallas kernels, local(): pl.pallas_call(hist_kernel, out_shape=(sds((hist_rows, feature), BF16), s...  35.5 us
    all_to_all x1, waiting for transfers between devices, local(): lax.all_to_all(slot_grads.reshape(peers, 1, capacity, feature), BOTH, spl...  29.9 us
    all_to_all x1, waiting for transfers between devices, local(): lax.all_to_all(send_rows, BOTH, split_axis=1, concat_axis=0, tiled=True)  26.1 us
    pallas_call x1, Pallas kernels, local(): pl.pallas_call(tgt_kernel, out_shape=(sds((tgt_rows, feature), BF16), sds...  14.6 us
    pallas_call x1, Pallas kernels, local(): pl.pallas_call(rows_kernel, out_shape=sds((slots, feature), BF16), in_spe...  12.9 us
    pallas_call x1, Pallas kernels, local(): pl.pallas_call(project_kernel, grid=(blocks,), out_shape=(sds((hist_rows,...  12.2 us
    all_to_all x1, blocking collectives, local(): lax.all_to_all(copies.reshape(16, 1, 16, 640), 'mem', split_axis=0, conca...  11.9 us
    all_to_all x1, starting transfers between devices, local(): lax.all_to_all(send_rows, BOTH, split_axis=1, concat_axis=0, tiled=True)  11.5 us
  transfers between devices with their start and end apart: 7, of which 6 were waited for; matrix products, arithmetic and copies ran while one was open for 5% of the time, Pallas kernels for 29%

profile of v4, /device:TPU:1, one launch (start us, length us, event | category | flops | bytes accessed | tf_op | source)
XLA Modules:
  0.0 227.2 jit_solution(629246051767979370)
XLA Ops:
  7.2 0.7 all-gather.5.cloned.1.call-update
  7.9 11.5 %all-to-all-start = ((bf16[1,128,16,512]{3,2,0,1:T(8,128)(2,1)}), bf16[1,128,16,512]{3,2,0,1:T(8,128)(2,1)S(1)}, u32[]{:S(2)}, u32[]{:S(2)}) async-start(bf16[1,128,16,512]{3,2,0,1:T(8,128)(2,1)} %bitcast.35), calls=%async_computation | async-start | bytes 4194304 | tf_op jit(solution)/shard_map/all_to_all | solution.py:486
  19.5 0.7 reshape.85.tid_col
  20.2 0.6 reshape.73.tid_row
  20.9 0.7 reshape.76.pos_row
  21.9 0.7 broadcast_in_dim_reshape.8.lo
  22.7 0.7 broadcast_in_dim_reshape.9.hi
  23.6 1.0 copy.43.lo
  24.6 0.6 and_select_fusion.first_ref
  25.2 26.1 %all-to-all-done = bf16[1,128,16,512]{3,2,0,1:T(8,128)(2,1)S(1)} async-done(((bf16[1,128,16,512]{3,2,0,1:T(8,128)(2,1)}), bf16[1,128,16,512]{3,2,0,1:T(8,128)(2,1)S(1)}, u32[]{:S(2)}, u32[]{:S(2)}) %all-to-all-start) | async-done | bytes 2097184 | tf_op jit(solution)/shard_map/all_to_all | solution.py:486
  51.3 1.3 copy-done.2
  52.6 12.2 %project.1 = (bf16[1024,512]{1,0:T(8,128)(2,1)}, bf16[1024,512]{1,0:T(8,128)(2,1)}, f32[1024,1]{1,0:T(8,128)}, bf16[512,1024]{1,0:T(8,128)(2,1)}, bf16[1024,2048...) custom-call(bf16[2048,512]{1,0:T(8,128)(2,1)} %bitcast.36, s32[1,2048]{1,0:T(1,128)} %reshape.76.pos_row, bf16[512,2048]{1,0:T(8,128)(2,1)} %w_proj.5), custom_call_target="tpu_custom_call" | custom-call | flops 5368709120 | bytes 20971520 | tf_op jit(solution)/shard_map/project/pallas_call | solution.py:508
  64.8 2.5 %all-gather.5.cloned.1.call-done.cand = bf16[2048,512]{1,0:T(8,128)(2,1)} async-done(((bf16[128,512]{1,0:T(8,128)(2,1)}), bf16[2048,512]{1,0:T(8,128)(2,1)}) %all-gather.5.cloned.1.call-update) | async-done | bytes 2097168 | tf_op jit(solution)/shard_map/all_gather | solution.py:485
  67.3 14.6 %tgt.1 = (bf16[128,512]{1,0:T(8,128)(2,1)}, bf16[144,512]{1,0:T(8,128)(2,1)}, f32[512,1024]{1,0:T(8,128)}, f32[512,1024]{1,0:T(8,128)}, bf16[2,512,128]{2,1,0:T(8,128)(2,1)}, /*index=5*/bf16[128,2048]{1,0:T(8,128)(2,1)}) custom-call(bf16[2048,512]{1,0:T(8,128)(2,1)} %all-gather.5.cloned.1.call-done.cand, s32[128,1]{1,0:T(8,128)} %reshape.85.tid_col, ...), custom_call_target="tpu_custom_call" | custom-call | flops 6442450944 | bytes 16777216 | tf_op jit(solution)/shard_map/tgt/pallas_call | solution.py:534
  82.0 0.8 iota.6.hi
  82.8 35.5 %hist.1 = (bf16[1024,512]{1,0:T(8,128)(2,1)}, bf16[16,4,16,640]{3,2,1,0:T(8,128)(2,1)}, bf16[16,4,16,640]{3,2,1,0:T(8,128)(2,1)}, bf16[1024,2048]{1,0:T(8,128)(2,1)}) custom-call(s32[1]{0:T(128)} %bitcast.core_ref, s32[4]{0:T(128)} %and_select_fusion.first_ref, s32[1024,1]{1,0:T(8,128)} %copy.43.lo, s32[1024,1]{1,0:T(8,128)} %iota.6.hi, ...), custom_call_target="tpu_custom_call" | custom-call | flops 19327352832 | bytes 25165824 | tf_op jit(solution)/shard_map/hist/pallas_call | solution.py:581
  118.5 3.2 %collective-permute-done = bf16[16,4,16,640]{3,2,1,0:T(8,128)(2,1)S(1)} collective-permute-done((bf16[16,4,16,640]{3,2,1,0:T(8,128)(2,1)}, bf16[16,4,16,640]{3,2,1,0:T(8,128)(2,1)S(1)}, u32[]{:S(2)}, u32[]{:S(2)}) %collective-permute-start) | collective-permute-done | bytes 1310752 | tf_op jit(solution)/shard_map/ppermute | solution.py:631
  121.7 2.8 %add_convert_fusion = bf16[16,4,16,640]{3,2,1,0:T(8,128)(2,1)} fusion(bf16[16,4,16,640]{3,2,1,0:T(8,128)(2,1)S(1)} %collective-permute-done, bf16[16,4,16,640]{3,2,1,0:T(8,128)(2,1)} %get-tuple-element.38), kind=kLoop, calls=%fused_computation | loop fusion | flops 2621440 | bytes 3932160 | tf_op jit(solution)/shard_map/convert_element_type | solution.py:632
  124.5 9.3 %all-to-all-start.2 = ((bf16[64,1,16,640]{3,2,1,0:T(8,128)(2,1)}), bf16[64,1,16,640]{3,2,1,0:T(8,128)(2,1)S(1)}, u32[]{:S(2)}, u32[]{:S(2)}) async-start(bf16[64,1,16,640]{3,2,1,0:T(8,128)(2,1)} %bitcast.15), calls=%async_computation.2 | async-start | bytes 2621440 | tf_op jit(solution)/shard_map/all_to_all | solution.py:634
  133.8 1.6 reshape.86.pos_col
  135.4 12.9 %rows.1.slot_grads = bf16[2048,512]{1,0:T(8,128)(2,1)} custom-call(bf16[1024,2048]{1,0:T(8,128)(2,1)} %get-tuple-element.34.d_pre, bf16[512,2048]{1,0:T(8,128)(2,1)} %w_proj.5, bf16[1024,512]{1,0:T(8,128)(2,1)} %get-tuple-element.35.normed, f32[1024,1]{1,0:T(8,128)} %get-tuple-element.36.rstd, bf16[1024,512]{1,0:T(8,128)(2,1)} %g_hist.3, ...), custom_call_target="tpu_custom_call" | custom-call | flops 5368709120 | bytes 16777216 | tf_op jit(solution)/shard_map/rows/pallas_call | solution.py:637
  148.3 5.6 %all-to-all-done.2 = bf16[64,1,16,640]{3,2,1,0:T(8,128)(2,1)S(1)} async-done(((bf16[64,1,16,640]{3,2,1,0:T(8,128)(2,1)}), bf16[64,1,16,640]{3,2,1,0:T(8,128)(2,1)S(1)}, u32[]{:S(2)}, u32[]{:S(2)}) %all-to-all-start.2) | async-done | bytes 1310752 | tf_op jit(solution)/shard_map/all_to_all | solution.py:634
  153.9 1.1 copy-done.1
  155.0 2.2 reduce.1
  157.2 11.9 %all_to_all.19 = bf16[16,1,16,640]{3,2,1,0:T(8,128)(2,1)} all-to-all(bf16[16,1,16,640]{3,2,1,0:T(8,128)(2,1)} %bitcast.37), channel_id=1, replica_groups=mesh['grp'=8,'mem'=16] {'mem'}, dimensions={0} | all-to-all | bytes 655360 | tf_op jit(solution)/shard_map/all_to_all | solution.py:655
  169.1 6.9 %all-to-all-start.1 = ((bf16[128,1,16,512]{3,2,1,0:T(8,128)(2,1)}), bf16[128,1,16,512]{3,2,1,0:T(8,128)(2,1)S(1)}, u32[]{:S(2)}, u32[]{:S(2)}) async-start(bf16[128,1,16,512]{3,2,1,0:T(8,128)(2,1)} %bitcast.10), calls=%async_computation.1 | async-start | bytes 4194304 | tf_op jit(solution)/shard_map/all_to_all | solution.py:660
  176.0 29.9 %all-to-all-done.1 = bf16[128,1,16,512]{3,2,1,0:T(8,128)(2,1)S(1)} async-done(((bf16[128,1,16,512]{3,2,1,0:T(8,128)(2,1)}), bf16[128,1,16,512]{3,2,1,0:T(8,128)(2,1)S(1)}, u32[]{:S(2)}, u32[]{:S(2)}) %all-to-all-start.1) | async-done | bytes 2097184 | tf_op jit(solution)/shard_map/all_to_all | solution.py:660
  205.9 3.1 %cand.1 = f32[128,512]{1,0:T(8,128)} custom-call(s32[1]{0:T(128)} %bitcast.12.first_ref, bf16[16,144,512]{2,1,0:T(8,128)(2,1)} %bitcast.34), custom_call_target="tpu_custom_call" | custom-call | tf_op jit(solution)/shard_map/cand/pallas_call | solution.py:677
  209.0 6.0 %all-gather.7.cloned.1.call-done = bf16[2048,640]{1,0:T(8,128)(2,1)} async-done(((bf16[256,640]{1,0:T(8,128)(2,1)}), bf16[2048,640]{1,0:T(8,128)(2,1)}) %all-gather.7.cloned.1.call-update) | async-done | bytes 2621456 | tf_op jit(solution)/shard_map/all_gather | solution.py:658
  215.0 1.7 copy-done
  216.7 2.7 %sums.1 = (f32[512,2048]{1,0:T(8,128)}, f32[512,512]{1,0:T(8,128)}) custom-call(bf16[8,4,4,16,640]{4,3,2,1,0:T(8,128)(2,1)S(1)} %bitcast.31), custom_call_target="tpu_custom_call" | custom-call | tf_op jit(solution)/shard_map/sums/pallas_call | solution.py:667
  219.4 1.3 copy.50
  (24 shorter events, 0.9 us)
Async XLA Ops:
  7.2 60.2 %all-gather.5.cloned.1.call-start = ((), (), s32[]{:S(2)}) async-start(), calls=%async_computation.4 | async-start | bytes 2228224 | tf_op jit(solution)/shard_map/all_gather | solution.py:485
  7.9 11.6 %copy-start.3 = (s32[8,16]{1,0:T(8,128)S(1)}, s32[8,16]{1,0:T(8,128)}, u32[]{:S(2)}) copy-start(s32[8,16]{1,0:T(8,128)} %param.13) | copy-start | bytes 1540
  7.9 12.9 %copy-start.4 = (s32[1,128,16]{1,2,0:T(8,128)S(1)}, s32[1,128,16]{1,2,0:T(8,128)}, u32[]{:S(2)}) copy-start(s32[1,128,16]{1,2,0:T(8,128)} %param.10) | copy-start | bytes 24580
  7.9 13.7 %copy-start.5 = (s32[1,8]{1,0:T(1,128)S(1)}, s32[1,8]{1,0:T(1,128)}, u32[]{:S(2)}) copy-start(s32[1,8]{1,0:T(1,128)} %param.11) | copy-start | bytes 100
  7.9 43.4 %all-to-all-start = ((bf16[1,128,16,512]{3,2,0,1:T(8,128)(2,1)}), bf16[1,128,16,512]{3,2,0,1:T(8,128)(2,1)S(1)}, u32[]{:S(2)}, u32[]{:S(2)}) async-start(bf16[1,128,16,512]{3,2,0,1:T(8,128)(2,1)} %bitcast.35), calls=%async_computation | async-start | bytes 4194304 | tf_op jit(solution)/shard_map/all_to_all | solution.py:486
  19.4 186.5 %all-gather.9.cloned.1.call-start = ((), (), s32[]{:S(2)}) async-start(), calls=%async_computation.6 | async-start | bytes 2506752 | tf_op jit(solution)/shard_map/all_gather | solution.py:578
  51.3 1.3 copy-start.2
  118.4 3.3 %collective-permute-start = (bf16[16,4,16,640]{3,2,1,0:T(8,128)(2,1)}, bf16[16,4,16,640]{3,2,1,0:T(8,128)(2,1)S(1)}, u32[]{:S(2)}, u32[]{:S(2)}) collective-permute-start(bf16[16,4,16,640]{3,2,1,0:T(8,128)(2,1)} %get-tuple-element.39), channel_id=1, source_target_pairs={{0,16},{1,17},{2,18},{3,19},{4,20},{5,21},{6,22},{7,23},{8,24},{9,... | collective-permute-start | bytes 3932168 | tf_op jit(solution)/shard_map/ppermute | solution.py:631
  124.5 29.5 %all-to-all-start.2 = ((bf16[64,1,16,640]{3,2,1,0:T(8,128)(2,1)}), bf16[64,1,16,640]{3,2,1,0:T(8,128)(2,1)S(1)}, u32[]{:S(2)}, u32[]{:S(2)}) async-start(bf16[64,1,16,640]{3,2,1,0:T(8,128)(2,1)} %bitcast.15), calls=%async_computation.2 | async-start | bytes 2621440 | tf_op jit(solution)/shard_map/all_to_all | solution.py:634
  133.8 81.2 %all-gather.7.cloned.1.call-start = ((), (), s32[]{:S(2)}) async-start(), calls=%async_computation.5 | async-start | bytes 2949120 | tf_op jit(solution)/shard_map/all_gather | solution.py:658
  153.9 1.1 copy-start.1
  169.1 36.8 %all-to-all-start.1 = ((bf16[128,1,16,512]{3,2,1,0:T(8,128)(2,1)}), bf16[128,1,16,512]{3,2,1,0:T(8,128)(2,1)S(1)}, u32[]{:S(2)}, u32[]{:S(2)}) async-start(bf16[128,1,16,512]{3,2,1,0:T(8,128)(2,1)} %bitcast.10), calls=%async_computation.1 | async-start | bytes 4194304 | tf_op jit(solution)/shard_map/all_to_all | solution.py:660
  215.0 1.7 copy-start
Sparse Core Ops, SparseCore 0:
  10.1 57.1 all-gather.4
  82.1 44.8 all-gather.8
  169.2 45.6 all-gather.6

commit v5 on v4

--- a/solution.py
+++ b/solution.py
@@ -146,10 +146,12 @@
     acts_in,
     out_tgt,
     d_tgt,
+    dk_o,
+    dv_o,
+    tgt_t,
+    d_pre,
     dk_t,
     dv_t,
-    tgt_t,
-    d_pre,
     k_s,
     v_s,
     sems,
@@ -231,6 +233,8 @@
     backward(
         q_t, k_own, v_own, every, tgt_rows, w_s, s_s, blocks, da_st, da_t, dq_acc, dk_own, dv_own
     )
+    dk_o[...] = dk_t[...].astype(BF16)
+    dv_o[...] = dv_t[...].astype(BF16)
     d_q = merge_heads(dq_acc, tgt_rows) * 0.125
     grads = (None, dv_own[...].T, d_q, dk_own[...].T * 2.0)
     for part in (1, 2, 3):
@@ -254,8 +258,7 @@
 def hist_kernel(
     core_ref,
     first_ref,
-    lo,
-    hi,
+    starts_ref,
     w_out,
     g_hist,
     g_tgt,
@@ -274,10 +277,14 @@
     acts,
     x_s,
     d_pre,
+    dv_add,
+    dk_add,
     dv_t,
     dk_t,
     normed_t,
     mixed_t,
+    out_s,
+    give_s,
     sems,
     w_s,
     s_s,
@@ -289,19 +296,23 @@
     q_t,
     da_t,
 ):
-    hist_rows, feature = out_hist.shape
+    hist_rows, feature = g_hist.shape
     blocks = hist_rows // BLK
     part_cols = [slice(part * feature, (part + 1) * feature) for part in range(4)]
+    gates, vals, qrys, ids = part_cols
     later = slice(2 * feature, 4 * feature)
     copies = fetch(
         [
             (acts_in.at[:, later], acts.at[:, later]),
-            (acts_in.at[:, part_cols[1]], acts.at[:, part_cols[1]]),
-            (acts_in.at[:, part_cols[0]], acts.at[:, part_cols[0]]),
+            (acts_in.at[:, vals], acts.at[:, vals]),
+            (acts_in.at[:, gates], acts.at[:, gates]),
             (x_in, x_s),
-            (slopes_in, d_pre),
-            (dv_in, dv_t),
-            (dk_in, dk_t),
+            (slopes_in.at[:, gates], d_pre.at[:, gates]),
+            (slopes_in.at[:, qrys], d_pre.at[:, qrys]),
+            (slopes_in.at[:, vals], d_pre.at[:, vals]),
+            (slopes_in.at[:, ids], d_pre.at[:, ids]),
+            (dv_in, dv_add),
+            (dk_in, dk_add),
             (normed_t_in, normed_t),
         ],
         sems,
@@ -309,23 +320,29 @@
     k_ref, v_ref = acts.at[:, part_cols[3]], acts.at[:, part_cols[1]]
     q_t[...] = jnp.zeros_like(q_t)
     da_t[...] = jnp.zeros_like(da_t)
+    dk_t[...] = jnp.zeros_like(dk_t)
+    dv_t[...] = jnp.zeros_like(dv_t)
     for copy in copies[:2]:
         copy.wait()
 
-    def hist_block(i, carry):
+    def hist_block(n, carry):
+        i = blocks - 1 - n
         r0 = pl.multiple_of(i * BLK, BLK)
         rows = pl.ds(r0, BLK)
         first = first_ref[i]
+        row = r0 + lax.broadcasted_iota(jnp.int32, (BLK, 1), 0)
+        lo = jnp.zeros((BLK, 1), jnp.int32)
+        for user in range(starts_ref.shape[0]):
+            lo = jnp.where(row >= starts_ref[user], starts_ref[user], lo)
         a_acc[...] = jnp.zeros_like(a_acc)
         dq_acc[...] = jnp.zeros_like(dq_acc)
-
         qry = acts[rows, part_cols[2]].astype(F32)
         stack_heads(qry, q_st, BLK)
         stack_columns(qry.T, q_t, BLK)
 
         def fwd(j, c):
             k0 = pl.multiple_of(j * BLK, BLK)
-            bias_s[...] = score_bias(lo[rows, :], hi[rows, :], k0)
+            bias_s[...] = score_bias(lo, row, k0)
             forward(q_st, k_ref, v_ref, pl.ds(k0, BLK), w_s, s_s, j, bias_s, a_acc)
             return c
 
@@ -336,9 +353,9 @@
 
         lax.fori_loop(first, i + 1, fwd, 0)
 
-        @pl.when(i == 0)
+        @pl.when(n == 0)
         def _():
-            for copy in copies[2:]:
+            for copy in copies[2:5]:
                 copy.wait()
 
         out, mixed, d_gate, d_att = middle(
@@ -348,32 +365,43 @@
             g_hist[rows, :],
             w_out[...],
         )
-        out_hist[rows, :] = out
+        out_s[rows, :] = out
         mixed_t[:, rows] = mixed.T.astype(BF16)
         d_pre[rows, part_cols[0]] = (d_gate * d_pre[rows, part_cols[0]].astype(F32)).astype(BF16)
         stack_heads(d_att, da_st, BLK)
         stack_columns(d_att.T, da_t, BLK)
         lax.fori_loop(first, i + 1, bwd, 0)
+
+        @pl.when(n == 0)
+        def _():
+            copies[5].wait()
+
         d_q = merge_heads(dq_acc, BLK) * 0.125 * d_pre[rows, part_cols[2]].astype(F32)
         d_pre[rows, part_cols[2]] = d_q.astype(BF16)
         return carry
 
     lax.fori_loop(0, blocks, hist_block, 0)
+    count = len(copies)
+    sent_out = pltpu.make_async_copy(out_s, out_hist, sems.at[count])
+    sent_out.start()
+    for copy in copies[6:]:
+        copy.wait()
 
     def spread(i, carry):
         rows = pl.ds(pl.multiple_of(i * BLK, BLK), BLK)
         vals, keys = part_cols[1], part_cols[3]
-        d_pre[rows, vals] = (dv_t[:, rows].T * d_pre[rows, vals].astype(F32)).astype(BF16)
-        d_pre[rows, keys] = (dk_t[:, rows].T * 2.0 * d_pre[rows, keys].astype(F32)).astype(BF16)
+        d_pre[rows, vals] = ((dv_t[:, rows] + dv_add[:, rows].astype(F32)).T * d_pre[rows, vals].astype(F32)).astype(BF16)
+        d_pre[rows, keys] = ((dk_t[:, rows] + dk_add[:, rows].astype(F32)).T * 2.0 * d_pre[rows, keys].astype(F32)).astype(BF16)
         return carry
 
     lax.fori_loop(0, blocks, spread, 0)
-    sent = pltpu.make_async_copy(d_pre, d_pre_o, sems.at[len(copies)])
+    sent = pltpu.make_async_copy(d_pre, d_pre_o, sems.at[count + 1])
     sent.start()
 
     core = core_ref[0]
     half_rows = feature // 2
-    for dest, half in ((give, 1 - core), (keep, core)):
+    sent_give = pltpu.make_async_copy(give_s, give, sems.at[count + 2])
+    for dest, half in ((give_s, 1 - core), (keep, core)):
         rows = pl.ds(pl.multiple_of(half * half_rows, half_rows), half_rows)
         for part in range(5):
             if part < 4:
@@ -384,7 +412,11 @@
             for group, dest_cols, cols in segments(part, feature):
                 piece = total[:, cols].reshape(16, 16, cols.stop - cols.start)
                 dest[:, group, :, dest_cols] = piece.astype(BF16)
+        if dest is give_s:
+            sent_give.start()
+    sent_out.wait()
     sent.wait()
+    sent_give.wait()
 
 
 def segments(part, feature):
@@ -490,9 +522,9 @@
     pos_col = slot_pos.reshape(slots, 1)
     ends = jnp.cumsum(lengths[0])
     starts = ends - lengths[0]
-    row = jnp.arange(hist_rows, dtype=jnp.int32)[:, None]
-    hist_lo = jnp.max(jnp.where(row >= starts[None, :], starts[None, :], 0), axis=1)
-    first = (hist_lo[::BLK] // BLK).astype(jnp.int32)
+    row = jnp.arange(0, hist_rows, BLK, dtype=jnp.int32)[:, None]
+    first = jnp.max(jnp.where(row >= starts[None, :], starts[None, :], 0), axis=1) // BLK
+    first = first.astype(jnp.int32)
     tgt_lo = jnp.repeat(starts, each).astype(jnp.int32)[:, None]
     tgt_hi = jnp.repeat(ends - 1, each).astype(jnp.int32)[:, None]
     core = lax.rem(lax.axis_index("grp"), 2).astype(jnp.int32)[None]
@@ -536,14 +568,16 @@
         out_shape=(
             sds((tgt_rows, feature), BF16),
             sds((tgt_rows + 16, feature), BF16),
-            sds((feature, hist_rows), F32),
-            sds((feature, hist_rows), F32),
+            sds((feature, hist_rows), BF16),
+            sds((feature, hist_rows), BF16),
             sds((2, feature, tgt_rows), BF16),
             sds((tgt_rows, 4 * feature), BF16),
         ),
         in_specs=[VMEM] * 8 + [ANY],
         out_specs=(VMEM,) * 6,
         scratch_shapes=[
+            scratch((feature, hist_rows), F32),
+            scratch((feature, hist_rows), F32),
             scratch((hist_rows, feature), BF16),
             scratch((hist_rows, feature), BF16),
             pltpu.SemaphoreType.DMA((2,)),
@@ -586,17 +620,21 @@
             sds(pieces, BF16),
             sds((hist_rows, 4 * feature), BF16),
         ),
-        in_specs=[SMEM] * 2 + [VMEM] * 7 + [ANY] * 6,
-        out_specs=(VMEM, VMEM, VMEM, ANY),
+        in_specs=[SMEM] * 3 + [VMEM] * 5 + [ANY] * 6,
+        out_specs=(ANY, VMEM, ANY, ANY),
         scratch_shapes=[
             scratch((hist_rows, 4 * feature), BF16),
             scratch((hist_rows, feature), BF16),
             scratch((hist_rows, 4 * feature), BF16),
+            scratch((feature, hist_rows), BF16),
+            scratch((feature, hist_rows), BF16),
             scratch((feature, hist_rows), F32),
             scratch((feature, hist_rows), F32),
             scratch((feature, hist_rows), BF16),
             scratch((feature, hist_rows), BF16),
-            pltpu.SemaphoreType.DMA((9,)),
+            scratch((hist_rows, feature), BF16),
+            scratch(pieces, BF16),
+            pltpu.SemaphoreType.DMA((14,)),
             scratch((blocks, PAIRS, 2 * BLK, BLK), BF16),
             scratch((blocks, PAIRS, 2 * BLK, BLK), BF16),
             scratch((BLK, BLK), F32),
@@ -613,8 +651,7 @@
     )(
         core,
         first,
-        hist_lo.astype(jnp.int32)[:, None],
-        row,
+        starts.astype(jnp.int32),
         w_out,
         g_hist,
         g_tgt,

time: 228 us -> 225 us (0.987)
  Pallas kernels: 83.3 us -> 80.9 us
    pallas_call x1, Pallas kernels: 35.5 us -> 32.9 us  [local(): pl.pallas_call(hist_kernel, out_shape=(sds((hist_rows, feature), BF16), s...]
    unnamed x14 -> x16, local copies, waits for them, and re-layouts: 5.54 us -> 5.55 us
  transfers between devices with their start and end apart: 7 -> 7, of which waited for: 6 -> 6; matrix products, arithmetic and copies ran while one was open for 5% -> 4% of each run, Pallas kernels for 29% -> 28%
where the time goes in v5:
time: 225 us; the launch traced here: 224 us
  Pallas kernels  80.9 us (36%)
  waiting for transfers between devices  74.9 us (33%)
  starting transfers between devices  28.1 us (12%)
  between operations  13.8 us (6%)
  blocking collectives  11.9 us (5%)
  local copies, waits for them, and re-layouts  10.7 us (5%)
  other arithmetic  3.79 us (2%)
    pallas_call x1, Pallas kernels, local(): pl.pallas_call(hist_kernel, out_shape=(sds((hist_rows, feature), BF16), s...  32.9 us
    all_to_all x1, waiting for transfers between devices, local(): lax.all_to_all(slot_grads.reshape(peers, 1, capacity, feature), BOTH, spl...  29.9 us
    all_to_all x1, waiting for transfers between devices, local(): lax.all_to_all(send_rows, BOTH, split_axis=1, concat_axis=0, tiled=True)  27.1 us
    pallas_call x1, Pallas kernels, local(): pl.pallas_call(tgt_kernel, out_shape=(sds((tgt_rows, feature), BF16), sds...  14.9 us
    pallas_call x1, Pallas kernels, local(): pl.pallas_call(rows_kernel, out_shape=sds((slots, feature), BF16), in_spe...  12.9 us
    pallas_call x1, Pallas kernels, local(): pl.pallas_call(project_kernel, grid=(blocks,), out_shape=(sds((hist_rows,...  12.2 us
    all_to_all x1, blocking collectives, local(): lax.all_to_all(copies.reshape(16, 1, 16, 640), 'mem', split_axis=0, conca...  11.9 us
    all_to_all x1, starting transfers between devices, local(): lax.all_to_all(send_rows, BOTH, split_axis=1, concat_axis=0, tiled=True)  11.5 us
  transfers between devices with their start and end apart: 7, of which 6 were waited for; matrix products, arithmetic and copies ran while one was open for 4% of the time, Pallas kernels for 28%

profile of v5, /device:TPU:1, one launch (start us, length us, event | category | flops | bytes accessed | tf_op | source)
XLA Modules:
  0.0 224.1 jit_solution(14404153251148061794)
XLA Ops:
  7.2 0.7 all-gather.5.cloned.1.call-update
  7.9 11.5 %all-to-all-start = ((bf16[1,128,16,512]{3,2,0,1:T(8,128)(2,1)}), bf16[1,128,16,512]{3,2,0,1:T(8,128)(2,1)S(1)}, u32[]{:S(2)}, u32[]{:S(2)}) async-start(bf16[1,128,16,512]{3,2,0,1:T(8,128)(2,1)} %bitcast.34), calls=%async_computation | async-start | bytes 4194304 | tf_op jit(solution)/shard_map/all_to_all | solution.py:518
  19.5 0.7 reshape.89.tid_col
  20.2 0.6 reshape.78.tid_row
  20.9 0.7 reshape.80.pos_row
  21.9 0.7 broadcast_in_dim_reshape.8.lo
  22.7 0.7 broadcast_in_dim_reshape.9.hi
  23.4 0.2 select_reduce_fusion
  23.6 0.6 and_select_fusion.first_ref
  24.2 27.1 %all-to-all-done = bf16[1,128,16,512]{3,2,0,1:T(8,128)(2,1)S(1)} async-done(((bf16[1,128,16,512]{3,2,0,1:T(8,128)(2,1)}), bf16[1,128,16,512]{3,2,0,1:T(8,128)(2,1)S(1)}, u32[]{:S(2)}, u32[]{:S(2)}) %all-to-all-start) | async-done | bytes 2097184 | tf_op jit(solution)/shard_map/all_to_all | solution.py:518
  51.3 1.3 copy-done.2
  52.6 12.2 %project.1 = (bf16[1024,512]{1,0:T(8,128)(2,1)}, bf16[1024,512]{1,0:T(8,128)(2,1)}, f32[1024,1]{1,0:T(8,128)}, bf16[512,1024]{1,0:T(8,128)(2,1)}, bf16[1024,2048...) custom-call(bf16[2048,512]{1,0:T(8,128)(2,1)} %bitcast.35, s32[1,2048]{1,0:T(1,128)} %reshape.80.pos_row, bf16[512,2048]{1,0:T(8,128)(2,1)} %w_proj.5), custom_call_target="tpu_custom_call" | custom-call | flops 5368709120 | bytes 20971520 | tf_op jit(solution)/shard_map/project/pallas_call | solution.py:540
  64.8 2.5 %all-gather.5.cloned.1.call-done.cand = bf16[2048,512]{1,0:T(8,128)(2,1)} async-done(((bf16[128,512]{1,0:T(8,128)(2,1)}), bf16[2048,512]{1,0:T(8,128)(2,1)}) %all-gather.5.cloned.1.call-update) | async-done | bytes 2097168 | tf_op jit(solution)/shard_map/all_gather | solution.py:517
  67.3 14.9 %tgt.1 = (bf16[128,512]{1,0:T(8,128)(2,1)}, bf16[144,512]{1,0:T(8,128)(2,1)}, bf16[512,1024]{1,0:T(8,128)(2,1)}, bf16[512,1024]{1,0:T(8,128)(2,1)}, bf16[2,512,1...) custom-call(bf16[2048,512]{1,0:T(8,128)(2,1)} %all-gather.5.cloned.1.call-done.cand, s32[128,1]{1,0:T(8,128)} %reshape.89.tid_col, ...), custom_call_target="tpu_custom_call" | custom-call | flops 6442450944 | bytes 16777216 | tf_op jit(solution)/shard_map/tgt/pallas_call | solution.py:566
  82.3 32.9 %hist.1 = (bf16[1024,512]{1,0:T(8,128)(2,1)}, bf16[16,4,16,640]{3,2,1,0:T(8,128)(2,1)}, bf16[16,4,16,640]{3,2,1,0:T(8,128)(2,1)}, bf16[1024,2048]{1,0:T(8,128)(2,1)}) custom-call(s32[1]{0:T(128)} %bitcast.core_ref, s32[4]{0:T(128)} %and_select_fusion.first_ref, s32[8]{0:T(128)} %copy-done.5, bf16[512,512]{1,0:T(8,128)(2,1)} %w_out.3, ...), custom_call_target="tpu_custom_call" | custom-call | flops 19327352832 | bytes 25165824 | tf_op jit(solution)/shard_map/hist/pallas_call | solution.py:615
  115.2 1.6 collective-permute-start
  116.7 2.9 %collective-permute-done = bf16[16,4,16,640]{3,2,1,0:T(8,128)(2,1)S(1)} collective-permute-done((bf16[16,4,16,640]{3,2,1,0:T(8,128)(2,1)}, bf16[16,4,16,640]{3,2,1,0:T(8,128)(2,1)S(1)}, u32[]{:S(2)}, u32[]{:S(2)}) %collective-permute-start) | collective-permute-done | bytes 1310752 | tf_op jit(solution)/shard_map/ppermute | solution.py:668
  119.6 2.8 %add_convert_fusion = bf16[16,4,16,640]{3,2,1,0:T(8,128)(2,1)} fusion(bf16[16,4,16,640]{3,2,1,0:T(8,128)(2,1)S(1)} %collective-permute-done, bf16[16,4,16,640]{3,2,1,0:T(8,128)(2,1)} %get-tuple-element.38), kind=kLoop, calls=%fused_computation | loop fusion | flops 2621440 | bytes 3932160 | tf_op jit(solution)/shard_map/convert_element_type | solution.py:669
  122.4 8.2 %all-to-all-start.2 = ((bf16[64,1,16,640]{3,2,1,0:T(8,128)(2,1)}), bf16[64,1,16,640]{3,2,1,0:T(8,128)(2,1)S(1)}, u32[]{:S(2)}, u32[]{:S(2)}) async-start(bf16[64,1,16,640]{3,2,1,0:T(8,128)(2,1)} %bitcast.14), calls=%async_computation.2 | async-start | bytes 2621440 | tf_op jit(solution)/shard_map/all_to_all | solution.py:671
  130.7 1.6 reshape.90.pos_col
  132.2 12.9 %rows.1.slot_grads = bf16[2048,512]{1,0:T(8,128)(2,1)} custom-call(bf16[1024,2048]{1,0:T(8,128)(2,1)} %get-tuple-element.34.d_pre, bf16[512,2048]{1,0:T(8,128)(2,1)} %w_proj.5, bf16[1024,512]{1,0:T(8,128)(2,1)} %get-tuple-element.35.normed, f32[1024,1]{1,0:T(8,128)} %get-tuple-element.36.rstd, bf16[1024,512]{1,0:T(8,128)(2,1)} %g_hist.3, ...), custom_call_target="tpu_custom_call" | custom-call | flops 5368709120 | bytes 16777216 | tf_op jit(solution)/shard_map/rows/pallas_call | solution.py:674
  145.1 5.7 %all-to-all-done.2 = bf16[64,1,16,640]{3,2,1,0:T(8,128)(2,1)S(1)} async-done(((bf16[64,1,16,640]{3,2,1,0:T(8,128)(2,1)}), bf16[64,1,16,640]{3,2,1,0:T(8,128)(2,1)S(1)}, u32[]{:S(2)}, u32[]{:S(2)}) %all-to-all-start.2) | async-done | bytes 1310752 | tf_op jit(solution)/shard_map/all_to_all | solution.py:671
  150.8 1.1 copy-done.1
  151.9 2.2 %reduce.1 = bf16[16,16,640]{2,1,0:T(8,128)(2,1)} custom-call(bf16[64,16,640]{2,1,0:T(8,128)(2,1)} %bitcast.32, bf16[2048,512]{1,0:T(8,128)(2,1)} %rows.1.slot_grads), custom_call_target="tpu_custom_call" | custom-call | tf_op jit(solution)/shard_map/reduce/pallas_call | solution.py:684
  154.2 11.9 %all_to_all.19 = bf16[16,1,16,640]{3,2,1,0:T(8,128)(2,1)} all-to-all(bf16[16,1,16,640]{3,2,1,0:T(8,128)(2,1)} %bitcast.36), channel_id=1, replica_groups=mesh['grp'=8,'mem'=16] {'mem'}, dimensions={0} | all-to-all | bytes 655360 | tf_op jit(solution)/shard_map/all_to_all | solution.py:692
  166.0 6.8 %all-to-all-start.1 = ((bf16[128,1,16,512]{3,2,1,0:T(8,128)(2,1)}), bf16[128,1,16,512]{3,2,1,0:T(8,128)(2,1)S(1)}, u32[]{:S(2)}, u32[]{:S(2)}) async-start(bf16[128,1,16,512]{3,2,1,0:T(8,128)(2,1)} %bitcast.9), calls=%async_computation.1 | async-start | bytes 4194304 | tf_op jit(solution)/shard_map/all_to_all | solution.py:697
  172.8 29.9 %all-to-all-done.1 = bf16[128,1,16,512]{3,2,1,0:T(8,128)(2,1)S(1)} async-done(((bf16[128,1,16,512]{3,2,1,0:T(8,128)(2,1)}), bf16[128,1,16,512]{3,2,1,0:T(8,128)(2,1)S(1)}, u32[]{:S(2)}, u32[]{:S(2)}) %all-to-all-start.1) | async-done | bytes 2097184 | tf_op jit(solution)/shard_map/all_to_all | solution.py:697
  202.7 3.1 %cand.1 = f32[128,512]{1,0:T(8,128)} custom-call(s32[1]{0:T(128)} %bitcast.11.first_ref, bf16[16,144,512]{2,1,0:T(8,128)(2,1)} %bitcast.33), custom_call_target="tpu_custom_call" | custom-call | tf_op jit(solution)/shard_map/cand/pallas_call | solution.py:714
  205.8 6.0 %all-gather.7.cloned.1.call-done = bf16[2048,640]{1,0:T(8,128)(2,1)} async-done(((bf16[256,640]{1,0:T(8,128)(2,1)}), bf16[2048,640]{1,0:T(8,128)(2,1)}) %all-gather.7.cloned.1.call-update) | async-done | bytes 2621456 | tf_op jit(solution)/shard_map/all_gather | solution.py:695
  211.8 1.7 copy-done
  213.5 2.7 %sums.1 = (f32[512,2048]{1,0:T(8,128)}, f32[512,512]{1,0:T(8,128)}) custom-call(bf16[8,4,4,16,640]{4,3,2,1,0:T(8,128)(2,1)S(1)} %bitcast.30), custom_call_target="tpu_custom_call" | custom-call | tf_op jit(solution)/shard_map/sums/pallas_call | solution.py:704
  216.2 1.3 copy.47
  (24 shorter events, 0.6 us)
Async XLA Ops:
  7.2 60.2 %all-gather.5.cloned.1.call-start = ((), (), s32[]{:S(2)}) async-start(), calls=%async_computation.4 | async-start | bytes 2228224 | tf_op jit(solution)/shard_map/all_gather | solution.py:517
  7.9 11.6 %copy-start.3 = (s32[8,16]{1,0:T(8,128)S(1)}, s32[8,16]{1,0:T(8,128)}, u32[]{:S(2)}) copy-start(s32[8,16]{1,0:T(8,128)} %param.13) | copy-start | bytes 1540
  7.9 12.9 %copy-start.4 = (s32[1,128,16]{1,2,0:T(8,128)S(1)}, s32[1,128,16]{1,2,0:T(8,128)}, u32[]{:S(2)}) copy-start(s32[1,128,16]{1,2,0:T(8,128)} %param.10) | copy-start | bytes 24580
  7.9 13.7 %copy-start.6 = (s32[1,8]{1,0:T(1,128)S(1)}, s32[1,8]{1,0:T(1,128)}, u32[]{:S(2)}) copy-start(s32[1,8]{1,0:T(1,128)} %param.11) | copy-start | bytes 100
  7.9 43.4 %all-to-all-start = ((bf16[1,128,16,512]{3,2,0,1:T(8,128)(2,1)}), bf16[1,128,16,512]{3,2,0,1:T(8,128)(2,1)S(1)}, u32[]{:S(2)}, u32[]{:S(2)}) async-start(bf16[1,128,16,512]{3,2,0,1:T(8,128)(2,1)} %bitcast.34), calls=%async_computation | async-start | bytes 4194304 | tf_op jit(solution)/shard_map/all_to_all | solution.py:518
  19.4 183.3 %all-gather.9.cloned.1.call-start = ((), (), s32[]{:S(2)}) async-start(), calls=%async_computation.6 | async-start | bytes 2506752 | tf_op jit(solution)/shard_map/all_gather | solution.py:612
  21.8 43.0 %copy-start.5 = (s32[8]{0:T(128)}, s32[8]{0:T(128)S(1)}, u32[]{:S(2)}) copy-start(s32[8]{0:T(128)S(1)} %get-tuple-element.43.starts_ref) | copy-start | bytes 100
  51.3 1.3 copy-start.2
  115.2 4.5 %collective-permute-start = (bf16[16,4,16,640]{3,2,1,0:T(8,128)(2,1)}, bf16[16,4,16,640]{3,2,1,0:T(8,128)(2,1)S(1)}, u32[]{:S(2)}, u32[]{:S(2)}) collective-permute-start(bf16[16,4,16,640]{3,2,1,0:T(8,128)(2,1)} %get-tuple-element.39), channel_id=1, source_target_pairs={{0,16},{1,17},{2,18},{3,19},{4,20},{5,21},{6,22},{7,23},{8,24},{9,... | collective-permute-start | bytes 3932168 | tf_op jit(solution)/shard_map/ppermute | solution.py:668
  122.4 28.4 %all-to-all-start.2 = ((bf16[64,1,16,640]{3,2,1,0:T(8,128)(2,1)}), bf16[64,1,16,640]{3,2,1,0:T(8,128)(2,1)S(1)}, u32[]{:S(2)}, u32[]{:S(2)}) async-start(bf16[64,1,16,640]{3,2,1,0:T(8,128)(2,1)} %bitcast.14), calls=%async_computation.2 | async-start | bytes 2621440 | tf_op jit(solution)/shard_map/all_to_all | solution.py:671
  130.6 81.2 %all-gather.7.cloned.1.call-start = ((), (), s32[]{:S(2)}) async-start(), calls=%async_computation.5 | async-start | bytes 2949120 | tf_op jit(solution)/shard_map/all_gather | solution.py:695
  150.8 1.1 copy-start.1
  166.0 36.7 %all-to-all-start.1 = ((bf16[128,1,16,512]{3,2,1,0:T(8,128)(2,1)}), bf16[128,1,16,512]{3,2,1,0:T(8,128)(2,1)S(1)}, u32[]{:S(2)}, u32[]{:S(2)}) async-start(bf16[128,1,16,512]{3,2,1,0:T(8,128)(2,1)} %bitcast.9), calls=%async_computation.1 | async-start | bytes 4194304 | tf_op jit(solution)/shard_map/all_to_all | solution.py:697
  211.8 1.7 copy-start
Sparse Core Ops, SparseCore 0:
  10.1 57.1 all-gather.4
  82.4 44.8 all-gather.8
  166.1 45.5 all-gather.6

commit v6 on v5

--- a/solution.py
+++ b/solution.py
@@ -83,14 +83,20 @@
         a_acc[pair] += mm(weight, v_ref[keys, cols])
 
 
-def backward(q_t, k_ref, v_ref, keys, width, w_s, s_s, slot, da_st, da_t, dq_acc, dk_t, dv_t):
+def backward(q_t, k_ref, v_ref, keys, width, w_s, s_s, slot, da_st, da_t, dq_acc, dk_t, dv_t, add):
     for pair in range(PAIRS):
         cols = slice(pair * 128, (pair + 1) * 128)
         d_weight = mm(da_st[pair], v_ref[keys, cols], NT)
         d_score = (d_weight * s_s[slot, pair, :, :width].astype(F32)).astype(BF16)
         dq_acc[pair] += mm(d_score, k_ref[keys, cols])
-        dv_t[cols, keys] += mm(da_t[pair], w_s[slot, pair, :, :width])
-        dk_t[cols, keys] += mm(q_t[pair], d_score)
+        d_val = mm(da_t[pair], w_s[slot, pair, :, :width])
+        d_key = mm(q_t[pair], d_score)
+        if add:
+            dv_t[cols, keys] += d_val
+            dk_t[cols, keys] += d_key
+        else:
+            dv_t[cols, keys] = d_val.astype(dv_t.dtype)
+            dk_t[cols, keys] = d_key.astype(dk_t.dtype)
 
 
 def middle(attended, x, gate, g, w_out):
@@ -150,8 +156,6 @@
     dv_o,
     tgt_t,
     d_pre,
-    dk_t,
-    dv_t,
     k_s,
     v_s,
     sems,
@@ -197,10 +201,6 @@
 
     a_acc[...] = jnp.zeros_like(a_acc)
     dq_acc[...] = jnp.zeros_like(dq_acc)
-    dk_own[...] = jnp.zeros_like(dk_own)
-    dv_own[...] = jnp.zeros_like(dv_own)
-    dk_t[...] = jnp.zeros_like(dk_t)
-    dv_t[...] = jnp.zeros_like(dv_t)
     for copy in copies:
         copy.wait()
 
@@ -212,7 +212,7 @@
 
     def bwd(j, c):
         keys = pl.ds(pl.multiple_of(j * BLK, BLK), BLK)
-        backward(q_t, k_s, v_s, keys, BLK, w_s, s_s, j, da_st, da_t, dq_acc, dk_t, dv_t)
+        backward(q_t, k_s, v_s, keys, BLK, w_s, s_s, j, da_st, da_t, dq_acc, dk_o, dv_o, False)
         return c
 
     lax.fori_loop(0, blocks, fwd, 0)
@@ -231,10 +231,9 @@
     stack_columns(d_att.T, da_t, tgt_rows)
     lax.fori_loop(0, blocks, bwd, 0)
     backward(
-        q_t, k_own, v_own, every, tgt_rows, w_s, s_s, blocks, da_st, da_t, dq_acc, dk_own, dv_own
-    )
-    dk_o[...] = dk_t[...].astype(BF16)
-    dv_o[...] = dv_t[...].astype(BF16)
+        q_t, k_own, v_own, every, tgt_rows, w_s, s_s, blocks, da_st, da_t, dq_acc, dk_own, dv_own,
+        False,
+    )
     d_q = merge_heads(dq_acc, tgt_rows) * 0.125
     grads = (None, dv_own[...].T, d_q, dk_own[...].T * 2.0)
     for part in (1, 2, 3):
@@ -348,7 +347,9 @@
 
         def bwd(j, c):
             keys = pl.ds(pl.multiple_of(j * BLK, BLK), BLK)
-            backward(q_t, k_ref, v_ref, keys, BLK, w_s, s_s, j, da_st, da_t, dq_acc, dk_t, dv_t)
+            backward(
+                q_t, k_ref, v_ref, keys, BLK, w_s, s_s, j, da_st, da_t, dq_acc, dk_t, dv_t, True
+            )
             return c
 
         lax.fori_loop(first, i + 1, fwd, 0)
@@ -468,29 +469,46 @@
     out[...] = total
 
 
-def reduce_kernel(pieces, slot_grads, copies):
+def reduce_kernel(pieces_in, slot_grads, copies, pieces, sems):
     del slot_grads
-    total = jnp.sum(pieces[...].astype(F32), axis=0).astype(BF16)
+    count = pieces.shape[0] // 4
+    chunks = [pl.ds(k * count, count) for k in range(4)]
+    parts = fetch([(pieces_in.at[chunk], pieces.at[chunk]) for chunk in chunks], sems)
+    total = jnp.zeros(pieces.shape[1:], F32)
+    for chunk, part in zip(chunks, parts):
+        part.wait()
+        total = total + jnp.sum(pieces[chunk].astype(F32), axis=0)
+    total = total.astype(BF16)
     for peer in range(copies.shape[0]):
         copies[peer] = total
 
 
-def sums_kernel(pieces, d_proj, d_out):
+def sums_kernel(pieces_in, d_proj_o, d_out_o, pieces, d_proj, d_out, sems, sent):
     feature = d_out.shape[1]
     quarter = d_out.shape[0] // 8
-    for level in range(4):
-        for core in range(2):
-            first = (core * 4 + level) * quarter
-            rows = slice(first, first + quarter)
-            for part in range(5):
-                for group, source_cols, cols in segments(part, feature):
-                    piece = pieces[level * 2 + core, :, group, :, source_cols].astype(F32)
-                    piece = piece.reshape(quarter, cols.stop - cols.start)
-                    if part < 4:
-                        base = part * feature
-                        d_proj[rows, base + cols.start : base + cols.stop] = piece
-                    else:
-                        d_out[rows, cols] = piece
+    count = pieces.shape[0]
+    parts = fetch([(pieces_in.at[k], pieces.at[k]) for k in range(count)], sems)
+    leaving = []
+    for k in range(count):
+        parts[k].wait()
+        first = ((k % 2) * 4 + k // 2) * quarter
+        rows = slice(first, first + quarter)
+        for part in range(5):
+            for group, source_cols, cols in segments(part, feature):
+                piece = pieces[k, :, group, :, source_cols].astype(F32)
+                piece = piece.reshape(quarter, cols.stop - cols.start)
+                if part < 4:
+                    base = part * feature
+                    d_proj[rows, base + cols.start : base + cols.stop] = piece
+                else:
+                    d_out[rows, cols] = piece
+        own = pl.ds(first, quarter)
+        leaving.append(pltpu.make_async_copy(d_proj.at[own], d_proj_o.at[own], sent.at[2 * k]))
+        leaving.append(pltpu.make_async_copy(d_out.at[own], d_out_o.at[own], sent.at[2 * k + 1]))
+        leaving[-2].start()
+        leaving[-1].start()
+    for copy in leaving:
+        copy.wait()
 
 
 VMEM = pl.BlockSpec(memory_space=pltpu.VMEM)
@@ -576,8 +594,6 @@
         in_specs=[VMEM] * 8 + [ANY],
         out_specs=(VMEM,) * 6,
         scratch_shapes=[
-            scratch((feature, hist_rows), F32),
-            scratch((feature, hist_rows), F32),
             scratch((hist_rows, feature), BF16),
             scratch((hist_rows, feature), BF16),
             pltpu.SemaphoreType.DMA((2,)),
@@ -684,9 +700,10 @@
     copies = pl.pallas_call(
         reduce_kernel,
         out_shape=sds((16, 16, 640), BF16),
-        in_specs=[VMEM, ANY],
+        in_specs=[ANY, ANY],
         out_specs=VMEM,
-        compiler_params=params(56),
+        scratch_shapes=[scratch((64, 16, 640), BF16), pltpu.SemaphoreType.DMA((4,))],
+        compiler_params=params(60),
         name="reduce",
     )(scattered.reshape(64, 16, 640), slot_grads)
     level = lax.all_to_all(
@@ -704,9 +721,16 @@
     sum_proj, sum_out = pl.pallas_call(
         sums_kernel,
         out_shape=(sds(w_proj.shape, F32), sds(w_out.shape, F32)),
-        in_specs=[VMEM],
-        out_specs=(VMEM, VMEM),
-        compiler_params=params(16),
+        in_specs=[ANY],
+        out_specs=(ANY, ANY),
+        scratch_shapes=[
+            scratch((8, 4, 4, 16, 640), BF16),
+            scratch(w_proj.shape, F32),
+            scratch(w_out.shape, F32),
+            pltpu.SemaphoreType.DMA((8,)),
+            pltpu.SemaphoreType.DMA((16,)),
+        ],
+        compiler_params=params(60),
         name="sums",
     )(everything.reshape(8, 4, 4, 16, 640))
 

time: 225 us -> 223 us (level)
    unnamed x16 -> x14, local copies, waits for them, and re-layouts: 5.55 us -> 3.81 us
where the time goes in v6:
time: 223 us; the launch traced here: 222 us
  Pallas kernels  80.8 us (36%)
  waiting for transfers between devices  74.7 us (33%)
  starting transfers between devices  28.2 us (13%)
  between operations  13.9 us (6%)
  blocking collectives  11.9 us (5%)
  local copies, waits for them, and re-layouts  8.96 us (4%)
  other arithmetic  3.8 us (2%)
    pallas_call x1, Pallas kernels, local(): pl.pallas_call(hist_kernel, out_shape=(sds((hist_rows, feature), BF16), s...  32.9 us
    all_to_all x1, waiting for transfers between devices, local(): lax.all_to_all(slot_grads.reshape(peers, 1, capacity, feature), BOTH, spl...  29.9 us
    all_to_all x1, waiting for transfers between devices, local(): lax.all_to_all(send_rows, BOTH, split_axis=1, concat_axis=0, tiled=True)  27.1 us
    pallas_call x1, Pallas kernels, local(): pl.pallas_call(tgt_kernel, out_shape=(sds((tgt_rows, feature), BF16), sds...  14.1 us
    pallas_call x1, Pallas kernels, local(): pl.pallas_call(rows_kernel, out_shape=sds((slots, feature), BF16), in_spe...  12.9 us
    pallas_call x1, Pallas kernels, local(): pl.pallas_call(project_kernel, grid=(blocks,), out_shape=(sds((hist_rows,...  12.2 us
    all_to_all x1, blocking collectives, local(): lax.all_to_all(copies.reshape(16, 1, 16, 640), 'mem', split_axis=0, conca...  11.9 us
    all_to_all x1, starting transfers between devices, local(): lax.all_to_all(send_rows, BOTH, split_axis=1, concat_axis=0, tiled=True)  11.5 us
  transfers between devices with their start and end apart: 7, of which 6 were waited for; matrix products, arithmetic and copies ran while one was open for 4% of the time, Pallas kernels for 28%

profile of v6, /device:TPU:1, one launch (start us, length us, event | category | flops | bytes accessed | tf_op | source)
XLA Modules:
  0.0 222.2 jit_solution(6562874293003155879)
XLA Ops:
  7.2 0.7 all-gather.5.cloned.1.call-update
  7.9 11.5 %all-to-all-start = ((bf16[1,128,16,512]{3,2,0,1:T(8,128)(2,1)}), bf16[1,128,16,512]{3,2,0,1:T(8,128)(2,1)S(1)}, u32[]{:S(2)}, u32[]{:S(2)}) async-start(bf16[1,128,16,512]{3,2,0,1:T(8,128)(2,1)} %bitcast.34), calls=%async_computation | async-start | bytes 4194304 | tf_op jit(solution)/shard_map/all_to_all | solution.py:536
  19.5 0.7 reshape.89.tid_col
  20.2 0.6 reshape.78.tid_row
  20.9 0.7 reshape.80.pos_row
  21.6 0.2 reduce-window.4
  21.9 0.7 broadcast_in_dim_reshape.8.lo
  22.7 0.7 broadcast_in_dim_reshape.9.hi
  23.4 0.2 select_reduce_fusion
  23.6 0.6 and_select_fusion.first_ref
  24.2 27.1 %all-to-all-done = bf16[1,128,16,512]{3,2,0,1:T(8,128)(2,1)S(1)} async-done(((bf16[1,128,16,512]{3,2,0,1:T(8,128)(2,1)}), bf16[1,128,16,512]{3,2,0,1:T(8,128)(2,1)S(1)}, u32[]{:S(2)}, u32[]{:S(2)}) %all-to-all-start) | async-done | bytes 2097184 | tf_op jit(solution)/shard_map/all_to_all | solution.py:536
  51.3 1.3 copy-done.1
  52.6 12.2 %project.1 = (bf16[1024,512]{1,0:T(8,128)(2,1)}, bf16[1024,512]{1,0:T(8,128)(2,1)}, f32[1024,1]{1,0:T(8,128)}, bf16[512,1024]{1,0:T(8,128)(2,1)}, bf16[1024,2048...) custom-call(bf16[2048,512]{1,0:T(8,128)(2,1)} %bitcast.35, s32[1,2048]{1,0:T(1,128)} %reshape.80.pos_row, bf16[512,2048]{1,0:T(8,128)(2,1)} %w_proj.5), custom_call_target="tpu_custom_call" | custom-call | flops 5368709120 | bytes 20971520 | tf_op jit(solution)/shard_map/project/pallas_call | solution.py:558
  64.8 2.5 %all-gather.5.cloned.1.call-done.cand = bf16[2048,512]{1,0:T(8,128)(2,1)} async-done(((bf16[128,512]{1,0:T(8,128)(2,1)}), bf16[2048,512]{1,0:T(8,128)(2,1)}) %all-gather.5.cloned.1.call-update) | async-done | bytes 2097168 | tf_op jit(solution)/shard_map/all_gather | solution.py:535
  67.3 14.1 %tgt.1 = (bf16[128,512]{1,0:T(8,128)(2,1)}, bf16[144,512]{1,0:T(8,128)(2,1)}, bf16[512,1024]{1,0:T(8,128)(2,1)}, bf16[512,1024]{1,0:T(8,128)(2,1)}, bf16[2,512,1...) custom-call(bf16[2048,512]{1,0:T(8,128)(2,1)} %all-gather.5.cloned.1.call-done.cand, s32[128,1]{1,0:T(8,128)} %reshape.89.tid_col, ...), custom_call_target="tpu_custom_call" | custom-call | flops 6442450944 | bytes 16777216 | tf_op jit(solution)/shard_map/tgt/pallas_call | solution.py:584
  81.4 32.9 %hist.1 = (bf16[1024,512]{1,0:T(8,128)(2,1)}, bf16[16,4,16,640]{3,2,1,0:T(8,128)(2,1)}, bf16[16,4,16,640]{3,2,1,0:T(8,128)(2,1)}, bf16[1024,2048]{1,0:T(8,128)(2,1)}) custom-call(s32[1]{0:T(128)} %bitcast.core_ref, s32[4]{0:T(128)} %and_select_fusion.first_ref, s32[8]{0:T(128)} %copy-done.4, bf16[512,512]{1,0:T(8,128)(2,1)} %w_out.3, ...), custom_call_target="tpu_custom_call" | custom-call | flops 19327352832 | bytes 25165824 | tf_op jit(solution)/shard_map/hist/pallas_call | solution.py:631
  114.3 1.6 collective-permute-start
  115.9 2.9 %collective-permute-done = bf16[16,4,16,640]{3,2,1,0:T(8,128)(2,1)S(1)} collective-permute-done((bf16[16,4,16,640]{3,2,1,0:T(8,128)(2,1)}, bf16[16,4,16,640]{3,2,1,0:T(8,128)(2,1)S(1)}, u32[]{:S(2)}, u32[]{:S(2)}) %collective-permute-start) | collective-permute-done | bytes 1310752 | tf_op jit(solution)/shard_map/ppermute | solution.py:684
  118.8 2.8 %add_convert_fusion = bf16[16,4,16,640]{3,2,1,0:T(8,128)(2,1)} fusion(bf16[16,4,16,640]{3,2,1,0:T(8,128)(2,1)S(1)} %collective-permute-done, bf16[16,4,16,640]{3,2,1,0:T(8,128)(2,1)} %get-tuple-element.38), kind=kLoop, calls=%fused_computation | loop fusion | flops 2621440 | bytes 3932160 | tf_op jit(solution)/shard_map/convert_element_type | solution.py:685
  121.6 8.2 %all-to-all-start.2 = ((bf16[64,1,16,640]{3,2,1,0:T(8,128)(2,1)}), bf16[64,1,16,640]{3,2,1,0:T(8,128)(2,1)S(1)}, u32[]{:S(2)}, u32[]{:S(2)}) async-start(bf16[64,1,16,640]{3,2,1,0:T(8,128)(2,1)} %bitcast.14), calls=%async_computation.2 | async-start | bytes 2621440 | tf_op jit(solution)/shard_map/all_to_all | solution.py:687
  129.8 1.6 reshape.90.pos_col
  131.4 12.9 %rows.1.slot_grads = bf16[2048,512]{1,0:T(8,128)(2,1)} custom-call(bf16[1024,2048]{1,0:T(8,128)(2,1)} %get-tuple-element.34.d_pre, bf16[512,2048]{1,0:T(8,128)(2,1)} %w_proj.5, bf16[1024,512]{1,0:T(8,128)(2,1)} %get-tuple-element.35.normed, f32[1024,1]{1,0:T(8,128)} %get-tuple-element.36.rstd, bf16[1024,512]{1,0:T(8,128)(2,1)} %g_hist.3, ...), custom_call_target="tpu_custom_call" | custom-call | flops 5368709120 | bytes 16777216 | tf_op jit(solution)/shard_map/rows/pallas_call | solution.py:690
  144.3 5.6 %all-to-all-done.2 = bf16[64,1,16,640]{3,2,1,0:T(8,128)(2,1)S(1)} async-done(((bf16[64,1,16,640]{3,2,1,0:T(8,128)(2,1)}), bf16[64,1,16,640]{3,2,1,0:T(8,128)(2,1)S(1)}, u32[]{:S(2)}, u32[]{:S(2)}) %all-to-all-start.2) | async-done | bytes 1310752 | tf_op jit(solution)/shard_map/all_to_all | solution.py:687
  149.9 1.1 copy-done
  151.0 2.1 reduce.1
  153.1 11.9 %all_to_all.19 = bf16[16,1,16,640]{3,2,1,0:T(8,128)(2,1)} all-to-all(bf16[16,1,16,640]{3,2,1,0:T(8,128)(2,1)} %bitcast.36), channel_id=1, replica_groups=mesh['grp'=8,'mem'=16] {'mem'}, dimensions={0} | all-to-all | bytes 655360 | tf_op jit(solution)/shard_map/all_to_all | solution.py:709
  164.9 6.9 %all-to-all-start.1 = ((bf16[128,1,16,512]{3,2,1,0:T(8,128)(2,1)}), bf16[128,1,16,512]{3,2,1,0:T(8,128)(2,1)S(1)}, u32[]{:S(2)}, u32[]{:S(2)}) async-start(bf16[128,1,16,512]{3,2,1,0:T(8,128)(2,1)} %bitcast.9), calls=%async_computation.1 | async-start | bytes 4194304 | tf_op jit(solution)/shard_map/all_to_all | solution.py:714
  171.8 29.9 %all-to-all-done.1 = bf16[128,1,16,512]{3,2,1,0:T(8,128)(2,1)S(1)} async-done(((bf16[128,1,16,512]{3,2,1,0:T(8,128)(2,1)}), bf16[128,1,16,512]{3,2,1,0:T(8,128)(2,1)S(1)}, u32[]{:S(2)}, u32[]{:S(2)}) %all-to-all-start.1) | async-done | bytes 2097184 | tf_op jit(solution)/shard_map/all_to_all | solution.py:714
  201.7 3.1 %cand.1 = f32[128,512]{1,0:T(8,128)} custom-call(s32[1]{0:T(128)} %bitcast.11.first_ref, bf16[16,144,512]{2,1,0:T(8,128)(2,1)} %bitcast.33), custom_call_target="tpu_custom_call" | custom-call | tf_op jit(solution)/shard_map/cand/pallas_call | solution.py:738
  204.8 6.0 %all-gather.7.cloned.1.call-done = bf16[2048,640]{1,0:T(8,128)(2,1)} async-done(((bf16[256,640]{1,0:T(8,128)(2,1)}), bf16[2048,640]{1,0:T(8,128)(2,1)}) %all-gather.7.cloned.1.call-update) | async-done | bytes 2621456 | tf_op jit(solution)/shard_map/all_gather | solution.py:712
  210.8 3.5 %sums.1 = (f32[512,2048]{1,0:T(8,128)}, f32[512,512]{1,0:T(8,128)}) custom-call(bf16[8,4,4,16,640]{4,3,2,1,0:T(8,128)(2,1)} %bitcast.32), custom_call_target="tpu_custom_call" | custom-call | tf_op jit(solution)/shard_map/sums/pallas_call | solution.py:721
  214.3 1.3 copy.47
  (22 shorter events, 0.4 us)
Async XLA Ops:
  7.2 60.2 %all-gather.5.cloned.1.call-start = ((), (), s32[]{:S(2)}) async-start(), calls=%async_computation.4 | async-start | bytes 2228224 | tf_op jit(solution)/shard_map/all_gather | solution.py:535
  7.9 11.6 %copy-start.2 = (s32[8,16]{1,0:T(8,128)S(1)}, s32[8,16]{1,0:T(8,128)}, u32[]{:S(2)}) copy-start(s32[8,16]{1,0:T(8,128)} %param.13) | copy-start | bytes 1540
  7.9 12.9 %copy-start.3 = (s32[1,128,16]{1,2,0:T(8,128)S(1)}, s32[1,128,16]{1,2,0:T(8,128)}, u32[]{:S(2)}) copy-start(s32[1,128,16]{1,2,0:T(8,128)} %param.10) | copy-start | bytes 24580
  7.9 13.7 %copy-start.5 = (s32[1,8]{1,0:T(1,128)S(1)}, s32[1,8]{1,0:T(1,128)}, u32[]{:S(2)}) copy-start(s32[1,8]{1,0:T(1,128)} %param.11) | copy-start | bytes 100
  7.9 43.4 %all-to-all-start = ((bf16[1,128,16,512]{3,2,0,1:T(8,128)(2,1)}), bf16[1,128,16,512]{3,2,0,1:T(8,128)(2,1)S(1)}, u32[]{:S(2)}, u32[]{:S(2)}) async-start(bf16[1,128,16,512]{3,2,0,1:T(8,128)(2,1)} %bitcast.34), calls=%async_computation | async-start | bytes 4194304 | tf_op jit(solution)/shard_map/all_to_all | solution.py:536
  19.4 182.3 %all-gather.9.cloned.1.call-start = ((), (), s32[]{:S(2)}) async-start(), calls=%async_computation.6 | async-start | bytes 2506752 | tf_op jit(solution)/shard_map/all_gather | solution.py:628
  21.8 43.0 %copy-start.4 = (s32[8]{0:T(128)}, s32[8]{0:T(128)S(1)}, u32[]{:S(2)}) copy-start(s32[8]{0:T(128)S(1)} %get-tuple-element.43.starts_ref) | copy-start | bytes 100
  51.3 1.3 copy-start.1
  114.3 4.5 %collective-permute-start = (bf16[16,4,16,640]{3,2,1,0:T(8,128)(2,1)}, bf16[16,4,16,640]{3,2,1,0:T(8,128)(2,1)S(1)}, u32[]{:S(2)}, u32[]{:S(2)}) collective-permute-start(bf16[16,4,16,640]{3,2,1,0:T(8,128)(2,1)} %get-tuple-element.39), channel_id=1, source_target_pairs={{0,16},{1,17},{2,18},{3,19},{4,20},{5,21},{6,22},{7,23},{8,24},{9,... | collective-permute-start | bytes 3932168 | tf_op jit(solution)/shard_map/ppermute | solution.py:684
  121.6 28.3 %all-to-all-start.2 = ((bf16[64,1,16,640]{3,2,1,0:T(8,128)(2,1)}), bf16[64,1,16,640]{3,2,1,0:T(8,128)(2,1)S(1)}, u32[]{:S(2)}, u32[]{:S(2)}) async-start(bf16[64,1,16,640]{3,2,1,0:T(8,128)(2,1)} %bitcast.14), calls=%async_computation.2 | async-start | bytes 2621440 | tf_op jit(solution)/shard_map/all_to_all | solution.py:687
  129.8 81.0 %all-gather.7.cloned.1.call-start = ((), (), s32[]{:S(2)}) async-start(), calls=%async_computation.5 | async-start | bytes 2949120 | tf_op jit(solution)/shard_map/all_gather | solution.py:712
  149.9 1.1 copy-start
  164.9 36.8 %all-to-all-start.1 = ((bf16[128,1,16,512]{3,2,1,0:T(8,128)(2,1)}), bf16[128,1,16,512]{3,2,1,0:T(8,128)(2,1)S(1)}, u32[]{:S(2)}, u32[]{:S(2)}) async-start(bf16[128,1,16,512]{3,2,1,0:T(8,128)(2,1)} %bitcast.9), calls=%async_computation.1 | async-start | bytes 4194304 | tf_op jit(solution)/shard_map/all_to_all | solution.py:714
Sparse Core Ops, SparseCore 0:
  10.1 57.1 all-gather.4
  81.6 44.8 all-gather.8
  165.1 45.7 all-gather.6

commit v7 on v6

--- a/solution.py
+++ b/solution.py
@@ -469,16 +469,9 @@
     out[...] = total
 
 
-def reduce_kernel(pieces_in, slot_grads, copies, pieces, sems):
+def reduce_kernel(pieces, slot_grads, copies):
     del slot_grads
-    count = pieces.shape[0] // 4
-    chunks = [pl.ds(k * count, count) for k in range(4)]
-    parts = fetch([(pieces_in.at[chunk], pieces.at[chunk]) for chunk in chunks], sems)
-    total = jnp.zeros(pieces.shape[1:], F32)
-    for chunk, part in zip(chunks, parts):
-        part.wait()
-        total = total + jnp.sum(pieces[chunk].astype(F32), axis=0)
-    total = total.astype(BF16)
+    total = jnp.sum(pieces[...].astype(F32), axis=0).astype(BF16)
     for peer in range(copies.shape[0]):
         copies[peer] = total
 
@@ -700,10 +693,9 @@
     copies = pl.pallas_call(
         reduce_kernel,
         out_shape=sds((16, 16, 640), BF16),
-        in_specs=[ANY, ANY],
+        in_specs=[VMEM, ANY],
         out_specs=VMEM,
-        scratch_shapes=[scratch((64, 16, 640), BF16), pltpu.SemaphoreType.DMA((4,))],
-        compiler_params=params(60),
+        compiler_params=params(16),
         name="reduce",
     )(scattered.reshape(64, 16, 640), slot_grads)
     level = lax.all_to_all(

time: 223 us -> 219 us (0.982)
  Pallas kernels: 80.8 us -> 74.6 us
  starting transfers between devices: 28.2 us -> 33 us
    all_to_all x1, starting transfers between devices: 8.15 us -> 12.6 us  [local(): lax.all_to_all(chip_sum, BOTH, split_axis=0, concat_axis=1, tiled=True, a...]
    pallas_call x1, Pallas kernels: 32.9 us -> 28.5 us  [local(): pl.pallas_call(hist_kernel, out_shape=(sds((hist_rows, feature), BF16), s...]
  transfers between devices with their start and end apart: 7 -> 7, of which waited for: 6 -> 6; matrix products, arithmetic and copies ran while one was open for 4% -> 4% of each run, Pallas kernels for 28% -> 26%
where the time goes in v7:
time: 219 us
  waiting for transfers between devices  74.7 us (34%)
  Pallas kernels  74.6 us (34%)
  starting transfers between devices  33 us (15%)
  between operations  13.8 us (6%)
  blocking collectives  11.1 us (5%)
  local copies, waits for them, and re-layouts  7.94 us (4%)
  other arithmetic  3.68 us (2%)
    all_to_all x1, waiting for transfers between devices, local(): lax.all_to_all(slot_grads.reshape(peers, 1, capacity, feature), BOTH, spl...  29.8 us
    pallas_call x1, Pallas kernels, local(): pl.pallas_call(hist_kernel, out_shape=(sds((hist_rows, feature), BF16), s...  28.5 us
    all_to_all x1, waiting for transfers between devices, local(): lax.all_to_all(send_rows, BOTH, split_axis=1, concat_axis=0, tiled=True)  27.2 us
    pallas_call x1, Pallas kernels, local(): pl.pallas_call(tgt_kernel, out_shape=(sds((tgt_rows, feature), BF16), sds...  14.1 us
    pallas_call x1, Pallas kernels, local(): pl.pallas_call(rows_kernel, out_shape=sds((slots, feature), BF16), in_spe...  12.9 us
    all_to_all x1, starting transfers between devices, local(): lax.all_to_all(chip_sum, BOTH, split_axis=0, concat_axis=1, tiled=True, a...  12.6 us
    pallas_call x1, Pallas kernels, local(): pl.pallas_call(project_kernel, grid=(blocks,), out_shape=(sds((hist_rows,...  12.2 us
    all_to_all x1, starting transfers between devices, local(): lax.all_to_all(send_rows, BOTH, split_axis=1, concat_axis=0, tiled=True)  11.5 us
  transfers between devices with their start and end apart: 7, of which 6 were waited for; matrix products, arithmetic and copies ran while one was open for 4% of the time, Pallas kernels for 26%

profile of v7, /device:TPU:1, one launch (start us, length us, event | category | flops | bytes accessed | tf_op | source)
XLA Modules:
  0.0 218.9 jit_solution(11119686578214021332)
XLA Ops:
  7.2 0.7 all-gather.5.cloned.1.call-update
  7.9 11.5 %all-to-all-start = ((bf16[1,128,16,512]{3,2,0,1:T(8,128)(2,1)}), bf16[1,128,16,512]{3,2,0,1:T(8,128)(2,1)S(1)}, u32[]{:S(2)}, u32[]{:S(2)}) async-start(bf16[1,128,16,512]{3,2,0,1:T(8,128)(2,1)} %bitcast.35), calls=%async_computation | async-start | bytes 4194304 | tf_op jit(solution)/shard_map/all_to_all | solution.py:529
  19.5 0.7 reshape.89.tid_col
  20.2 0.7 reshape.78.tid_row
  20.9 0.1 copy.37
  21.0 0.7 reshape.80.pos_row
  21.7 0.2 reduce-window.4
  21.9 0.7 broadcast_in_dim_reshape.8.lo
  22.7 0.7 broadcast_in_dim_reshape.9.hi
  23.4 0.2 select_reduce_fusion
  23.6 0.5 and_select_fusion.first_ref
  24.2 27.2 %all-to-all-done = bf16[1,128,16,512]{3,2,0,1:T(8,128)(2,1)S(1)} async-done(((bf16[1,128,16,512]{3,2,0,1:T(8,128)(2,1)}), bf16[1,128,16,512]{3,2,0,1:T(8,128)(2,1)S(1)}, u32[]{:S(2)}, u32[]{:S(2)}) %all-to-all-start) | async-done | bytes 2097184 | tf_op jit(solution)/shard_map/all_to_all | solution.py:529
  51.3 1.3 copy-done
  52.6 12.2 %project.1 = (bf16[1024,512]{1,0:T(8,128)(2,1)}, bf16[1024,512]{1,0:T(8,128)(2,1)}, f32[1024,1]{1,0:T(8,128)}, bf16[512,1024]{1,0:T(8,128)(2,1)}, bf16[1024,2048...) custom-call(bf16[2048,512]{1,0:T(8,128)(2,1)} %bitcast.36, s32[1,2048]{1,0:T(1,128)} %reshape.80.pos_row, bf16[512,2048]{1,0:T(8,128)(2,1)} %w_proj.5), custom_call_target="tpu_custom_call" | custom-call | flops 5368709120 | bytes 20971520 | tf_op jit(solution)/shard_map/project/pallas_call | solution.py:551
  64.8 2.5 %all-gather.5.cloned.1.call-done.cand = bf16[2048,512]{1,0:T(8,128)(2,1)} async-done(((bf16[128,512]{1,0:T(8,128)(2,1)}), bf16[2048,512]{1,0:T(8,128)(2,1)}) %all-gather.5.cloned.1.call-update) | async-done | bytes 2097168 | tf_op jit(solution)/shard_map/all_gather | solution.py:528
  67.3 14.1 %tgt.1 = (bf16[128,512]{1,0:T(8,128)(2,1)}, bf16[144,512]{1,0:T(8,128)(2,1)}, bf16[512,1024]{1,0:T(8,128)(2,1)}, bf16[512,1024]{1,0:T(8,128)(2,1)}, bf16[2,512,1...) custom-call(bf16[2048,512]{1,0:T(8,128)(2,1)} %all-gather.5.cloned.1.call-done.cand, s32[128,1]{1,0:T(8,128)} %reshape.89.tid_col, ...), custom_call_target="tpu_custom_call" | custom-call | flops 6442450944 | bytes 16777216 | tf_op jit(solution)/shard_map/tgt/pallas_call | solution.py:577
  81.4 28.5 %hist.1 = (bf16[1024,512]{1,0:T(8,128)(2,1)}, bf16[16,4,16,640]{3,2,1,0:T(8,128)(2,1)}, bf16[16,4,16,640]{3,2,1,0:T(8,128)(2,1)}, bf16[1024,2048]{1,0:T(8,128)(2,1)}) custom-call(s32[1]{0:T(128)} %bitcast.core_ref, s32[4]{0:T(128)} %and_select_fusion.first_ref, s32[8]{0:T(128)} %copy-done.3, bf16[512,512]{1,0:T(8,128)(2,1)} %w_out.3, ...), custom_call_target="tpu_custom_call" | custom-call | flops 19327352832 | bytes 25165824 | tf_op jit(solution)/shard_map/hist/pallas_call | solution.py:624
  110.0 1.6 collective-permute-start
  111.6 2.9 %collective-permute-done = bf16[16,4,16,640]{3,2,1,0:T(8,128)(2,1)S(1)} collective-permute-done((bf16[16,4,16,640]{3,2,1,0:T(8,128)(2,1)}, bf16[16,4,16,640]{3,2,1,0:T(8,128)(2,1)S(1)}, u32[]{:S(2)}, u32[]{:S(2)}) %collective-permute-start) | collective-permute-done | bytes 1310752 | tf_op jit(solution)/shard_map/ppermute | solution.py:677
  114.5 2.8 %add_convert_fusion = bf16[16,4,16,640]{3,2,1,0:T(8,128)(2,1)} fusion(bf16[16,4,16,640]{3,2,1,0:T(8,128)(2,1)S(1)} %collective-permute-done, bf16[16,4,16,640]{3,2,1,0:T(8,128)(2,1)} %get-tuple-element.38), kind=kLoop, calls=%fused_computation | loop fusion | flops 2621440 | bytes 3932160 | tf_op jit(solution)/shard_map/convert_element_type | solution.py:678
  117.2 12.6 %all-to-all-start.2 = ((bf16[64,1,16,640]{3,2,1,0:T(8,128)(2,1)}), bf16[64,1,16,640]{3,2,1,0:T(8,128)(2,1)S(1)}, u32[]{:S(2)}, u32[]{:S(2)}) async-start(bf16[64,1,16,640]{3,2,1,0:T(8,128)(2,1)} %bitcast.14), calls=%async_computation.2 | async-start | bytes 2621440 | tf_op jit(solution)/shard_map/all_to_all | solution.py:680
  129.8 1.6 reshape.90.pos_col
  131.4 12.9 %rows.1.slot_grads = bf16[2048,512]{1,0:T(8,128)(2,1)} custom-call(bf16[1024,2048]{1,0:T(8,128)(2,1)} %get-tuple-element.34.d_pre, bf16[512,2048]{1,0:T(8,128)(2,1)} %w_proj.5, bf16[1024,512]{1,0:T(8,128)(2,1)} %get-tuple-element.35.normed, f32[1024,1]{1,0:T(8,128)} %get-tuple-element.36.rstd, bf16[1024,512]{1,0:T(8,128)(2,1)} %g_hist.3, ...), custom_call_target="tpu_custom_call" | custom-call | flops 5368709120 | bytes 16777216 | tf_op jit(solution)/shard_map/rows/pallas_call | solution.py:683
  144.3 5.7 %all-to-all-done.2 = bf16[64,1,16,640]{3,2,1,0:T(8,128)(2,1)S(1)} async-done(((bf16[64,1,16,640]{3,2,1,0:T(8,128)(2,1)}), bf16[64,1,16,640]{3,2,1,0:T(8,128)(2,1)S(1)}, u32[]{:S(2)}, u32[]{:S(2)}) %all-to-all-start.2) | async-done | bytes 1310752 | tf_op jit(solution)/shard_map/all_to_all | solution.py:680
  150.0 0.2 reduce.1
  150.2 11.1 %all_to_all.19 = bf16[16,1,16,640]{3,2,1,0:T(8,128)(2,1)} all-to-all(bf16[16,1,16,640]{3,2,1,0:T(8,128)(2,1)S(1)} %bitcast.31), channel_id=1, replica_groups=mesh['grp'=8,'mem'=16] {'mem'}, dimensions={0} | all-to-all | bytes 655360 | tf_op jit(solution)/shard_map/all_to_all | solution.py:701
  161.4 7.2 %all-to-all-start.1 = ((bf16[128,1,16,512]{3,2,1,0:T(8,128)(2,1)}), bf16[128,1,16,512]{3,2,1,0:T(8,128)(2,1)S(1)}, u32[]{:S(2)}, u32[]{:S(2)}) async-start(bf16[128,1,16,512]{3,2,1,0:T(8,128)(2,1)} %bitcast.9), calls=%async_computation.1 | async-start | bytes 4194304 | tf_op jit(solution)/shard_map/all_to_all | solution.py:706
  168.6 29.8 %all-to-all-done.1 = bf16[128,1,16,512]{3,2,1,0:T(8,128)(2,1)S(1)} async-done(((bf16[128,1,16,512]{3,2,1,0:T(8,128)(2,1)}), bf16[128,1,16,512]{3,2,1,0:T(8,128)(2,1)S(1)}, u32[]{:S(2)}, u32[]{:S(2)}) %all-to-all-start.1) | async-done | bytes 2097184 | tf_op jit(solution)/shard_map/all_to_all | solution.py:706
  198.4 3.1 %cand.1 = f32[128,512]{1,0:T(8,128)} custom-call(s32[1]{0:T(128)} %bitcast.11.first_ref, bf16[16,144,512]{2,1,0:T(8,128)(2,1)} %bitcast.34), custom_call_target="tpu_custom_call" | custom-call | tf_op jit(solution)/shard_map/cand/pallas_call | solution.py:730
  201.5 6.0 %all-gather.7.cloned.1.call-done = bf16[2048,640]{1,0:T(8,128)(2,1)} async-done(((bf16[256,640]{1,0:T(8,128)(2,1)}), bf16[2048,640]{1,0:T(8,128)(2,1)}) %all-gather.7.cloned.1.call-update) | async-done | bytes 2621456 | tf_op jit(solution)/shard_map/all_gather | solution.py:704
  207.5 3.5 %sums.1 = (f32[512,2048]{1,0:T(8,128)}, f32[512,512]{1,0:T(8,128)}) custom-call(bf16[8,4,4,16,640]{4,3,2,1,0:T(8,128)(2,1)} %bitcast.33), custom_call_target="tpu_custom_call" | custom-call | tf_op jit(solution)/shard_map/sums/pallas_call | solution.py:713
  211.0 1.3 copy.47
  (20 shorter events, 0.3 us)
Async XLA Ops:
  7.2 60.2 %all-gather.5.cloned.1.call-start = ((), (), s32[]{:S(2)}) async-start(), calls=%async_computation.4 | async-start | bytes 2228224 | tf_op jit(solution)/shard_map/all_gather | solution.py:528
  7.9 11.6 %copy-start.1 = (s32[8,16]{1,0:T(8,128)S(1)}, s32[8,16]{1,0:T(8,128)}, u32[]{:S(2)}) copy-start(s32[8,16]{1,0:T(8,128)} %param.13) | copy-start | bytes 1540
  7.9 13.0 %copy-start.2 = (s32[1,128,16]{1,2,0:T(8,128)S(1)}, s32[1,128,16]{1,2,0:T(8,128)}, u32[]{:S(2)}) copy-start(s32[1,128,16]{1,2,0:T(8,128)} %param.10) | copy-start | bytes 24580
  7.9 13.8 %copy-start.4 = (s32[1,8]{1,0:T(1,128)S(1)}, s32[1,8]{1,0:T(1,128)}, u32[]{:S(2)}) copy-start(s32[1,8]{1,0:T(1,128)} %param.11) | copy-start | bytes 100
  7.9 43.4 %all-to-all-start = ((bf16[1,128,16,512]{3,2,0,1:T(8,128)(2,1)}), bf16[1,128,16,512]{3,2,0,1:T(8,128)(2,1)S(1)}, u32[]{:S(2)}, u32[]{:S(2)}) async-start(bf16[1,128,16,512]{3,2,0,1:T(8,128)(2,1)} %bitcast.35), calls=%async_computation | async-start | bytes 4194304 | tf_op jit(solution)/shard_map/all_to_all | solution.py:529
  19.4 178.9 %all-gather.9.cloned.1.call-start = ((), (), s32[]{:S(2)}) async-start(), calls=%async_computation.6 | async-start | bytes 2506752 | tf_op jit(solution)/shard_map/all_gather | solution.py:621
  21.9 42.9 %copy-start.3 = (s32[8]{0:T(128)}, s32[8]{0:T(128)S(1)}, u32[]{:S(2)}) copy-start(s32[8]{0:T(128)S(1)} %get-tuple-element.43.starts_ref) | copy-start | bytes 100
  51.3 1.3 copy-start
  110.0 4.5 %collective-permute-start = (bf16[16,4,16,640]{3,2,1,0:T(8,128)(2,1)}, bf16[16,4,16,640]{3,2,1,0:T(8,128)(2,1)S(1)}, u32[]{:S(2)}, u32[]{:S(2)}) collective-permute-start(bf16[16,4,16,640]{3,2,1,0:T(8,128)(2,1)} %get-tuple-element.39), channel_id=1, source_target_pairs={{0,16},{1,17},{2,18},{3,19},{4,20},{5,21},{6,22},{7,23},{8,24},{9,... | collective-permute-start | bytes 3932168 | tf_op jit(solution)/shard_map/ppermute | solution.py:677
  117.2 32.8 %all-to-all-start.2 = ((bf16[64,1,16,640]{3,2,1,0:T(8,128)(2,1)}), bf16[64,1,16,640]{3,2,1,0:T(8,128)(2,1)S(1)}, u32[]{:S(2)}, u32[]{:S(2)}) async-start(bf16[64,1,16,640]{3,2,1,0:T(8,128)(2,1)} %bitcast.14), calls=%async_computation.2 | async-start | bytes 2621440 | tf_op jit(solution)/shard_map/all_to_all | solution.py:680
  129.8 77.7 %all-gather.7.cloned.1.call-start = ((), (), s32[]{:S(2)}) async-start(), calls=%async_computation.5 | async-start | bytes 2949120 | tf_op jit(solution)/shard_map/all_gather | solution.py:704
  161.4 37.0 %all-to-all-start.1 = ((bf16[128,1,16,512]{3,2,1,0:T(8,128)(2,1)}), bf16[128,1,16,512]{3,2,1,0:T(8,128)(2,1)S(1)}, u32[]{:S(2)}, u32[]{:S(2)}) async-start(bf16[128,1,16,512]{3,2,1,0:T(8,128)(2,1)} %bitcast.9), calls=%async_computation.1 | async-start | bytes 4194304 | tf_op jit(solution)/shard_map/all_to_all | solution.py:706
Sparse Core Ops, SparseCore 0:
  10.1 57.1 all-gather.4
  81.6 44.8 all-gather.8
  161.5 45.9 all-gather.6

commit v8 on v7

--- a/solution.py
+++ b/solution.py
@@ -654,7 +654,7 @@
             scratch((PAIRS, 128, 2 * BLK), BF16),
             scratch((PAIRS, 128, 2 * BLK), BF16),
         ],
-        compiler_params=params(56),
+        compiler_params=params(44),
         cost_estimate=cost(18 << 30, 24 << 20),
         name="hist",
     )(

time: 219 us -> 222 us (1.014)
  local copies, waits for them, and re-layouts: 7.94 us -> 13.6 us
  starting transfers between devices: 33 us -> 28.3 us
  Pallas kernels: 74.6 us -> 77.1 us
    unnamed x12 -> x28, local copies, waits for them, and re-layouts: 2.76 us -> 8.43 us
    all_to_all x1, starting transfers between devices: 12.6 us -> 9.29 us  [local(): lax.all_to_all(chip_sum, BOTH, split_axis=0, concat_axis=1, tiled=True, a...]
    pallas_call x1, Pallas kernels: 28.5 us -> 31 us  [local(): pl.pallas_call(hist_kernel, out_shape=(sds((hist_rows, feature), BF16), s...]
  transfers between devices with their start and end apart: 7 -> 7, of which waited for: 6 -> 6; matrix products, arithmetic and copies ran while one was open for 4% -> 3% of each run, Pallas kernels for 26% -> 27%
where the time goes in v8:
time: 222 us; the launch traced here: 221 us
  Pallas kernels  77.1 us (35%)
  waiting for transfers between devices  75.4 us (34%)
  starting transfers between devices  28.3 us (13%)
  between operations  13.9 us (6%)
  local copies, waits for them, and re-layouts  13.6 us (6%)
  blocking collectives  11.1 us (5%)
    pallas_call x1, Pallas kernels, local(): pl.pallas_call(hist_kernel, out_shape=(sds((hist_rows, feature), BF16), s...  31 us
    all_to_all x1, waiting for transfers between devices, local(): lax.all_to_all(slot_grads.reshape(peers, 1, capacity, feature), BOTH, spl...  29.8 us
    all_to_all x1, waiting for transfers between devices, local(): lax.all_to_all(send_rows, BOTH, split_axis=1, concat_axis=0, tiled=True)  27.7 us
    pallas_call x1, Pallas kernels, local(): pl.pallas_call(tgt_kernel, out_shape=(sds((tgt_rows, feature), BF16), sds...  14.2 us
    pallas_call x1, Pallas kernels, local(): pl.pallas_call(rows_kernel, out_shape=sds((slots, feature), BF16), in_spe...  12.9 us
    pallas_call x1, Pallas kernels, local(): pl.pallas_call(project_kernel, grid=(blocks,), out_shape=(sds((hist_rows,...  12.1 us
    all_to_all x1, starting transfers between devices, local(): lax.all_to_all(send_rows, BOTH, split_axis=1, concat_axis=0, tiled=True)  11.5 us
    all_to_all x1, blocking collectives, local(): lax.all_to_all(copies.reshape(16, 1, 16, 640), 'mem', split_axis=0, conca...  11.1 us
  transfers between devices with their start and end apart: 7, of which 6 were waited for; matrix products, arithmetic and copies ran while one was open for 3% of the time, Pallas kernels for 27%

profile of v8, /device:TPU:1, one launch (start us, length us, event | category | flops | bytes accessed | tf_op | source)
XLA Modules:
  0.0 221.3 jit_solution(14852657891916434010)
XLA Ops:
  7.2 0.7 all-gather.5.cloned.1.call-update
  7.9 11.5 %all-to-all-start = ((bf16[1,128,16,512]{3,2,0,1:T(8,128)(2,1)}), bf16[1,128,16,512]{3,2,0,1:T(8,128)(2,1)S(1)}, u32[]{:S(2)}, u32[]{:S(2)}) async-start(bf16[1,128,16,512]{3,2,0,1:T(8,128)(2,1)} %bitcast.35), calls=%async_computation | async-start | bytes 4194304 | tf_op jit(solution)/shard_map/all_to_all | solution.py:529
  19.5 0.7 reshape.89.tid_col
  20.2 0.6 reshape.78.tid_row
  20.9 0.7 reshape.80.pos_row
  21.9 0.7 broadcast_in_dim_reshape.8.lo
  22.7 0.7 broadcast_in_dim_reshape.9.hi
  23.6 27.7 %all-to-all-done = bf16[1,128,16,512]{3,2,0,1:T(8,128)(2,1)S(1)} async-done(((bf16[1,128,16,512]{3,2,0,1:T(8,128)(2,1)}), bf16[1,128,16,512]{3,2,0,1:T(8,128)(2,1)S(1)}, u32[]{:S(2)}, u32[]{:S(2)}) %all-to-all-start) | async-done | bytes 2097184 | tf_op jit(solution)/shard_map/all_to_all | solution.py:529
  51.3 1.3 copy-done.9
  52.6 12.1 %project.1 = (bf16[1024,512]{1,0:T(8,128)(2,1)}, bf16[1024,512]{1,0:T(8,128)(2,1)}, f32[1024,1]{1,0:T(8,128)}, bf16[512,1024]{1,0:T(8,128)(2,1)}, bf16[1024,2048...) custom-call(bf16[2048,512]{1,0:T(8,128)(2,1)} %bitcast.36, s32[1,2048]{1,0:T(1,128)} %reshape.80.pos_row, bf16[512,2048]{1,0:T(8,128)(2,1)} %w_proj.5), custom_call_target="tpu_custom_call" | custom-call | flops 5368709120 | bytes 20971520 | tf_op jit(solution)/shard_map/project/pallas_call | solution.py:551
  64.8 2.6 %all-gather.5.cloned.1.call-done.cand = bf16[2048,512]{1,0:T(8,128)(2,1)} async-done(((bf16[128,512]{1,0:T(8,128)(2,1)}), bf16[2048,512]{1,0:T(8,128)(2,1)}) %all-gather.5.cloned.1.call-update) | async-done | bytes 2097168 | tf_op jit(solution)/shard_map/all_gather | solution.py:528
  67.3 14.2 %tgt.1 = (bf16[128,512]{1,0:T(8,128)(2,1)}, bf16[144,512]{1,0:T(8,128)(2,1)}, bf16[512,1024]{1,0:T(8,128)(2,1)}, bf16[512,1024]{1,0:T(8,128)(2,1)}, bf16[2,512,1...) custom-call(bf16[2048,512]{1,0:T(8,128)(2,1)} %all-gather.5.cloned.1.call-done.cand, s32[128,1]{1,0:T(8,128)} %reshape.89.tid_col, ...), custom_call_target="tpu_custom_call" | custom-call | flops 6442450944 | bytes 16777216 | tf_op jit(solution)/shard_map/tgt/pallas_call | solution.py:577
  81.6 1.2 copy-done.3
  82.8 1.2 copy-done.4
  84.1 1.2 copy-done.6
  85.3 1.0 copy-done.7
  86.3 0.9 copy-done.8
  87.3 31.0 %hist.1 = (bf16[1024,512]{1,0:T(8,128)(2,1)}, bf16[16,4,16,640]{3,2,1,0:T(8,128)(2,1)S(1)}, bf16[16,4,16,640]{3,2,1,0:T(8,128)(2,1)S(1)}, bf16[1024,2048]{1,0:T(8,128)(2,1)}) custom-call(s32[1]{0:T(128)} %bitcast.core_ref, s32[4]{0:T(128)S(1)} %and_select_fusion.first_ref, s32[8]{0:T(128)S(1)} %get-tuple-element.43.starts_ref, ...), custom_call_target="tpu_custom_call" | custom-call | flops 19327352832 | bytes 25165824 | tf_op jit(solution)/shard_map/hist/pallas_call | solution.py:624
  118.4 3.0 %collective-permute-done = bf16[16,4,16,640]{3,2,1,0:T(8,128)(2,1)S(1)} collective-permute-done((bf16[16,4,16,640]{3,2,1,0:T(8,128)(2,1)S(1)}, bf16[16,4,16,640]{3,2,1,0:T(8,128)(2,1)S(1)}, u32[]{:S(2)}, u32[]{:S(2)}) %collective-permute-start) | collective-permute-done | bytes 1310752 | tf_op jit(solution)/shard_map/ppermute | solution.py:677
  121.4 1.5 add_convert_fusion
  122.9 9.3 %all-to-all-start.2 = ((bf16[64,1,16,640]{3,2,1,0:T(8,128)(2,1)}), bf16[64,1,16,640]{3,2,1,0:T(8,128)(2,1)S(1)}, u32[]{:S(2)}, u32[]{:S(2)}) async-start(bf16[64,1,16,640]{3,2,1,0:T(8,128)(2,1)} %bitcast.14), calls=%async_computation.2 | async-start | bytes 2621440 | tf_op jit(solution)/shard_map/all_to_all | solution.py:680
  132.3 1.6 reshape.90.pos_col
  133.8 12.9 %rows.1.slot_grads = bf16[2048,512]{1,0:T(8,128)(2,1)} custom-call(bf16[1024,2048]{1,0:T(8,128)(2,1)} %get-tuple-element.34.d_pre, bf16[512,2048]{1,0:T(8,128)(2,1)} %w_proj.5, bf16[1024,512]{1,0:T(8,128)(2,1)} %get-tuple-element.35.normed, f32[1024,1]{1,0:T(8,128)} %get-tuple-element.36.rstd, bf16[1024,512]{1,0:T(8,128)(2,1)} %g_hist.3, ...), custom_call_target="tpu_custom_call" | custom-call | flops 5368709120 | bytes 16777216 | tf_op jit(solution)/shard_map/rows/pallas_call | solution.py:683
  146.7 5.6 %all-to-all-done.2 = bf16[64,1,16,640]{3,2,1,0:T(8,128)(2,1)S(1)} async-done(((bf16[64,1,16,640]{3,2,1,0:T(8,128)(2,1)}), bf16[64,1,16,640]{3,2,1,0:T(8,128)(2,1)S(1)}, u32[]{:S(2)}, u32[]{:S(2)}) %all-to-all-start.2) | async-done | bytes 1310752 | tf_op jit(solution)/shard_map/all_to_all | solution.py:680
  152.4 0.2 reduce.1
  152.6 11.1 %all_to_all.19 = bf16[16,1,16,640]{3,2,1,0:T(8,128)(2,1)} all-to-all(bf16[16,1,16,640]{3,2,1,0:T(8,128)(2,1)S(1)} %bitcast.31), channel_id=1, replica_groups=mesh['grp'=8,'mem'=16] {'mem'}, dimensions={0} | all-to-all | bytes 655360 | tf_op jit(solution)/shard_map/all_to_all | solution.py:701
  163.7 7.3 %all-to-all-start.1 = ((bf16[128,1,16,512]{3,2,1,0:T(8,128)(2,1)}), bf16[128,1,16,512]{3,2,1,0:T(8,128)(2,1)S(1)}, u32[]{:S(2)}, u32[]{:S(2)}) async-start(bf16[128,1,16,512]{3,2,1,0:T(8,128)(2,1)} %bitcast.9), calls=%async_computation.1 | async-start | bytes 4194304 | tf_op jit(solution)/shard_map/all_to_all | solution.py:706
  171.0 29.8 %all-to-all-done.1 = bf16[128,1,16,512]{3,2,1,0:T(8,128)(2,1)S(1)} async-done(((bf16[128,1,16,512]{3,2,1,0:T(8,128)(2,1)}), bf16[128,1,16,512]{3,2,1,0:T(8,128)(2,1)S(1)}, u32[]{:S(2)}, u32[]{:S(2)}) %all-to-all-start.1) | async-done | bytes 2097184 | tf_op jit(solution)/shard_map/all_to_all | solution.py:706
  200.8 3.1 %cand.1 = f32[128,512]{1,0:T(8,128)} custom-call(s32[1]{0:T(128)} %bitcast.11.first_ref, bf16[16,144,512]{2,1,0:T(8,128)(2,1)} %bitcast.34), custom_call_target="tpu_custom_call" | custom-call | tf_op jit(solution)/shard_map/cand/pallas_call | solution.py:730
  203.9 6.0 %all-gather.7.cloned.1.call-done = bf16[2048,640]{1,0:T(8,128)(2,1)} async-done(((bf16[256,640]{1,0:T(8,128)(2,1)}), bf16[2048,640]{1,0:T(8,128)(2,1)}) %all-gather.7.cloned.1.call-update) | async-done | bytes 2621456 | tf_op jit(solution)/shard_map/all_gather | solution.py:704
  209.9 3.5 %sums.1 = (f32[512,2048]{1,0:T(8,128)}, f32[512,512]{1,0:T(8,128)}) custom-call(bf16[8,4,4,16,640]{4,3,2,1,0:T(8,128)(2,1)} %bitcast.33), custom_call_target="tpu_custom_call" | custom-call | tf_op jit(solution)/shard_map/sums/pallas_call | solution.py:713
  213.5 1.3 copy.47
  (36 shorter events, 0.9 us)
Async XLA Ops:
  7.2 60.2 %all-gather.5.cloned.1.call-start = ((), (), s32[]{:S(2)}) async-start(), calls=%async_computation.4 | async-start | bytes 2228224 | tf_op jit(solution)/shard_map/all_gather | solution.py:528
  7.9 11.6 %copy-start.10 = (s32[8,16]{1,0:T(8,128)S(1)}, s32[8,16]{1,0:T(8,128)}, u32[]{:S(2)}) copy-start(s32[8,16]{1,0:T(8,128)} %param.13) | copy-start | bytes 1540
  7.9 12.9 %copy-start.11 = (s32[1,128,16]{1,2,0:T(8,128)S(1)}, s32[1,128,16]{1,2,0:T(8,128)}, u32[]{:S(2)}) copy-start(s32[1,128,16]{1,2,0:T(8,128)} %param.10) | copy-start | bytes 24580
  7.9 13.7 %copy-start.12 = (s32[1,8]{1,0:T(1,128)S(1)}, s32[1,8]{1,0:T(1,128)}, u32[]{:S(2)}) copy-start(s32[1,8]{1,0:T(1,128)} %param.11) | copy-start | bytes 100
  7.9 43.4 %all-to-all-start = ((bf16[1,128,16,512]{3,2,0,1:T(8,128)(2,1)}), bf16[1,128,16,512]{3,2,0,1:T(8,128)(2,1)S(1)}, u32[]{:S(2)}, u32[]{:S(2)}) async-start(bf16[1,128,16,512]{3,2,0,1:T(8,128)(2,1)} %bitcast.35), calls=%async_computation | async-start | bytes 4194304 | tf_op jit(solution)/shard_map/all_to_all | solution.py:529
  19.4 181.4 %all-gather.9.cloned.1.call-start = ((), (), s32[]{:S(2)}) async-start(), calls=%async_computation.6 | async-start | bytes 2506752 | tf_op jit(solution)/shard_map/all_gather | solution.py:621
  51.3 1.3 copy-start.9
  67.3 14.3 %copy-start = (bf16[1024,512]{1,0:T(8,128)(2,1)S(1)}, bf16[1024,512]{1,0:T(8,128)(2,1)}, u32[]{:S(2)}) copy-start(bf16[1024,512]{1,0:T(8,128)(2,1)} %g_hist.3) | copy-start | bytes 3145732
  67.3 14.3 %copy-start.1 = (bf16[512,512]{1,0:T(8,128)(2,1)S(1)}, bf16[512,512]{1,0:T(8,128)(2,1)}, u32[]{:S(2)}) copy-start(bf16[512,512]{1,0:T(8,128)(2,1)} %w_out.3) | copy-start | bytes 1572868
  67.3 14.3 %copy-start.2 = (bf16[128,512]{1,0:T(8,128)(2,1)S(1)}, bf16[128,512]{1,0:T(8,128)(2,1)}, u32[]{:S(2)}) copy-start(bf16[128,512]{1,0:T(8,128)(2,1)} %g_tgt.3) | copy-start | bytes 393220
  67.3 14.3 %copy-start.5 = (bf16[1024,512]{1,0:T(8,128)(2,1)S(1)}, bf16[1024,512]{1,0:T(8,128)(2,1)}, u32[]{:S(2)}) copy-start(bf16[1024,512]{1,0:T(8,128)(2,1)} %get-tuple-element.27.x_in) | copy-start | bytes 3145732
  81.6 1.2 copy-start.3
  82.8 1.2 copy-start.4
  84.1 1.2 copy-start.6
  85.3 1.0 copy-start.7
  86.3 0.9 copy-start.8
  118.3 3.1 %collective-permute-start = (bf16[16,4,16,640]{3,2,1,0:T(8,128)(2,1)S(1)}, bf16[16,4,16,640]{3,2,1,0:T(8,128)(2,1)S(1)}, u32[]{:S(2)}, u32[]{:S(2)}) collective-permute-start(bf16[16,4,16,640]{3,2,1,0:T(8,128)(2,1)S(1)} %get-tuple-element.39), channel_id=1, source_target_pairs={{0,16},{1,17},{2,18},{3,19},{4,20},{5,21},{6,22},{7,23},{8,24},{9,... | collective-permute-start | bytes 3932168 | tf_op jit(solution)/shard_map/ppermute | solution.py:677
  122.9 29.5 %all-to-all-start.2 = ((bf16[64,1,16,640]{3,2,1,0:T(8,128)(2,1)}), bf16[64,1,16,640]{3,2,1,0:T(8,128)(2,1)S(1)}, u32[]{:S(2)}, u32[]{:S(2)}) async-start(bf16[64,1,16,640]{3,2,1,0:T(8,128)(2,1)} %bitcast.14), calls=%async_computation.2 | async-start | bytes 2621440 | tf_op jit(solution)/shard_map/all_to_all | solution.py:680
  132.2 77.7 %all-gather.7.cloned.1.call-start = ((), (), s32[]{:S(2)}) async-start(), calls=%async_computation.5 | async-start | bytes 2949120 | tf_op jit(solution)/shard_map/all_gather | solution.py:704
  163.7 37.1 %all-to-all-start.1 = ((bf16[128,1,16,512]{3,2,1,0:T(8,128)(2,1)}), bf16[128,1,16,512]{3,2,1,0:T(8,128)(2,1)S(1)}, u32[]{:S(2)}, u32[]{:S(2)}) async-start(bf16[128,1,16,512]{3,2,1,0:T(8,128)(2,1)} %bitcast.9), calls=%async_computation.1 | async-start | bytes 4194304 | tf_op jit(solution)/shard_map/all_to_all | solution.py:706
Sparse Core Ops, SparseCore 0:
  10.1 57.1 all-gather.4
  81.7 44.8 all-gather.8
  163.9 46.0 all-gather.6
